TPU v7x, 32 devices: a whole 2x2x4 slice. The times are simulated.
32 devices in a mesh: row: 4 (over y, x), col: 8 (over z, core).
Axes of the slice: x: 2, y: 2, z: 4, core: 2. Of those that a mesh axis runs over, the one named last changes fastest.
Arguments:
- observed: float32 [16, 512, 1024], P(None, 'row', 'col'), may hold values from 0.2 to 3
- estimate: float32 [16, 512, 1024], P(None, 'row', 'col'), may hold values from 0.5 to 2
- psf_bank: float32 [128, 16, 2, 4, 33], P(('row', 'col')), may hold values from 0.05 to 1
- zone_ids: int32 [4, 8, 16, 2], P('row', 'col'), may hold values from 0 to 31, all different within a row
- mix_weights: float32 [4, 8, 16, 2], P('row', 'col'), may hold values from 0.2 to 1
- illumination: float32 [16, 64, 8], P(None, 'row', 'col'), may hold values from 0.3 to 3
Outputs:
- restored: float32 [16, 512, 1024], P(None, 'row', 'col')
Inputs may be any that keep to these rules, and one draw needn't show every extreme that they name: `zone_ids`: at each depth a tile names 2 different zones.
All inputs are finite; a program needn't handle non-finite values.
Results may differ from a plain program's by a relative error of at most 0.001.
Values may be sent and summed in bfloat16 or wider, within the bound.
No kernel may reach another device: no remote copies, remote signals or barrier semaphores. Data moves between devices by JAX's collectives and lax.ppermute only.
A program may use at most 192 MiB of HBM per device.

v0:
```python
import jax
import jax.numpy as jnp
from jax import lax
from jax.sharding import PartitionSpec as P

ITERS = 2


def extended_2(cells, sides, width):
    for axis, dim in sides:
        count = lax.axis_size(axis)
        ends = count - 1
        head = lax.slice_in_dim(cells, 0, width, axis=dim)
        tail = lax.slice_in_dim(cells, cells.shape[dim] - width, cells.shape[dim], axis=dim)
        cells = jnp.concatenate(
            [
                lax.ppermute(tail, axis, [(i, (i + 1) % count) for i in range(ends)]),
                cells,
                lax.ppermute(head, axis, [((i + 1) % count, i) for i in range(ends)]),
            ],
            axis=dim,
        )
    return cells


def band_table(size, taps):
    half = taps // 2
    offsets = (
        jnp.arange(size + 2 * half, dtype=jnp.int32)[None, :]
        - jnp.arange(size, dtype=jnp.int32)[:, None]
    )
    return (offsets[None, :, :] == jnp.arange(taps, dtype=jnp.int32)[:, None, None]).astype(
        jnp.bfloat16
    )


def toeplitz(taps_b, table):
    return jnp.einsum("zjt,tye->zjye", taps_b, table, preferred_element_type=jnp.float32).astype(
        jnp.bfloat16
    )


def apply_band(extended, rows_toe, cols_toe):
    passes = jnp.einsum(
        "zjye,zef->zjyf", rows_toe, extended, preferred_element_type=jnp.float32
    ).astype(jnp.bfloat16)
    return jnp.einsum("zjyf,zjxf->zyx", passes, cols_toe, preferred_element_type=jnp.float32)


def shards(observed, estimate, psf_bank, zone_ids, mix_weights, illumination):
    depth, rows, cols = estimate.shape
    zones_here, _, _, rank, taps = psf_bank.shape
    listed_here = zone_ids[0, 0]
    weights = mix_weights[0, 0]
    blended = listed_here.shape[1]
    piece = lax.all_gather(psf_bank, "col", axis=0, tiled=True)
    labels = jnp.arange(piece.shape[0], dtype=jnp.int32)
    onehot = (listed_here[:, :, None] == labels[None, None, :]).astype(jnp.float32)
    selected = jnp.einsum("zkm,mzfrt->zkfrt", onehot, piece, precision=lax.Precision.HIGHEST)
    row_f = selected[:, :, 0]
    col_f = selected[:, :, 1]
    total = jnp.sum(weights[:, :, None] * jnp.sum(row_f, -1) * jnp.sum(col_f, -1), axis=(1, 2))
    row_taps = (
        (weights[:, :, None, None] * row_f / total[:, None, None, None])
        .reshape(depth, blended * rank, taps)
        .astype(jnp.bfloat16)
    )
    col_taps = col_f.reshape(depth, blended * rank, taps).astype(jnp.bfloat16)
    table_rows = band_table(rows, taps)
    table_cols = band_table(cols, taps)
    fwd_rows = toeplitz(row_taps, table_rows)
    fwd_cols = toeplitz(col_taps, table_cols)
    back_rows = toeplitz(row_taps[:, :, ::-1], table_rows)
    back_cols = toeplitz(col_taps[:, :, ::-1], table_cols)
    coarse = lax.all_gather(illumination, "row", axis=1, tiled=True)
    length = coarse.shape[1]
    coarse_here = illumination.shape[1]
    stiffness = float(length * length) / 16.0
    main_diag = jnp.full((depth, length), 1.0 + 2.0 * stiffness, jnp.float32)
    main_diag = main_diag.at[:, 0].set(1.0 + stiffness).at[:, -1].set(1.0 + stiffness)
    lower_diag = jnp.full((depth, length), -stiffness, jnp.float32).at[:, 0].set(0.0)
    upper_diag = jnp.full((depth, length), -stiffness, jnp.float32).at[:, -1].set(0.0)
    smooth = lax.linalg.tridiagonal_solve(lower_diag, main_diag, upper_diag, coarse)
    local_smooth = lax.dynamic_slice_in_dim(
        smooth, lax.axis_index("row") * coarse_here, coarse_here, 1
    )
    factor = jnp.repeat(local_smooth, rows // coarse_here, axis=1)
    current = estimate
    for step in range(ITERS):
        extended = extended_2(current.astype(jnp.bfloat16), (("row", 1), ("col", 2)), 16)
        blurred = apply_band(extended, fwd_rows, fwd_cols)
        ratio = (observed / blurred).astype(jnp.bfloat16)
        ratio_wide = extended_2(ratio, (("row", 1), ("col", 2)), 16)
        back = apply_band(ratio_wide, back_rows, back_cols)
        current = current * back / factor
    return current


def solution(mesh):
    placed = (
        P(None, "row", "col"),
        P(None, "row", "col"),
        P(("row", "col"), None, None, None, None),
        P("row", "col", None, None),
        P("row", "col", None, None),
        P(None, "row", "col"),
    )
    return jax.shard_map(
        shards, mesh=mesh, in_specs=placed, out_specs=P(None, "row", "col"), check_vma=False
    )
```

profile of v0, /device:TPU:1, one launch (start us, length us, event | category | flops | bytes accessed | tf_op | source)
XLA Modules:
  0.0 165.7 jit_solution(18300423973675017021)
XLA Ops:
  0.0 1.5 copy.37
  1.5 0.2 fusion.541
  1.8 4.0 %collective-permute-start = (bf16[16,16,128]{1,2,0:T(8,128)(2,1)S(1)}, bf16[16,16,128]{1,2,0:T(8,128)(2,1)S(1)}, u32[]{:S(2)}, u32[]{:S(2)}) collective-permute-start(bf16[16,16,128]{1,2,0:T(8,128)(2,1)S(1)} %get-tuple-element.270), channel_id=1, source_target_pairs={{0,8},{8,16},{16,24},{1,9},{9,17},{17,25},{2,10},{10,18},{18,26},{... | collective-permute-start | bytes 196616 | tf_op jit(solution)/shard_map/ppermute | solution.py:17
  5.8 1.3 collective-permute-start.1
  7.1 0.6 compare_reduce_fusion
  7.9 24.5 %all_gather.6 = f32[32,16,2,4,33]{4,1,3,2,0:T(8,128)S(1)} all-gather(f32[4,16,2,4,33]{4,1,3,2,0:T(8,128)S(1)} %copy.32), channel_id=1, replica_groups=mesh['row'=4,'col'=8] {'col'}, dimensions={0}, use_global_device_ids=true | all-gather | bytes 608256 | tf_op jit(solution)/shard_map/all_gather | solution.py:56
  32.4 2.1 %fusion.57 = f32[16,2,2,4,33]{4,1,3,2,0:T(2,128)S(1)} fusion(f32[32,16,2,4,33]{4,1,3,2,0:T(8,128)S(1)} %all_gather.6, s32[16,2]{1,0:T(8,128)S(1)} %copy.31), kind=kOutput, calls=%fused_computation.30 | convolution fusion | flops 3245056 | bytes 574592 | tf_op jit(solution)/shard_map/zkm,mzfrt->zkfrt/dot_general | solution.py:59
  34.6 0.3 slice_reduce_fusion.1
  35.7 8.2 %all_gather.7 = f32[16,64,1]{0,2,1:T(1,128)S(1)} all-gather(f32[16,16,1]{0,2,1:T(1,128)S(1)} %copy.50), channel_id=1, replica_groups=mesh['row'=4,'col'=8] {'row'}, dimensions={1}, use_global_device_ids=true | all-gather | bytes 5120 | tf_op jit(solution)/shard_map/all_gather | solution.py:75
  43.9 0.2 scatter.14
  44.1 0.5 broadcast_divide_fusion.18
  44.7 0.3 bitcast_subtract_fusion.54
  45.0 0.1 rev.7
  45.1 0.2 multiply_reduce_fusion
  45.3 0.1 fusion.196
  45.4 0.1 rev.6
  45.5 3.9 %fusion.29 = bf16[16,8,128,160]{2,1,3,0:T(8,128)(2,1)} fusion(s32[128,160]{0,1:T(8,128)S(1)} %iota_subtract_fusion, bf16[16,8,33,1]{2,0,1,3:T(8,128)(2,1)S(1)} %bitcast.1698), kind=kOutput, calls=%fused_computation.26 | convolution fusion | flops 176312320 | bytes 5333248 | tf_op jit(solution)/shard_map/zjt,tye->zjye/dot_general | solution.py:38
  49.4 3.8 %fusion.38 = bf16[16,8,128,160]{2,1,3,0:T(8,128)(2,1)} fusion(s32[128,160]{0,1:T(8,128)S(1)} %iota_subtract_fusion, bf16[16,8,33,1]{2,0,1,3:T(8,128)(2,1)S(1)} %bitcast.1697), kind=kOutput, calls=%fused_computation.29 | convolution fusion | flops 176312320 | bytes 5333248 | tf_op jit(solution)/shard_map/zjt,tye->zjye/dot_general | solution.py:38
  53.2 3.8 %fusion.32 = bf16[16,8,128,160]{2,1,3,0:T(8,128)(2,1)} fusion(s32[128,160]{0,1:T(8,128)S(1)} %iota_subtract_fusion, bf16[16,8,33,1]{2,0,1,3:T(8,128)(2,1)S(1)} %bitcast.1694), kind=kOutput, calls=%fused_computation.27 | convolution fusion | flops 176312320 | bytes 5333248 | tf_op jit(solution)/shard_map/zjt,tye->zjye/dot_general | solution.py:38
  57.0 3.8 %fusion.35 = bf16[16,8,128,160]{2,1,3,0:T(8,128)(2,1)} fusion(s32[128,160]{0,1:T(8,128)S(1)} %iota_subtract_fusion, bf16[16,8,33,1]{2,0,1,3:T(8,128)(2,1)S(1)} %bitcast.1696), kind=kOutput, calls=%fused_computation.28 | convolution fusion | flops 176312320 | bytes 5333248 | tf_op jit(solution)/shard_map/zjt,tye->zjye/dot_general | solution.py:38
  60.8 0.2 fusion.215
  61.0 0.4 subtract_bitcast_fusion
  61.7 0.2 pad_maximum_fusion.5
  61.9 3.5 %collective-permute-start.2 = (bf16[16,160,16]{1,2,0:T(8,128)(2,1)S(1)}, bf16[16,160,16]{1,2,0:T(8,128)(2,1)S(1)}, u32[]{:S(2)}, u32[]{:S(2)}) collective-permute-start(bf16[16,160,16]{1,2,0:T(8,128)(2,1)S(1)} %get-tuple-element.256), channel_id=1, source_target_pairs={{0,1},{1,2},{2,3},{3,4},{4,5},{5,6},{6,7},{8,9},{9,10},{10,11},{11... | collective-permute-start | bytes 245768 | tf_op jit(solution)/shard_map/ppermute | solution.py:17
  65.4 2.1 %collective-permute-start.3 = (bf16[16,160,16]{1,2,0:T(8,128)(2,1)S(1)}, bf16[16,160,16]{1,2,0:T(8,128)(2,1)S(1)}, u32[]{:S(2)}, u32[]{:S(2)}) collective-permute-start(bf16[16,160,16]{1,2,0:T(8,128)(2,1)S(1)} %get-tuple-element.257), channel_id=1, source_target_pairs={{1,0},{2,1},{3,2},{4,3},{5,4},{6,5},{7,6},{9,8},{10,9},{11,10},{12... | collective-permute-start | bytes 245768 | tf_op jit(solution)/shard_map/ppermute | solution.py:19
  72.9 0.2 concatenate.57
  73.1 7.7 %divide_convert_fusion.1 = bf16[16,128,128]{2,1,0:T(8,128)(2,1)S(1)} fusion(f32[16,128,128]{2,1,0:T(8,128)} %param.14, bf16[16,8,128,160]{2,1,3,0:T(8,128)(2,1)} %fusion.35, bf16[16,8,128,160]{2,1,3,0:T(8,128)(2,1)} %fusion.32, bf16[16,160,16]{1,2,0:T(8,128)(2,1)S(1)} %collective-permute-done.3, bf16[16,16,128]{1,2,0:T(8,128)(2,1)S(1)} %collective-permute-done.1, ...), kind=kOutput, calls=%fused_computation.79 | convolution fusion | flops 1517191168 | bytes 12877824 | tf_op jit(solution)/shard_map/zjyf,zjxf->zyx/dot_general | solution.py:47
  80.8 2.3 %collective-permute-start.4 = (bf16[16,16,128]{2,1,0:T(8,128)(2,1)S(1)}, bf16[16,16,128]{2,1,0:T(8,128)(2,1)S(1)}, u32[]{:S(2)}, u32[]{:S(2)}) collective-permute-start(bf16[16,16,128]{2,1,0:T(8,128)(2,1)S(1)} %get-tuple-element.268), channel_id=1, source_target_pairs={{0,8},{8,16},{16,24},{1,9},{9,17},{17,25},{2,10},{10,18},{18,26},{... | collective-permute-start | bytes 196616 | tf_op jit(solution)/shard_map/ppermute | solution.py:17
  83.1 1.3 collective-permute-start.5
  84.5 0.2 collective-permute-done.4
  84.7 4.2 %collective-permute-done.5 = bf16[16,16,128]{2,1,0:T(8,128)(2,1)S(1)} collective-permute-done((bf16[16,16,128]{2,1,0:T(8,128)(2,1)S(1)}, bf16[16,16,128]{2,1,0:T(8,128)(2,1)S(1)}, u32[]{:S(2)}, u32[]{:S(2)}) %collective-permute-start.5) | collective-permute-done | bytes 65568 | tf_op jit(solution)/shard_map/ppermute | solution.py:19
  89.0 0.3 fusion.537
  89.3 0.3 copy.42
  89.6 0.3 copy.43
  89.9 2.4 %collective-permute-start.7 = (bf16[16,160,16]{1,2,0:T(8,128)(2,1)S(1)}, bf16[16,160,16]{1,2,0:T(8,128)(2,1)S(1)}, u32[]{:S(2)}, u32[]{:S(2)}) collective-permute-start(bf16[16,160,16]{1,2,0:T(8,128)(2,1)S(1)} %copy.43), channel_id=1, source_target_pairs={{1,0},{2,1},{3,2},{4,3},{5,4},{6,5},{7,6},{9,8},{10,9},{11,10},{12... | collective-permute-start | bytes 245768 | tf_op jit(solution)/shard_map/ppermute | solution.py:19
  92.3 3.7 %collective-permute-start.6 = (bf16[16,160,16]{1,2,0:T(8,128)(2,1)S(1)}, bf16[16,160,16]{1,2,0:T(8,128)(2,1)S(1)}, u32[]{:S(2)}, u32[]{:S(2)}) collective-permute-start(bf16[16,160,16]{1,2,0:T(8,128)(2,1)S(1)} %copy.42), channel_id=1, source_target_pairs={{0,1},{1,2},{2,3},{3,4},{4,5},{5,6},{6,7},{8,9},{9,10},{10,11},{11... | collective-permute-start | bytes 245768 | tf_op jit(solution)/shard_map/ppermute | solution.py:17
  96.1 1.9 %collective-permute-done.6 = bf16[16,160,16]{1,2,0:T(8,128)(2,1)S(1)} collective-permute-done((bf16[16,160,16]{1,2,0:T(8,128)(2,1)S(1)}, bf16[16,160,16]{1,2,0:T(8,128)(2,1)S(1)}, u32[]{:S(2)}, u32[]{:S(2)}) %collective-permute-start.6) | collective-permute-done | bytes 81952 | tf_op jit(solution)/shard_map/ppermute | solution.py:17
  98.0 0.3 copy.44
  98.3 0.3 copy.45
  98.6 8.8 %fusion.542 = (bf16[16,128,128]{2,1,0:T(8,128)(2,1)S(1)}, f32[16,128,128]{2,1,0:T(8,128)}) fusion(f32[16,128]{1,0:T(8,128)S(1)} %copy.116, f32[16,128,128]{2,1,0:T(8,128)S(1)} %copy-done, bf16[16,8,128,160]{2,1,3,0:T(8,128)(2,1)} %fusion.38, bf16[16,8,128,160]{2,1,3,0:T(8,128)(2,1)} %fusion.29, bf16[16,160,16]{2,1,0:T(8,128)(2,1)S(1)} %copy.45, ...), kind=kOutput, calls=%fused_computation.661 | convolution fusion | flops 1517453312 | bytes 13934592 | tf_op jit(solution)/shard_map/zjyf,zjxf->zyx/dot_general | solution.py:47
  107.4 4.0 %collective-permute-start.8 = (bf16[16,16,128]{2,1,0:T(8,128)(2,1)S(1)}, bf16[16,16,128]{2,1,0:T(8,128)(2,1)S(1)}, u32[]{:S(2)}, u32[]{:S(2)}) collective-permute-start(bf16[16,16,128]{2,1,0:T(8,128)(2,1)S(1)} %get-tuple-element.266), channel_id=1, source_target_pairs={{0,8},{8,16},{16,24},{1,9},{9,17},{17,25},{2,10},{10,18},{18,26},{... | collective-permute-start | bytes 196616 | tf_op jit(solution)/shard_map/ppermute | solution.py:17
  111.4 1.3 collective-permute-start.9
  112.7 3.7 %collective-permute-done.9 = bf16[16,16,128]{2,1,0:T(8,128)(2,1)S(1)} collective-permute-done((bf16[16,16,128]{2,1,0:T(8,128)(2,1)S(1)}, bf16[16,16,128]{2,1,0:T(8,128)(2,1)S(1)}, u32[]{:S(2)}, u32[]{:S(2)}) %collective-permute-start.9) | collective-permute-done | bytes 65568 | tf_op jit(solution)/shard_map/ppermute | solution.py:19
  116.5 0.3 fusion.536
  116.7 0.3 copy.117
  117.0 5.8 %collective-permute-start.10 = (bf16[16,160,16]{1,2,0:T(8,128)(2,1)S(1)}, bf16[16,160,16]{1,2,0:T(8,128)(2,1)S(1)}, u32[]{:S(2)}, u32[]{:S(2)}) collective-permute-start(bf16[16,160,16]{1,2,0:T(8,128)(2,1)S(1)} %copy.117), channel_id=1, source_target_pairs={{0,1},{1,2},{2,3},{3,4},{4,5},{5,6},{6,7},{8,9},{9,10},{10,11},{11... | collective-permute-start | bytes 245768 | tf_op jit(solution)/shard_map/ppermute | solution.py:17
  122.8 0.3 copy.118
  123.1 2.2 %collective-permute-start.11 = (bf16[16,160,16]{1,2,0:T(8,128)(2,1)S(1)}, bf16[16,160,16]{1,2,0:T(8,128)(2,1)S(1)}, u32[]{:S(2)}, u32[]{:S(2)}) collective-permute-start(bf16[16,160,16]{1,2,0:T(8,128)(2,1)S(1)} %copy.118), channel_id=1, source_target_pairs={{1,0},{2,1},{3,2},{4,3},{5,4},{6,5},{7,6},{9,8},{10,9},{11,10},{12... | collective-permute-start | bytes 245768 | tf_op jit(solution)/shard_map/ppermute | solution.py:19
  125.3 0.3 copy.119
  125.6 3.8 %collective-permute-done.11 = bf16[16,160,16]{1,2,0:T(8,128)(2,1)S(1)} collective-permute-done((bf16[16,160,16]{1,2,0:T(8,128)(2,1)S(1)}, bf16[16,160,16]{1,2,0:T(8,128)(2,1)S(1)}, u32[]{:S(2)}, u32[]{:S(2)}) %collective-permute-start.11) | collective-permute-done | bytes 81952 | tf_op jit(solution)/shard_map/ppermute | solution.py:19
  129.4 0.3 copy.120
  129.7 8.3 %divide_convert_fusion = bf16[16,128,128]{2,1,0:T(8,128)(2,1)S(1)} fusion(f32[16,128,128]{2,1,0:T(8,128)S(1)} %copy-done.6, bf16[16,8,128,160]{2,1,3,0:T(8,128)(2,1)} %fusion.35, bf16[16,8,128,160]{2,1,3,0:T(8,128)(2,1)} %fusion.32, bf16[16,160,16]{2,1,0:T(8,128)(2,1)S(1)} %copy.120, bf16[16,16,128]{2,1,0:T(8,128)(2,1)S(1)} %collective-permute-done.9, ...), kind=kOutput, calls=%fused_computation.78 | convolution fusion | flops 1517191168 | bytes 12877824 | tf_op jit(solution)/shard_map/zjyf,zjxf->zyx/dot_general | solution.py:47
  138.1 3.0 %collective-permute-start.12 = (bf16[16,16,128]{2,1,0:T(8,128)(2,1)S(1)}, bf16[16,16,128]{2,1,0:T(8,128)(2,1)S(1)}, u32[]{:S(2)}, u32[]{:S(2)}) collective-permute-start(bf16[16,16,128]{2,1,0:T(8,128)(2,1)S(1)} %get-tuple-element.264), channel_id=1, source_target_pairs={{0,8},{8,16},{16,24},{1,9},{9,17},{17,25},{2,10},{10,18},{18,26},{... | collective-permute-start | bytes 196616 | tf_op jit(solution)/shard_map/ppermute | solution.py:17
  141.1 1.3 collective-permute-start.13
  142.4 3.7 %collective-permute-done.13 = bf16[16,16,128]{2,1,0:T(8,128)(2,1)S(1)} collective-permute-done((bf16[16,16,128]{2,1,0:T(8,128)(2,1)S(1)}, bf16[16,16,128]{2,1,0:T(8,128)(2,1)S(1)}, u32[]{:S(2)}, u32[]{:S(2)}) %collective-permute-start.13) | collective-permute-done | bytes 65568 | tf_op jit(solution)/shard_map/ppermute | solution.py:19
  146.2 0.3 fusion.535
  146.5 0.3 copy.124
  146.8 3.3 %collective-permute-start.14 = (bf16[16,160,16]{1,2,0:T(8,128)(2,1)S(1)}, bf16[16,160,16]{1,2,0:T(8,128)(2,1)S(1)}, u32[]{:S(2)}, u32[]{:S(2)}) collective-permute-start(bf16[16,160,16]{1,2,0:T(8,128)(2,1)S(1)} %copy.124), channel_id=1, source_target_pairs={{0,1},{1,2},{2,3},{3,4},{4,5},{5,6},{6,7},{8,9},{9,10},{10,11},{11... | collective-permute-start | bytes 245768 | tf_op jit(solution)/shard_map/ppermute | solution.py:17
  150.1 0.3 copy.125
  150.4 1.9 %collective-permute-start.15 = (bf16[16,160,16]{1,2,0:T(8,128)(2,1)S(1)}, bf16[16,160,16]{1,2,0:T(8,128)(2,1)S(1)}, u32[]{:S(2)}, u32[]{:S(2)}) collective-permute-start(bf16[16,160,16]{1,2,0:T(8,128)(2,1)S(1)} %copy.125), channel_id=1, source_target_pairs={{1,0},{2,1},{3,2},{4,3},{5,4},{6,5},{7,6},{9,8},{10,9},{11,10},{12... | collective-permute-start | bytes 245768 | tf_op jit(solution)/shard_map/ppermute | solution.py:19
  152.3 0.3 copy.126
  152.6 4.0 %collective-permute-done.15 = bf16[16,160,16]{1,2,0:T(8,128)(2,1)S(1)} collective-permute-done((bf16[16,160,16]{1,2,0:T(8,128)(2,1)S(1)}, bf16[16,160,16]{1,2,0:T(8,128)(2,1)S(1)}, u32[]{:S(2)}, u32[]{:S(2)}) %collective-permute-start.15) | collective-permute-done | bytes 81952 | tf_op jit(solution)/shard_map/ppermute | solution.py:19
  156.7 0.3 copy.127
  157.0 8.7 %fusion.176 = f32[16,128,128]{2,1,0:T(8,128)} fusion(f32[16,128,128]{2,1,0:T(8,128)S(1)} %copy-done.7, bf16[16,8,128,160]{2,1,3,0:T(8,128)(2,1)} %fusion.38, bf16[16,8,128,160]{2,1,3,0:T(8,128)(2,1)} %fusion.29, bf16[16,160,16]{2,1,0:T(8,128)(2,1)S(1)} %copy.127, bf16[16,16,128]{2,1,0:T(8,128)(2,1)S(1)} %collective-permute-done.13, ...), kind=kOutput, calls=%fused_computation.81 | convolution fusion | flops 1517191168 | bytes 13410304 | tf_op jit(solution)/shard_map/zjyf,zjxf->zyx/dot_general | solution.py:47
  (129 shorter events, 6.3 us)
Async XLA Ops:
  0.0 7.7 %copy-start.5 = (s32[1,1,16,2]{2,3,1,0:T(2,128)S(1)}, s32[1,1,16,2]{2,3,1,0:T(2,128)}, u32[]{:S(2)}) copy-start(s32[1,1,16,2]{2,3,1,0:T(2,128)} %param.17) | copy-start | bytes 388
  0.0 7.8 %copy-start.2 = (f32[4,16,2,4,33]{4,3,2,1,0:T(4,128)S(1)}, f32[4,16,2,4,33]{4,3,2,1,0:T(4,128)}, u32[]{:S(2)}) copy-start(f32[4,16,2,4,33]{4,3,2,1,0:T(4,128)} %param.16) | copy-start | bytes 202756
  1.8 59.9 %collective-permute-start = (bf16[16,16,128]{1,2,0:T(8,128)(2,1)S(1)}, bf16[16,16,128]{1,2,0:T(8,128)(2,1)S(1)}, u32[]{:S(2)}, u32[]{:S(2)}) collective-permute-start(bf16[16,16,128]{1,2,0:T(8,128)(2,1)S(1)} %get-tuple-element.270), channel_id=1, source_target_pairs={{0,8},{8,16},{16,24},{1,9},{9,17},{17,25},{2,10},{10,18},{18,26},{... | collective-permute-start | bytes 196616 | tf_op jit(solution)/shard_map/ppermute | solution.py:17
  5.8 55.9 %collective-permute-start.1 = (bf16[16,16,128]{1,2,0:T(8,128)(2,1)S(1)}, bf16[16,16,128]{1,2,0:T(8,128)(2,1)S(1)}, u32[]{:S(2)}, u32[]{:S(2)}) collective-permute-start(bf16[16,16,128]{1,2,0:T(8,128)(2,1)S(1)} %get-tuple-element.271), channel_id=1, source_target_pairs={{8,0},{16,8},{24,16},{9,1},{17,9},{25,17},{10,2},{18,10},{26,18},{... | collective-permute-start | bytes 196616 | tf_op jit(solution)/shard_map/ppermute | solution.py:19
  7.8 27.7 %copy-start.4 = (f32[1,1,16,2]{2,3,1,0:T(2,128)S(1)}, f32[1,1,16,2]{2,3,1,0:T(2,128)}, u32[]{:S(2)}) copy-start(f32[1,1,16,2]{2,3,1,0:T(2,128)} %param.18) | copy-start | bytes 388
  7.8 27.8 %copy-start.3 = (f32[16,16,1]{1,2,0:T(1,128)S(1)}, f32[16,16,1]{1,2,0:T(1,128)}, u32[]{:S(2)}) copy-start(f32[16,16,1]{1,2,0:T(1,128)} %param.19) | copy-start | bytes 3076
  61.9 11.2 %collective-permute-start.2 = (bf16[16,160,16]{1,2,0:T(8,128)(2,1)S(1)}, bf16[16,160,16]{1,2,0:T(8,128)(2,1)S(1)}, u32[]{:S(2)}, u32[]{:S(2)}) collective-permute-start(bf16[16,160,16]{1,2,0:T(8,128)(2,1)S(1)} %get-tuple-element.256), channel_id=1, source_target_pairs={{0,1},{1,2},{2,3},{3,4},{4,5},{5,6},{6,7},{8,9},{9,10},{10,11},{11... | collective-permute-start | bytes 245768 | tf_op jit(solution)/shard_map/ppermute | solution.py:17
  65.4 7.7 %collective-permute-start.3 = (bf16[16,160,16]{1,2,0:T(8,128)(2,1)S(1)}, bf16[16,160,16]{1,2,0:T(8,128)(2,1)S(1)}, u32[]{:S(2)}, u32[]{:S(2)}) collective-permute-start(bf16[16,160,16]{1,2,0:T(8,128)(2,1)S(1)} %get-tuple-element.257), channel_id=1, source_target_pairs={{1,0},{2,1},{3,2},{4,3},{5,4},{6,5},{7,6},{9,8},{10,9},{11,10},{12... | collective-permute-start | bytes 245768 | tf_op jit(solution)/shard_map/ppermute | solution.py:19
  80.8 4.0 %collective-permute-start.4 = (bf16[16,16,128]{2,1,0:T(8,128)(2,1)S(1)}, bf16[16,16,128]{2,1,0:T(8,128)(2,1)S(1)}, u32[]{:S(2)}, u32[]{:S(2)}) collective-permute-start(bf16[16,16,128]{2,1,0:T(8,128)(2,1)S(1)} %get-tuple-element.268), channel_id=1, source_target_pairs={{0,8},{8,16},{16,24},{1,9},{9,17},{17,25},{2,10},{10,18},{18,26},{... | collective-permute-start | bytes 196616 | tf_op jit(solution)/shard_map/ppermute | solution.py:17
  83.1 5.9 %collective-permute-start.5 = (bf16[16,16,128]{2,1,0:T(8,128)(2,1)S(1)}, bf16[16,16,128]{2,1,0:T(8,128)(2,1)S(1)}, u32[]{:S(2)}, u32[]{:S(2)}) collective-permute-start(bf16[16,16,128]{2,1,0:T(8,128)(2,1)S(1)} %get-tuple-element.269), channel_id=1, source_target_pairs={{8,0},{16,8},{24,16},{9,1},{17,9},{25,17},{10,2},{18,10},{26,18},{... | collective-permute-start | bytes 196616 | tf_op jit(solution)/shard_map/ppermute | solution.py:19
  89.0 9.6 %copy-start = (f32[16,128,128]{2,1,0:T(8,128)S(1)}, f32[16,128,128]{2,1,0:T(8,128)}, u32[]{:S(2)}) copy-start(f32[16,128,128]{2,1,0:T(8,128)} %param.15) | copy-start | bytes 3145732
  89.9 8.3 %collective-permute-start.7 = (bf16[16,160,16]{1,2,0:T(8,128)(2,1)S(1)}, bf16[16,160,16]{1,2,0:T(8,128)(2,1)S(1)}, u32[]{:S(2)}, u32[]{:S(2)}) collective-permute-start(bf16[16,160,16]{1,2,0:T(8,128)(2,1)S(1)} %copy.43), channel_id=1, source_target_pairs={{1,0},{2,1},{3,2},{4,3},{5,4},{6,5},{7,6},{9,8},{10,9},{11,10},{12... | collective-permute-start | bytes 245768 | tf_op jit(solution)/shard_map/ppermute | solution.py:19
  92.3 5.6 %collective-permute-start.6 = (bf16[16,160,16]{1,2,0:T(8,128)(2,1)S(1)}, bf16[16,160,16]{1,2,0:T(8,128)(2,1)S(1)}, u32[]{:S(2)}, u32[]{:S(2)}) collective-permute-start(bf16[16,160,16]{1,2,0:T(8,128)(2,1)S(1)} %copy.42), channel_id=1, source_target_pairs={{0,1},{1,2},{2,3},{3,4},{4,5},{5,6},{6,7},{8,9},{9,10},{10,11},{11... | collective-permute-start | bytes 245768 | tf_op jit(solution)/shard_map/ppermute | solution.py:17
  107.4 15.8 %copy-start.1 = (bf16[16,128,128]{2,1,0:T(8,128)(2,1)}, bf16[16,128,128]{2,1,0:T(8,128)(2,1)S(1)}, u32[]{:S(2)}) copy-start(bf16[16,128,128]{2,1,0:T(8,128)(2,1)S(1)} %get-tuple-element.273) | copy-start | bytes 1572868
  107.4 5.3 %collective-permute-start.8 = (bf16[16,16,128]{2,1,0:T(8,128)(2,1)S(1)}, bf16[16,16,128]{2,1,0:T(8,128)(2,1)S(1)}, u32[]{:S(2)}, u32[]{:S(2)}) collective-permute-start(bf16[16,16,128]{2,1,0:T(8,128)(2,1)S(1)} %get-tuple-element.266), channel_id=1, source_target_pairs={{0,8},{8,16},{16,24},{1,9},{9,17},{17,25},{2,10},{10,18},{18,26},{... | collective-permute-start | bytes 196616 | tf_op jit(solution)/shard_map/ppermute | solution.py:17
  111.4 5.0 %collective-permute-start.9 = (bf16[16,16,128]{2,1,0:T(8,128)(2,1)S(1)}, bf16[16,16,128]{2,1,0:T(8,128)(2,1)S(1)}, u32[]{:S(2)}, u32[]{:S(2)}) collective-permute-start(bf16[16,16,128]{2,1,0:T(8,128)(2,1)S(1)} %get-tuple-element.267), channel_id=1, source_target_pairs={{8,0},{16,8},{24,16},{9,1},{17,9},{25,17},{10,2},{18,10},{26,18},{... | collective-permute-start | bytes 196616 | tf_op jit(solution)/shard_map/ppermute | solution.py:19
  116.4 13.3 %copy-start.6 = (f32[16,128,128]{2,1,0:T(8,128)S(1)}, f32[16,128,128]{2,1,0:T(8,128)}, u32[]{:S(2)}) copy-start(f32[16,128,128]{2,1,0:T(8,128)} %param.14) | copy-start | bytes 3145732
  117.0 8.3 %collective-permute-start.10 = (bf16[16,160,16]{1,2,0:T(8,128)(2,1)S(1)}, bf16[16,160,16]{1,2,0:T(8,128)(2,1)S(1)}, u32[]{:S(2)}, u32[]{:S(2)}) collective-permute-start(bf16[16,160,16]{1,2,0:T(8,128)(2,1)S(1)} %copy.117), channel_id=1, source_target_pairs={{0,1},{1,2},{2,3},{3,4},{4,5},{5,6},{6,7},{8,9},{9,10},{10,11},{11... | collective-permute-start | bytes 245768 | tf_op jit(solution)/shard_map/ppermute | solution.py:17
  123.1 6.3 %collective-permute-start.11 = (bf16[16,160,16]{1,2,0:T(8,128)(2,1)S(1)}, bf16[16,160,16]{1,2,0:T(8,128)(2,1)S(1)}, u32[]{:S(2)}, u32[]{:S(2)}) collective-permute-start(bf16[16,160,16]{1,2,0:T(8,128)(2,1)S(1)} %copy.118), channel_id=1, source_target_pairs={{1,0},{2,1},{3,2},{4,3},{5,4},{6,5},{7,6},{9,8},{10,9},{11,10},{12... | collective-permute-start | bytes 245768 | tf_op jit(solution)/shard_map/ppermute | solution.py:19
  138.1 4.3 %collective-permute-start.12 = (bf16[16,16,128]{2,1,0:T(8,128)(2,1)S(1)}, bf16[16,16,128]{2,1,0:T(8,128)(2,1)S(1)}, u32[]{:S(2)}, u32[]{:S(2)}) collective-permute-start(bf16[16,16,128]{2,1,0:T(8,128)(2,1)S(1)} %get-tuple-element.264), channel_id=1, source_target_pairs={{0,8},{8,16},{16,24},{1,9},{9,17},{17,25},{2,10},{10,18},{18,26},{... | collective-permute-start | bytes 196616 | tf_op jit(solution)/shard_map/ppermute | solution.py:17
  141.1 5.0 %collective-permute-start.13 = (bf16[16,16,128]{2,1,0:T(8,128)(2,1)S(1)}, bf16[16,16,128]{2,1,0:T(8,128)(2,1)S(1)}, u32[]{:S(2)}, u32[]{:S(2)}) collective-permute-start(bf16[16,16,128]{2,1,0:T(8,128)(2,1)S(1)} %get-tuple-element.265), channel_id=1, source_target_pairs={{8,0},{16,8},{24,16},{9,1},{17,9},{25,17},{10,2},{18,10},{26,18},{... | collective-permute-start | bytes 196616 | tf_op jit(solution)/shard_map/ppermute | solution.py:19
  146.2 10.8 %copy-start.7 = (f32[16,128,128]{2,1,0:T(8,128)S(1)}, f32[16,128,128]{2,1,0:T(8,128)}, u32[]{:S(2)}) copy-start(f32[16,128,128]{2,1,0:T(8,128)} %get-tuple-element.274) | copy-start | bytes 3145732
  146.8 5.6 %collective-permute-start.14 = (bf16[16,160,16]{1,2,0:T(8,128)(2,1)S(1)}, bf16[16,160,16]{1,2,0:T(8,128)(2,1)S(1)}, u32[]{:S(2)}, u32[]{:S(2)}) collective-permute-start(bf16[16,160,16]{1,2,0:T(8,128)(2,1)S(1)} %copy.124), channel_id=1, source_target_pairs={{0,1},{1,2},{2,3},{3,4},{4,5},{5,6},{6,7},{8,9},{9,10},{10,11},{11... | collective-permute-start | bytes 245768 | tf_op jit(solution)/shard_map/ppermute | solution.py:17
  150.4 6.3 %collective-permute-start.15 = (bf16[16,160,16]{1,2,0:T(8,128)(2,1)S(1)}, bf16[16,160,16]{1,2,0:T(8,128)(2,1)S(1)}, u32[]{:S(2)}, u32[]{:S(2)}) collective-permute-start(bf16[16,160,16]{1,2,0:T(8,128)(2,1)S(1)} %copy.125), channel_id=1, source_target_pairs={{1,0},{2,1},{3,2},{4,3},{5,4},{6,5},{7,6},{9,8},{10,9},{11,10},{12... | collective-permute-start | bytes 245768 | tf_op jit(solution)/shard_map/ppermute | solution.py:19
where the time goes:
time: 166 us
  matrix products  50.9 us (31%)
  starting transfers between devices  43.3 us (26%)
  blocking collectives  32.7 us (20%)
  waiting for transfers between devices  21.6 us (13%)
  local copies, waits for them, and re-layouts  12.8 us (8%)
  other arithmetic  3.17 us (2%)
    dot_general x4, matrix products, apply_band(): jnp.einsum('zjyf,zjxf->zyx', passes, cols_toe, preferred_element_type=jnp...  33.4 us
    ppermute x8, starting transfers between devices, extended_2(): lax.ppermute(tail, axis, [(i, (i + 1) % count) for i in range(ends)])  29.5 us
    all_gather x1, blocking collectives, shards(): piece = lax.all_gather(psf_bank, 'col', axis=0, tiled=True)  24.5 us
    ppermute x8, waiting for transfers between devices, extended_2(): lax.ppermute(head, axis, [((i + 1) % count, i) for i in range(ends)])  19.5 us
    dot_general x4, matrix products, toeplitz(): jnp.einsum('zjt,tye->zjye', taps_b, table, preferred_element_type=jnp.flo...  15.3 us
    ppermute x8, starting transfers between devices, extended_2(): lax.ppermute(head, axis, [((i + 1) % count, i) for i in range(ends)])  13.8 us
    all_gather x1, blocking collectives, shards(): coarse = lax.all_gather(illumination, 'row', axis=1, tiled=True)  8.18 us
    broadcast_in_dim x64, local copies, waits for them, and re-layouts, shards(): lax.linalg.tridiagonal_solve(lower_diag, main_diag, upper_diag, coarse)  5.29 us
  transfers between devices with their start and end apart: 16, of which 7 were waited for; matrix products, arithmetic and copies ran while one was open for 17% of the time, Pallas kernels for 0%

commit v1 on v0

v1 whole, which is shorter than its diff:
```python
import functools

import jax
import jax.numpy as jnp
import numpy as np
from jax import lax
from jax.experimental import pallas as pl
from jax.experimental.pallas import tpu as pltpu
from jax.sharding import PartitionSpec as P

ITERS = 2
F32 = jnp.float32
BF16 = jnp.bfloat16
HIGHEST = lax.Precision.HIGHEST
VMEM = pl.BlockSpec(memory_space=pltpu.VMEM)
SMEM = pl.BlockSpec(memory_space=pltpu.SMEM)

TILE = 128
HALO = 16
PACK = TILE // HALO
TAP_ROWS = 48


def lanes(shape):
    return lax.broadcasted_iota(jnp.int32, shape, len(shape) - 1)


def sublanes(shape):
    return lax.broadcasted_iota(jnp.int32, shape, len(shape) - 2)


def call(body, outs, specs, scratch=(), name=None, flops=0):
    return pl.pallas_call(
        body,
        out_shape=outs,
        in_specs=specs,
        out_specs=jax.tree.map(lambda _: VMEM, outs),
        scratch_shapes=list(scratch),
        compiler_params=pltpu.CompilerParams(vmem_limit_bytes=16 * 1024 * 1024),
        cost_estimate=pl.CostEstimate(flops=flops, bytes_accessed=1 << 20, transcendentals=0),
        name=name,
    )


def shift(cells, axis, by):
    count = lax.axis_size(axis)
    return lax.ppermute(cells, axis, [(i, (i + by) % count) for i in range(count)])


def gathered(piece, axis):
    count = lax.axis_size(axis)
    if count <= 8:
        return [piece] + [shift(piece, axis, s) for s in range(1, count)]
    every = lax.all_gather(piece, axis, axis=0)
    me = lax.axis_index(axis)
    return [lax.dynamic_index_in_dim(every, (me - s) % count, 0, False) for s in range(count)]


def bank_kernel(bank_ref, out_ref):
    rows, taps = bank_ref.shape
    for block in range(rows // TILE):
        part = bank_ref[block * TILE : (block + 1) * TILE, :]
        part = jnp.concatenate([part, jnp.zeros((TILE, TILE - taps), F32)], axis=1)
        out_ref[:, block * TILE : (block + 1) * TILE] = part.T[:TAP_ROWS].astype(BF16)


def taps_kernel(cols, taps, meta_ref, ids_ref, mix_ref, *refs):
    pieces, uv_ref = refs[:cols], refs[cols]
    col = meta_ref[5]
    blended = ids_ref.shape[0]
    zones = pieces[0].shape[1] // TILE
    lane = lanes((1, TILE))
    is_row = (lane & 7) < 4
    picked = []
    total = jnp.zeros((1, TILE), F32)
    for k in range(blended):
        ids = ids_ref[k : k + 1, :]
        got = jnp.zeros((TAP_ROWS, TILE), F32)
        for s in range(cols):
            first = lax.rem(col + cols - s, cols) * zones
            for m in range(zones):
                got = jnp.where(
                    ids == first + m,
                    pieces[s][:, m * TILE : (m + 1) * TILE].astype(F32),
                    got,
                )
        sums = jnp.sum(got, axis=0, keepdims=True)
        both = sums * pltpu.roll(sums, TILE - 4, 1)
        total = total + jnp.where(is_row, both * mix_ref[k : k + 1, :], 0.0)
        picked.append(got)
    group = (lanes((TILE, TILE)) >> 3) == (sublanes((TILE, TILE)) >> 3)
    total = jnp.dot(
        jnp.broadcast_to(total, (8, TILE)),
        group.astype(F32),
        precision=HIGHEST,
        preferred_element_type=F32,
    )[:1]
    tap = sublanes((TAP_ROWS, 2 * TILE))
    at = lanes((TAP_ROWS, 2 * TILE))
    half = taps // 2
    goes = jnp.where(at < TILE, (tap - half) & (TILE - 1), TILE + ((half - tap) & (TILE - 1)))
    place = ((goes == at) & (tap < taps)).astype(F32).astype(BF16)
    for k in range(blended):
        got = picked[k]
        scaled = mix_ref[k : k + 1, :] * got / total
        chosen = jnp.where(is_row, scaled, got).astype(BF16)
        uv_ref[k] = lax.dot_general(
            chosen, place, (((0,), (0,)), ((), ())), preferred_element_type=F32
        ).reshape(uv_ref.shape[1:])


def turned(uv_ref, z, k, r, part, rows, by):
    line = uv_ref[k, z, r : r + 1, part * TILE : (part + 1) * TILE]
    return pltpu.roll(
        jnp.broadcast_to(line, (rows, TILE)), by % TILE, 1, stride=1, stride_axis=0
    )


def bands_kernel(part, rows, meta_ref, uv_ref, *refs):
    if part == 0:
        ct_ref, rt_ref, edge_ref = refs
    else:
        inverse_ref, illum, (ct_ref, rt_ref, edge_ref, inv_ref) = refs[0], refs[1 : 1 + rows], refs[1 + rows :]
        coarse = illum[0].shape[0]
        smooth = jnp.zeros((TILE, illum[0].shape[1]), F32)
        for s in range(rows):
            first = pl.multiple_of(lax.rem(meta_ref[4] + rows - s, rows) * coarse, coarse)
            smooth = smooth + lax.dot_general(
                inverse_ref[meta_ref[4], pl.ds(first, coarse), :],
                illum[s][...],
                (((0,), (0,)), ((), ())),
                precision=HIGHEST,
                preferred_element_type=F32,
            )
        inv = 1.0 / smooth
        for g in range(inv_ref.shape[0]):
            inv_ref[g] = inv[:, g * PACK : (g + 1) * PACK]
    lane = lanes((HALO, TILE))
    low = lane < TILE // 2
    none = jnp.zeros((HALO, TILE), F32)
    zero = jnp.zeros((HALO, 8 * TILE), BF16)

    def one(z, carry):
        at = lax.rem(z, PACK)
        for t in range(PACK):
            ct_ref[z, TILE + t * HALO : TILE + (t + 1) * HALO, :] = zero
        left = pl.multiple_of(TILE + at * HALO, HALO)
        right = pl.multiple_of(TILE + ((at + 4) & 7) * HALO, HALO)
        for j in range(8):
            here = slice(j * TILE, (j + 1) * TILE)
            full = turned(uv_ref, z, j // 4, 4 + j % 4, 1 - part, TILE, 0)
            first, last = full[:HALO], full[TILE - HALO :]
            ct_ref[z, :HALO, here] = jnp.where(low, first, none).astype(BF16)
            ct_ref[z, HALO : TILE - HALO, here] = full[HALO : TILE - HALO].astype(BF16)
            ct_ref[z, TILE - HALO : TILE, here] = jnp.where(low, none, last).astype(BF16)
            ct_ref[z, pl.ds(left, HALO), here] = jnp.where(low, last, none).astype(BF16)
            ct_ref[z, pl.ds(right, HALO), here] = jnp.where(low, none, first).astype(BF16)
        above, below = [none, none], [none, none]
        for j in range(8):
            here = slice(j * TILE, (j + 1) * TILE)
            full = turned(uv_ref, z, j // 4, j % 4, part, TILE, 0)
            first, last = full[:HALO], full[TILE - HALO :]
            rt_ref[z, :HALO, here] = jnp.where(low, first, none).astype(BF16)
            rt_ref[z, HALO : TILE - HALO, here] = full[HALO : TILE - HALO].astype(BF16)
            rt_ref[z, TILE - HALO :, here] = jnp.where(low, none, last).astype(BF16)
            spot = (j % 4) * 2
            up = turned(uv_ref, z, j // 4, j % 4, part, HALO, (spot + 1) * HALO)
            down = turned(uv_ref, z, j // 4, j % 4, part, HALO, spot * HALO)
            above[j // 4] = jnp.where(lane >> 4 == spot, up, above[j // 4])
            below[j // 4] = jnp.where(lane >> 4 == spot + 1, down, below[j // 4])
        edge_ref[z] = jnp.concatenate(
            [jnp.concatenate(above, axis=1), jnp.concatenate(below, axis=1)], axis=0
        ).astype(BF16)
        return carry

    lax.fori_loop(0, ct_ref.shape[0], one, 0)


def joined_halo(left, right, parity, meta_ref):
    lane = lanes(left.shape)
    take_left = (lane < TILE // 2) == (parity == 0)
    left = jnp.where(meta_ref[0] > 0, left, jnp.zeros_like(left))
    right = jnp.where(meta_ref[1] > 0, right, jnp.zeros_like(right))
    return jnp.where(take_left, left, right)


def pack_strips(value, i, g8, rows, lr_ref, rr_ref):
    lane = lanes(value.shape) >> 4
    at = (i + 4) % PACK
    to_right = pltpu.roll(value, (i * HALO - 112) % TILE, 1)
    to_left = pltpu.roll(value, at * HALO, 1)
    if i == 0:
        rr_ref[g8, rows] = to_right
        lr_ref[g8, rows] = to_left
    else:
        rr_ref[g8, rows] = jnp.where(lane == i, to_right, rr_ref[g8, rows])
        lr_ref[g8, rows] = jnp.where(lane == at, to_left, lr_ref[g8, rows])


def finish(part, blurred, g8, i, rows, a_ref, inv_ref, outs):
    z = g8 * PACK + i
    if part == 0:
        value = a_ref[z, rows] / blurred
    else:
        value = a_ref[z, rows] * blurred * inv_ref[g8, rows, i : i + 1]
        outs[0][z, rows] = value
        outs = outs[1:]
    if outs:
        b_ref, lr_ref, rr_ref = outs
        value = value.astype(BF16)
        b_ref[z, rows] = value
        pack_strips(value, i, g8, rows, lr_ref, rr_ref)


def main_kernel(part, meta_ref, ct_ref, rt_ref, field_ref, left_ref, right_ref, a_ref, inv_ref, rim_ref, *refs):
    outs, q_ref = refs[:-1], refs[-1]
    inner = slice(HALO, TILE - HALO)

    def group(g8, carry):
        halos = [joined_halo(left_ref[g8], right_ref[g8], parity, meta_ref) for parity in range(2)]

        def columns(i):
            wide = jnp.concatenate([field_ref[g8 * PACK + i], halos[i // 4]], axis=1)
            for n in range(4):
                got = jnp.dot(
                    wide, ct_ref[g8 * PACK + i, :, n * 256 : (n + 1) * 256], preferred_element_type=F32
                ).astype(BF16)
                q_ref[i % 4, n * 256 : n * 256 + TILE, :] = got[:, :TILE]
                q_ref[i % 4, n * 256 + TILE : (n + 1) * 256, :] = got[:, TILE:]

        def rows(i):
            z = g8 * PACK + i
            blurred = jnp.dot(rt_ref[z], q_ref[i % 4], preferred_element_type=F32)
            rim_ref[z, :HALO] = blurred[:HALO]
            rim_ref[z, HALO:] = blurred[TILE - HALO :]
            finish(part, blurred[inner], g8, i, inner, a_ref, inv_ref, outs)

        columns(0)
        for i in range(PACK):
            if i + 1 < PACK:
                columns(i + 1)
            rows(i)
        return carry

    lax.fori_loop(0, field_ref.shape[0] // PACK, group, 0)


def edge_kernel(part, meta_ref, ct_ref, edge_ref, rim_ref, top_ref, bot_ref, a_ref, inv_ref, *refs):
    count = len(refs) // 2
    made, outs, q_ref = refs[:count], refs[count:-1], refs[-1]
    depth = rim_ref.shape[0]
    inner = slice(HALO, TILE - HALO)

    def group(g8, carry):
        halos = [
            [joined_halo(ref[depth + g8], ref[depth + 2 + g8], parity, meta_ref) for parity in range(2)]
            for ref in (top_ref, bot_ref)
        ]
        for old, new in zip(made, outs):
            each = pl.ds(g8 * (new.shape[0] // (depth // PACK)), new.shape[0] // (depth // PACK))
            new[each, inner] = old[each, inner]

        def columns(i):
            z = g8 * PACK + i
            sides = []
            for s, ref in enumerate((top_ref, bot_ref)):
                side = jnp.concatenate([ref[z], halos[s][i // 4]], axis=1)
                sides.append(jnp.where(meta_ref[2 + s] > 0, side, jnp.zeros_like(side)))
            wide = jnp.concatenate(sides, axis=0)
            for n in range(4):
                got = jnp.dot(
                    wide, ct_ref[z, :, n * 256 : (n + 1) * 256], preferred_element_type=F32
                ).astype(BF16)
                q_ref[i % 4, n * 64 : n * 64 + 32, :] = got[:, :TILE]
                q_ref[i % 4, n * 64 + 32 : (n + 1) * 64, :] = got[:, TILE:]

        def rows(i):
            z = g8 * PACK + i
            blurred = rim_ref[z] + jnp.dot(edge_ref[z], q_ref[i % 4], preferred_element_type=F32)
            for s, at in enumerate((slice(0, HALO), slice(TILE - HALO, TILE))):
                finish(part, blurred[s * HALO : (s + 1) * HALO], g8, i, at, a_ref, inv_ref, outs)

        columns(0)
        for i in range(PACK):
            if i + 1 < PACK:
                columns(i + 1)
            rows(i)
        return carry

    lax.fori_loop(0, depth // PACK, group, 0)


def first_kernel(est_ref, b_ref, lr_ref, rr_ref):
    def group(g8, carry):
        for i in range(PACK):
            value = est_ref[g8 * PACK + i].astype(BF16)
            b_ref[g8 * PACK + i] = value
            pack_strips(value, i, g8, slice(0, TILE), lr_ref, rr_ref)
        return carry

    lax.fori_loop(0, est_ref.shape[0] // PACK, group, 0)


def smoothing(length, rows):
    stiffness = float(length * length) / 16.0
    d = np.diff(np.eye(length), axis=0)
    inverse = np.linalg.inv(np.eye(length) + stiffness * d.T @ d)
    wide = np.repeat(inverse, TILE * rows // length, axis=0)
    return jnp.asarray(wide.reshape(rows, TILE, length).transpose(0, 2, 1), F32)


def shards(observed, estimate, psf_bank, zone_ids, mix_weights, illumination):
    depth = estimate.shape[0]
    zones_here, _, _, rank, taps = psf_bank.shape
    n_row, n_col = lax.axis_size("row"), lax.axis_size("col")
    row, col = lax.axis_index("row"), lax.axis_index("col")
    groups = depth // PACK
    flag = lambda x: x.astype(jnp.int32)
    meta = jnp.stack(
        [flag(col > 0), flag(col < n_col - 1), flag(row > 0), flag(row < n_row - 1), flag(row), flag(col)]
    )
    volume = jax.ShapeDtypeStruct((depth, TILE, TILE), F32)
    narrow = jax.ShapeDtypeStruct((depth, TILE, TILE), BF16)
    strip = jax.ShapeDtypeStruct((groups, TILE, TILE), BF16)

    bank = call(
        bank_kernel, jax.ShapeDtypeStruct((TAP_ROWS, zones_here * TILE), BF16), [VMEM], name="bank"
    )(psf_bank.reshape(zones_here * depth * 2 * rank, taps))
    pieces = gathered(bank, "col")
    profiles = gathered(illumination[:, :, 0].T, "row")
    per_lane = lambda x: jnp.repeat(x[0, 0].T, 2 * rank, axis=1)
    inverse = smoothing(illumination.shape[1] * n_row, n_row)
    uv = call(
        functools.partial(taps_kernel, n_col, taps),
        jax.ShapeDtypeStruct((zone_ids.shape[-1], depth, 2 * rank, 2 * TILE), F32),
        [SMEM] + [VMEM] * (2 + n_col),
        name="taps",
    )(meta, per_lane(zone_ids), per_lane(mix_weights), *pieces)

    def bands(part, uv):
        shape = lambda *s: jax.ShapeDtypeStruct((depth,) + s, BF16)
        outs = (shape(2 * TILE, 8 * TILE), shape(TILE, 8 * TILE), shape(2 * HALO, 2 * TILE))
        args = [meta, uv]
        if part == 1:
            outs = outs + (jax.ShapeDtypeStruct((groups, TILE, PACK), F32),)
            args = args + [inverse] + profiles
        return call(
            functools.partial(bands_kernel, part, n_row),
            outs,
            [SMEM] + [VMEM] * (len(args) - 1),
            name="bands",
            flops=4 * 10**9,
        )(*args)

    def blur(part, last, made, field, lr, rr, other):
        ct, rt, edge, inv = made
        left, right = shift(rr, "col", 1), shift(lr, "col", -1)
        ends = [
            jnp.concatenate([field[:, rows], left[:, rows], right[:, rows]], axis=0)
            for rows in (slice(0, HALO), slice(TILE - HALO, TILE))
        ]
        bot, top = shift(ends[0], "row", -1), shift(ends[1], "row", 1)
        rim = jax.ShapeDtypeStruct((depth, 2 * HALO, TILE), F32)
        outs = ((volume,) if part == 1 else ()) + (() if last else (narrow, strip, strip))
        main, *got = call(
            functools.partial(main_kernel, part),
            (rim,) + outs,
            [SMEM] + [VMEM] * 7,
            [pltpu.VMEM((4, 8 * TILE, TILE), BF16)],
            name="main",
            flops=4 * 10**9,
        )(meta, ct, rt, field, left, right, other, inv)
        return call(
            functools.partial(edge_kernel, part),
            outs,
            [SMEM] + [VMEM] * (7 + len(outs)),
            [pltpu.VMEM((4, 2 * TILE, TILE), BF16)],
            name="edge",
            flops=2 * 10**9,
        )(meta, ct, edge, main, top, bot, other, inv, *got)

    current = estimate
    field, lr, rr = call(first_kernel, (narrow, strip, strip), [VMEM], name="first")(estimate)
    unused = jnp.zeros((groups, TILE, PACK), F32)
    forward = (*bands(0, uv), unused)
    backward = None
    for step in range(ITERS):
        last = step == ITERS - 1
        ratio, lr, rr = blur(0, False, forward, field, lr, rr, observed)
        if backward is None:
            backward = bands(1, lax.optimization_barrier((uv, lr))[0])
        current, *rest = blur(1, last, backward, ratio, lr, rr, current)
        if not last:
            field, lr, rr = rest
    return current


def solution(mesh):
    placed = (
        P(None, "row", "col"),
        P(None, "row", "col"),
        P(("row", "col"), None, None, None, None),
        P("row", "col", None, None),
        P("row", "col", None, None),
        P(None, "row", "col"),
    )
    return jax.shard_map(
        shards, mesh=mesh, in_specs=placed, out_specs=P(None, "row", "col"), check_vma=False
    )
```

time: 166 us -> 84.6 us (0.51)
  the two profiles are of different devices: /device:TPU:1 before, /device:TPU:0 now
where the time goes in v1:
time: 84.6 us; the launch traced here: 84.3 us
  Pallas kernels  37.7 us (45%)
  starting transfers between devices  36.2 us (43%)
  waiting for transfers between devices  5.24 us (6%)
  local copies, waits for them, and re-layouts  4.79 us (6%)
    ppermute x26, starting transfers between devices, shift(): lax.ppermute(cells, axis, [(i, (i + by) % count) for i in range(count)])  36.2 us
    pallas_call x4, Pallas kernels, blur(): call(functools.partial(main_kernel, part), (rim,) + outs, [SMEM] + [VMEM]...  14 us
    pallas_call x4, Pallas kernels, blur(): call(functools.partial(edge_kernel, part), outs, [SMEM] + [VMEM] * (7 + l...  12.9 us
    pallas_call x2, Pallas kernels, bands(): call(functools.partial(bands_kernel, part, n_row), outs, [SMEM] + [VMEM]...  9.07 us
    ppermute x26, waiting for transfers between devices, shift(): lax.ppermute(cells, axis, [(i, (i + by) % count) for i in range(count)])  5.24 us
    unnamed x11, local copies, waits for them, and re-layouts  2.96 us
  transfers between devices with their start and end apart: 26, of which 4 were waited for; matrix products, arithmetic and copies ran while one was open for 3% of the time, Pallas kernels for 33%

profile of v1, /device:TPU:0, one launch (start us, length us, event | category | flops | bytes accessed | tf_op | source)
XLA Modules:
  0.0 84.3 jit_solution(15816259234120561846)
XLA Ops:
  0.0 0.9 %copy-done.3 = f32[4,16,2,4,33]{4,3,2,1,0:T(4,128)S(1)} copy-done((f32[4,16,2,4,33]{4,3,2,1,0:T(4,128)S(1)}, f32[4,16,2,4,33]{4,3,2,1,0:T(4,128)}, u32[]{:S(2)}) %copy-start.3) | copy-done | bytes 67608
  1.0 0.1 bank.1.refs_0_
  1.0 4.5 %collective-permute-start.6 = (bf16[48,512]{1,0:T(8,128)(2,1)S(1)}, bf16[48,512]{1,0:T(8,128)(2,1)S(1)}, u32[]{:S(2)}, u32[]{:S(2)}) collective-permute-start(bf16[48,512]{1,0:T(8,128)(2,1)S(1)} %bank.1.refs_0_), channel_id=1, source_target_pairs={{0,7},{1,0},{2,1},{3,2},{4,3},{5,4},{6,5},{7,6},{8,15},{9,8},{10,9... | collective-permute-start | bytes 147464 | tf_op jit(solution)/shard_map/ppermute | solution.py:47
  5.6 0.6 collective-permute-start.5
  6.2 0.0 collective-permute-start.4
  6.2 2.7 %collective-permute-start.3 = (bf16[48,512]{1,0:T(8,128)(2,1)S(1)}, bf16[48,512]{1,0:T(8,128)(2,1)S(1)}, u32[]{:S(2)}, u32[]{:S(2)}) collective-permute-start(bf16[48,512]{1,0:T(8,128)(2,1)S(1)} %bank.1.refs_0_), channel_id=1, source_target_pairs={{0,4},{1,5},{2,6},{3,7},{4,0},{5,1},{6,2},{7,3},{8,12},{9,13},{10,... | collective-permute-start | bytes 147464 | tf_op jit(solution)/shard_map/ppermute | solution.py:47
  8.9 0.0 collective-permute-start.2
  8.9 1.2 %copy-done = f32[16,128,128]{2,1,0:T(8,128)S(1)} copy-done((f32[16,128,128]{2,1,0:T(8,128)S(1)}, f32[16,128,128]{2,1,0:T(8,128)}, u32[]{:S(2)}) %copy-start) | copy-done | bytes 1048600
  10.1 0.4 first.1
  10.6 0.0 copy-start.2
  10.6 0.7 collective-permute-start.1
  11.3 0.0 collective-permute-done.5.refs_6_
  11.3 0.8 collective-permute-start
  12.1 0.8 copy.9
  12.9 0.7 broadcast_in_dim.9
  13.7 0.1 reshape.9.ids_ref
  13.8 0.8 broadcast_in_dim.10
  14.5 0.1 reshape.10.mix_ref
  14.6 0.1 stack.43.meta_ref
  14.7 2.5 %collective-permute-start.13 = (f32[16,16]{1,0:T(8,128)S(1)}, f32[16,16]{1,0:T(8,128)S(1)}, u32[]{:S(2)}, u32[]{:S(2)}) collective-permute-start(f32[16,16]{1,0:T(8,128)S(1)} %bitcast.17), channel_id=1, source_target_pairs={{0,24},{8,0},{16,8},{24,16},{1,25},{9,1},{17,9},{25,17},{2,26},{10... | collective-permute-start | bytes 3080 | tf_op jit(solution)/shard_map/ppermute | solution.py:47
  17.2 0.0 collective-permute-done.3.refs_4_
  17.2 0.5 collective-permute-start.12
  17.7 0.0 collective-permute-done.2.refs_3_
  17.7 0.6 collective-permute-start.11
  18.3 0.0 collective-permute-done.1.refs_2_
  18.3 0.1 collective-permute-start.7
  18.3 0.0 collective-permute-done.refs_1_
  18.3 3.5 %collective-permute-start.8 = (bf16[2,128,128]{2,1,0:T(8,128)(2,1)S(1)}, bf16[2,128,128]{2,1,0:T(8,128)(2,1)S(1)}, u32[]{:S(2)}, u32[]{:S(2)}) collective-permute-start(bf16[2,128,128]{2,1,0:T(8,128)(2,1)S(1)} %get-tuple-element.46), channel_id=1, source_target_pairs={{0,7},{1,0},{2,1},{3,2},{4,3},{5,4},{6,5},{7,6},{8,15},{9,8},{10,9... | collective-permute-start | bytes 196616 | tf_op jit(solution)/shard_map/ppermute | solution.py:47
  21.8 1.2 %taps.1.uv_ref = f32[2,16,8,256]{3,2,1,0:T(8,128)S(1)} custom-call(s32[6]{0:T(128)S(1)} %stack.43.meta_ref, s32[2,128]{1,0:T(2,128)S(1)} %reshape.9.ids_ref, f32[2,128]{1,0:T(2,128)S(1)} %reshape.10.mix_ref, bf16[48,512]{1,0:T(8,128)(2,1)S(1)} %bank.1.refs_0_, bf16[48,512]{1,0:T(8,128)(2,1)S(1)} %collective-permute-done.refs_1_, ...), custom_call_target="tpu_custom_call" | custom-call | bytes 1048576 | tf_op jit(solution)/shard_map/taps/pallas_call | solution.py:333
  23.0 4.3 %bands.2 = (bf16[16,256,1024]{2,1,0:T(8,128)(2,1)S(1)}, bf16[16,128,1024]{2,1,0:T(8,128)(2,1)S(1)}, bf16[16,32,256]{2,1,0:T(8,128)(2,1)S(1)}) custom-call(s32[6]{0:T(128)S(1)} %stack.43.meta_ref, f32[2,16,8,256]{3,2,1,0:T(8,128)S(1)} %taps.1.uv_ref), custom_call_target="tpu_custom_call" | custom-call | flops 4000000000 | bytes 1048576 | tf_op jit(solution)/shard_map/bands/pallas_call | solution.py:347
  27.3 0.0 collective-permute-done.8.right_ref
  27.4 2.4 %collective-permute-start.9 = (bf16[20,16,128]{2,1,0:T(8,128)(2,1)S(1)}, bf16[20,16,128]{2,1,0:T(8,128)(2,1)S(1)}, u32[]{:S(2)}, u32[]{:S(2)}) collective-permute-start(bf16[20,16,128]{2,1,0:T(8,128)(2,1)S(1)} %pad_maximum_fusion), channel_id=1, source_target_pairs={{0,8},{8,16},{16,24},{24,0},{1,9},{9,17},{17,25},{25,1},{2,10},{10... | collective-permute-start | bytes 245768 | tf_op jit(solution)/shard_map/ppermute | solution.py:47
  29.8 0.6 collective-permute-start.10
  30.4 3.6 %main.4 = (f32[16,32,128]{2,1,0:T(8,128)S(1)}, bf16[16,128,128]{2,1,0:T(8,128)(2,1)S(1)}, bf16[2,128,128]{2,1,0:T(8,128)(2,1)S(1)}, bf16[2,128,128]{2,1,0:T(8,128)(2,1)S(1)}) custom-call(s32[6]{0:T(128)S(1)} %stack.43.meta_ref, bf16[16,256,1024]{2,1,0:T(8,128)(2,1)S(1)} %get-tuple-element.41.ct_ref, bf16[16,128,1024]{2,1,0:T(8,128)(2,1)S(1)} %get-tuple-element.43.rt_ref, ...), custom_call_target="tpu_custom_call" | custom-call | flops 4000000000 | bytes 1048576 | tf_op jit(solution)/shard_map/main/pallas_call | solution.py:365
  34.0 0.0 copy-start.4
  34.0 0.3 collective-permute-done.10.bot_ref
  34.3 3.0 %edge.4 = (bf16[16,128,128]{2,1,0:T(8,128)(2,1)S(1)}, bf16[2,128,128]{2,1,0:T(8,128)(2,1)S(1)}, bf16[2,128,128]{2,1,0:T(8,128)(2,1)S(1)}) custom-call(s32[6]{0:T(128)S(1)} %stack.43.meta_ref, bf16[16,256,1024]{2,1,0:T(8,128)(2,1)S(1)} %get-tuple-element.41.ct_ref, bf16[16,32,256]{2,1,0:T(8,128)(2,1)S(1)} %get-tuple-element.42.edge_ref, ...), custom_call_target="tpu_custom_call" | custom-call | flops 2000000000 | bytes 1048576 | tf_op jit(solution)/shard_map/edge/pallas_call | solution.py:373
  37.3 0.0 collective-permute-start.15
  37.4 0.5 collective-permute-start.14
  37.9 0.0 collective-permute-done.13.refs_4_
  37.9 0.0 collective-permute-done.12.refs_3_
  37.9 4.8 %bands.3 = (bf16[16,256,1024]{2,1,0:T(8,128)(2,1)S(1)}, bf16[16,128,1024]{2,1,0:T(8,128)(2,1)S(1)}, bf16[16,32,256]{2,1,0:T(8,128)(2,1)S(1)}, f32[2,128,8]{2,1,0:T(8,128)S(1)}) custom-call(s32[6]{0:T(128)S(1)} %stack.43.meta_ref, f32[2,16,8,256]{3,2,1,0:T(8,128)S(1)} %taps.1.uv_ref, f32[4,64,128]{2,1,0:T(8,128)S(1)} %copy-done.4, f32[16,16]{1,0:T(8,128)S(1)} %bitcast.20, ...), custom_call_target="tpu_custom_call" | custom-call | flops 4000000000 | bytes 1048576 | tf_op jit(solution)/shard_map/bands/pallas_call | solution.py:347
  42.7 0.2 collective-permute-done.14.left_ref
  42.9 1.3 %collective-permute-start.16 = (bf16[20,16,128]{2,1,0:T(8,128)(2,1)S(1)}, bf16[20,16,128]{2,1,0:T(8,128)(2,1)S(1)}, u32[]{:S(2)}, u32[]{:S(2)}) collective-permute-start(bf16[20,16,128]{2,1,0:T(8,128)(2,1)S(1)} %pad_maximum_fusion.2), channel_id=1, source_target_pairs={{0,8},{8,16},{16,24},{24,0},{1,9},{9,17},{17,25},{25,1},{2,10},{10... | collective-permute-start | bytes 245768 | tf_op jit(solution)/shard_map/ppermute | solution.py:47
  44.2 1.8 %collective-permute-start.17 = (bf16[20,16,128]{2,1,0:T(8,128)(2,1)S(1)}, bf16[20,16,128]{2,1,0:T(8,128)(2,1)S(1)}, u32[]{:S(2)}, u32[]{:S(2)}) collective-permute-start(bf16[20,16,128]{2,1,0:T(8,128)(2,1)S(1)} %pad_maximum_fusion.3), channel_id=1, source_target_pairs={{0,24},{8,0},{16,8},{24,16},{1,25},{9,1},{17,9},{25,17},{2,26},{10... | collective-permute-start | bytes 245768 | tf_op jit(solution)/shard_map/ppermute | solution.py:47
  46.0 3.5 %main.5 = (f32[16,32,128]{2,1,0:T(8,128)S(1)}, f32[16,128,128]{2,1,0:T(8,128)S(1)}, bf16[16,128,128]{2,1,0:T(8,128)(2,1)S(1)}, bf16[2,128,128]{2,1,0:T(8,128)(2,1)S(1)}, bf16[2,128,128]{2,1,0:T(8,128)(2,1)S(1)}) custom-call(s32[6]{0:T(128)S(1)} %stack.43.meta_ref, bf16[16,256,1024]{2,1,0:T(8,128)(2,1)S(1)} %get-tuple-element.53.ct_ref, ...), custom_call_target="tpu_custom_call" | custom-call | flops 4000000000 | bytes 1048576 | tf_op jit(solution)/shard_map/main/pallas_call | solution.py:365
  49.5 0.0 collective-permute-done.17.bot_ref
  49.5 3.0 %edge.5 = (f32[16,128,128]{2,1,0:T(8,128)S(1)}, bf16[16,128,128]{2,1,0:T(8,128)(2,1)S(1)}, bf16[2,128,128]{2,1,0:T(8,128)(2,1)S(1)}, bf16[2,128,128]{2,1,0:T(8,128)(2,1)S(1)}) custom-call(s32[6]{0:T(128)S(1)} %stack.43.meta_ref, bf16[16,256,1024]{2,1,0:T(8,128)(2,1)S(1)} %get-tuple-element.53.ct_ref, bf16[16,32,256]{2,1,0:T(8,128)(2,1)S(1)} %get-tuple-element.54.edge_ref, ...), custom_call_target="tpu_custom_call" | custom-call | flops 2000000000 | bytes 1048576 | tf_op jit(solution)/shard_map/edge/pallas_call | solution.py:373
  52.5 0.0 collective-permute-start.18
  52.6 3.5 %collective-permute-start.19 = (bf16[2,128,128]{2,1,0:T(8,128)(2,1)S(1)}, bf16[2,128,128]{2,1,0:T(8,128)(2,1)S(1)}, u32[]{:S(2)}, u32[]{:S(2)}) collective-permute-start(bf16[2,128,128]{2,1,0:T(8,128)(2,1)S(1)} %get-tuple-element.66), channel_id=1, source_target_pairs={{0,7},{1,0},{2,1},{3,2},{4,3},{5,4},{6,5},{7,6},{8,15},{9,8},{10,9... | collective-permute-start | bytes 196616 | tf_op jit(solution)/shard_map/ppermute | solution.py:47
  56.1 2.1 %collective-permute-done.18.left_ref = bf16[2,128,128]{2,1,0:T(8,128)(2,1)S(1)} collective-permute-done((bf16[2,128,128]{2,1,0:T(8,128)(2,1)S(1)}, bf16[2,128,128]{2,1,0:T(8,128)(2,1)S(1)}, u32[]{:S(2)}, u32[]{:S(2)}) %collective-permute-start.18) | collective-permute-done | bytes 65568 | tf_op jit(solution)/shard_map/ppermute | solution.py:47
  58.3 1.3 %collective-permute-start.20 = (bf16[20,16,128]{2,1,0:T(8,128)(2,1)S(1)}, bf16[20,16,128]{2,1,0:T(8,128)(2,1)S(1)}, u32[]{:S(2)}, u32[]{:S(2)}) collective-permute-start(bf16[20,16,128]{2,1,0:T(8,128)(2,1)S(1)} %pad_maximum_fusion.4), channel_id=1, source_target_pairs={{0,8},{8,16},{16,24},{24,0},{1,9},{9,17},{17,25},{25,1},{2,10},{10... | collective-permute-start | bytes 245768 | tf_op jit(solution)/shard_map/ppermute | solution.py:47
  59.6 1.8 %collective-permute-start.21 = (bf16[20,16,128]{2,1,0:T(8,128)(2,1)S(1)}, bf16[20,16,128]{2,1,0:T(8,128)(2,1)S(1)}, u32[]{:S(2)}, u32[]{:S(2)}) collective-permute-start(bf16[20,16,128]{2,1,0:T(8,128)(2,1)S(1)} %pad_maximum_fusion.5), channel_id=1, source_target_pairs={{0,24},{8,0},{16,8},{24,16},{1,25},{9,1},{17,9},{25,17},{2,26},{10... | collective-permute-start | bytes 245768 | tf_op jit(solution)/shard_map/ppermute | solution.py:47
  61.3 3.6 %main.6 = (f32[16,32,128]{2,1,0:T(8,128)S(1)}, bf16[16,128,128]{2,1,0:T(8,128)(2,1)S(1)}, bf16[2,128,128]{2,1,0:T(8,128)(2,1)S(1)}, bf16[2,128,128]{2,1,0:T(8,128)(2,1)S(1)}) custom-call(s32[6]{0:T(128)S(1)} %stack.43.meta_ref, bf16[16,256,1024]{2,1,0:T(8,128)(2,1)S(1)} %get-tuple-element.41.ct_ref, bf16[16,128,1024]{2,1,0:T(8,128)(2,1)S(1)} %get-tuple-element.43.rt_ref, ...), custom_call_target="tpu_custom_call" | custom-call | flops 4000000000 | bytes 1048576 | tf_op jit(solution)/shard_map/main/pallas_call | solution.py:365
  64.9 0.0 collective-permute-done.20.top_ref
  64.9 0.0 collective-permute-done.21.bot_ref
  64.9 3.0 %edge.6 = (bf16[16,128,128]{2,1,0:T(8,128)(2,1)S(1)}, bf16[2,128,128]{2,1,0:T(8,128)(2,1)S(1)}, bf16[2,128,128]{2,1,0:T(8,128)(2,1)S(1)}) custom-call(s32[6]{0:T(128)S(1)} %stack.43.meta_ref, bf16[16,256,1024]{2,1,0:T(8,128)(2,1)S(1)} %get-tuple-element.41.ct_ref, bf16[16,32,256]{2,1,0:T(8,128)(2,1)S(1)} %get-tuple-element.42.edge_ref, ...), custom_call_target="tpu_custom_call" | custom-call | flops 2000000000 | bytes 1048576 | tf_op jit(solution)/shard_map/edge/pallas_call | solution.py:373
  67.9 0.0 collective-permute-start.22
  67.9 3.5 %collective-permute-start.23 = (bf16[2,128,128]{2,1,0:T(8,128)(2,1)S(1)}, bf16[2,128,128]{2,1,0:T(8,128)(2,1)S(1)}, u32[]{:S(2)}, u32[]{:S(2)}) collective-permute-start(bf16[2,128,128]{2,1,0:T(8,128)(2,1)S(1)} %get-tuple-element.73), channel_id=1, source_target_pairs={{0,7},{1,0},{2,1},{3,2},{4,3},{5,4},{6,5},{7,6},{8,15},{9,8},{10,9... | collective-permute-start | bytes 196616 | tf_op jit(solution)/shard_map/ppermute | solution.py:47
  71.5 2.5 %collective-permute-done.22.left_ref = bf16[2,128,128]{2,1,0:T(8,128)(2,1)S(1)} collective-permute-done((bf16[2,128,128]{2,1,0:T(8,128)(2,1)S(1)}, bf16[2,128,128]{2,1,0:T(8,128)(2,1)S(1)}, u32[]{:S(2)}, u32[]{:S(2)}) %collective-permute-start.22) | collective-permute-done | bytes 65568 | tf_op jit(solution)/shard_map/ppermute | solution.py:47
  74.1 1.0 %collective-permute-start.24 = (bf16[20,16,128]{2,1,0:T(8,128)(2,1)S(1)}, bf16[20,16,128]{2,1,0:T(8,128)(2,1)S(1)}, u32[]{:S(2)}, u32[]{:S(2)}) collective-permute-start(bf16[20,16,128]{2,1,0:T(8,128)(2,1)S(1)} %pad_maximum_fusion.6), channel_id=1, source_target_pairs={{0,8},{8,16},{16,24},{24,0},{1,9},{9,17},{17,25},{25,1},{2,10},{10... | collective-permute-start | bytes 245768 | tf_op jit(solution)/shard_map/ppermute | solution.py:47
  75.1 2.0 %collective-permute-start.25 = (bf16[20,16,128]{2,1,0:T(8,128)(2,1)S(1)}, bf16[20,16,128]{2,1,0:T(8,128)(2,1)S(1)}, u32[]{:S(2)}, u32[]{:S(2)}) collective-permute-start(bf16[20,16,128]{2,1,0:T(8,128)(2,1)S(1)} %pad_maximum_fusion.7), channel_id=1, source_target_pairs={{0,24},{8,0},{16,8},{24,16},{1,25},{9,1},{17,9},{25,17},{2,26},{10... | collective-permute-start | bytes 245768 | tf_op jit(solution)/shard_map/ppermute | solution.py:47
  77.1 3.4 %main.7 = (f32[16,32,128]{2,1,0:T(8,128)S(1)}, f32[16,128,128]{2,1,0:T(8,128)S(1)}) custom-call(s32[6]{0:T(128)S(1)} %stack.43.meta_ref, bf16[16,256,1024]{2,1,0:T(8,128)(2,1)S(1)} %get-tuple-element.53.ct_ref, bf16[16,128,1024]{2,1,0:T(8,128)(2,1)S(1)} %get-tuple-element.55.rt_ref, bf16[16,128,128]{2,1,0:T(8,128)(2,1)S(1)} %get-tuple-element.71.field_ref, ...), custom_call_target="tpu_custom_call" | custom-call | flops 4000000000 | bytes 1048576 | tf_op jit(solution)/shard_map/main/pallas_call | solution.py:365
  80.5 3.8 %edge.7 = f32[16,128,128]{2,1,0:T(8,128)} custom-call(s32[6]{0:T(128)S(1)} %stack.43.meta_ref, bf16[16,256,1024]{2,1,0:T(8,128)(2,1)S(1)} %get-tuple-element.53.ct_ref, bf16[16,32,256]{2,1,0:T(8,128)(2,1)S(1)} %get-tuple-element.54.edge_ref, f32[16,32,128]{2,1,0:T(8,128)S(1)} %get-tuple-element.75.rim_ref, ...), custom_call_target="tpu_custom_call" | custom-call | flops 2000000000 | bytes 1048576 | tf_op jit(solution)/shard_map/edge/pallas_call | solution.py:373
  (38 shorter events, 0.2 us)
Async XLA Ops:
  0.0 0.9 %copy-start.3 = (f32[4,16,2,4,33]{4,3,2,1,0:T(4,128)S(1)}, f32[4,16,2,4,33]{4,3,2,1,0:T(4,128)}, u32[]{:S(2)}) copy-start(f32[4,16,2,4,33]{4,3,2,1,0:T(4,128)} %param.9) | copy-start | bytes 202756
  1.0 9.6 %collective-permute-start.6 = (bf16[48,512]{1,0:T(8,128)(2,1)S(1)}, bf16[48,512]{1,0:T(8,128)(2,1)S(1)}, u32[]{:S(2)}, u32[]{:S(2)}) collective-permute-start(bf16[48,512]{1,0:T(8,128)(2,1)S(1)} %bank.1.refs_0_), channel_id=1, source_target_pairs={{0,7},{1,0},{2,1},{3,2},{4,3},{5,4},{6,5},{7,6},{8,15},{9,8},{10,9... | collective-permute-start | bytes 147464 | tf_op jit(solution)/shard_map/ppermute | solution.py:47
  5.6 5.8 %collective-permute-start.5 = (bf16[48,512]{1,0:T(8,128)(2,1)S(1)}, bf16[48,512]{1,0:T(8,128)(2,1)S(1)}, u32[]{:S(2)}, u32[]{:S(2)}) collective-permute-start(bf16[48,512]{1,0:T(8,128)(2,1)S(1)} %bank.1.refs_0_), channel_id=1, source_target_pairs={{0,6},{1,7},{2,0},{3,1},{4,2},{5,3},{6,4},{7,5},{8,14},{9,15},{10,... | collective-permute-start | bytes 147464 | tf_op jit(solution)/shard_map/ppermute | solution.py:47
  6.2 8.5 %collective-permute-start.4 = (bf16[48,512]{1,0:T(8,128)(2,1)S(1)}, bf16[48,512]{1,0:T(8,128)(2,1)S(1)}, u32[]{:S(2)}, u32[]{:S(2)}) collective-permute-start(bf16[48,512]{1,0:T(8,128)(2,1)S(1)} %bank.1.refs_0_), channel_id=1, source_target_pairs={{0,5},{1,6},{2,7},{3,0},{4,1},{5,2},{6,3},{7,4},{8,13},{9,14},{10,... | collective-permute-start | bytes 147464 | tf_op jit(solution)/shard_map/ppermute | solution.py:47
  6.2 10.9 %collective-permute-start.3 = (bf16[48,512]{1,0:T(8,128)(2,1)S(1)}, bf16[48,512]{1,0:T(8,128)(2,1)S(1)}, u32[]{:S(2)}, u32[]{:S(2)}) collective-permute-start(bf16[48,512]{1,0:T(8,128)(2,1)S(1)} %bank.1.refs_0_), channel_id=1, source_target_pairs={{0,4},{1,5},{2,6},{3,7},{4,0},{5,1},{6,2},{7,3},{8,12},{9,13},{10,... | collective-permute-start | bytes 147464 | tf_op jit(solution)/shard_map/ppermute | solution.py:47
  8.9 8.8 %collective-permute-start.2 = (bf16[48,512]{1,0:T(8,128)(2,1)S(1)}, bf16[48,512]{1,0:T(8,128)(2,1)S(1)}, u32[]{:S(2)}, u32[]{:S(2)}) collective-permute-start(bf16[48,512]{1,0:T(8,128)(2,1)S(1)} %bank.1.refs_0_), channel_id=1, source_target_pairs={{0,3},{1,4},{2,5},{3,6},{4,7},{5,0},{6,1},{7,2},{8,11},{9,12},{10,... | collective-permute-start | bytes 147464 | tf_op jit(solution)/shard_map/ppermute | solution.py:47
  8.9 1.2 %copy-start = (f32[16,128,128]{2,1,0:T(8,128)S(1)}, f32[16,128,128]{2,1,0:T(8,128)}, u32[]{:S(2)}) copy-start(f32[16,128,128]{2,1,0:T(8,128)} %a_ref.9) | copy-start | bytes 3145732
  10.6 19.9 %copy-start.2 = (f32[16,128,128]{2,1,0:T(8,128)S(1)}, f32[16,128,128]{2,1,0:T(8,128)}, u32[]{:S(2)}) copy-start(f32[16,128,128]{2,1,0:T(8,128)} %a_ref.11) | copy-start | bytes 3145732
  10.6 7.7 %collective-permute-start.1 = (bf16[48,512]{1,0:T(8,128)(2,1)S(1)}, bf16[48,512]{1,0:T(8,128)(2,1)S(1)}, u32[]{:S(2)}, u32[]{:S(2)}) collective-permute-start(bf16[48,512]{1,0:T(8,128)(2,1)S(1)} %bank.1.refs_0_), channel_id=1, source_target_pairs={{0,2},{1,3},{2,4},{3,5},{4,6},{5,7},{6,0},{7,1},{8,10},{9,11},{10,... | collective-permute-start | bytes 147464 | tf_op jit(solution)/shard_map/ppermute | solution.py:47
  11.3 7.0 %collective-permute-start = (bf16[48,512]{1,0:T(8,128)(2,1)S(1)}, bf16[48,512]{1,0:T(8,128)(2,1)S(1)}, u32[]{:S(2)}, u32[]{:S(2)}) collective-permute-start(bf16[48,512]{1,0:T(8,128)(2,1)S(1)} %bank.1.refs_0_), channel_id=1, source_target_pairs={{0,1},{1,2},{2,3},{3,4},{4,5},{5,6},{6,7},{7,0},{8,9},{9,10},{10,1... | collective-permute-start | bytes 147464 | tf_op jit(solution)/shard_map/ppermute | solution.py:47
  14.7 23.2 %collective-permute-start.13 = (f32[16,16]{1,0:T(8,128)S(1)}, f32[16,16]{1,0:T(8,128)S(1)}, u32[]{:S(2)}, u32[]{:S(2)}) collective-permute-start(f32[16,16]{1,0:T(8,128)S(1)} %bitcast.17), channel_id=1, source_target_pairs={{0,24},{8,0},{16,8},{24,16},{1,25},{9,1},{17,9},{25,17},{2,26},{10... | collective-permute-start | bytes 3080 | tf_op jit(solution)/shard_map/ppermute | solution.py:47
  17.2 20.7 %collective-permute-start.12 = (f32[16,16]{1,0:T(8,128)S(1)}, f32[16,16]{1,0:T(8,128)S(1)}, u32[]{:S(2)}, u32[]{:S(2)}) collective-permute-start(f32[16,16]{1,0:T(8,128)S(1)} %bitcast.18), channel_id=1, source_target_pairs={{0,16},{8,24},{16,0},{24,8},{1,17},{9,25},{17,1},{25,9},{2,18},{10... | collective-permute-start | bytes 3080 | tf_op jit(solution)/shard_map/ppermute | solution.py:47
  17.7 20.2 %collective-permute-start.11 = (f32[16,16]{1,0:T(8,128)S(1)}, f32[16,16]{1,0:T(8,128)S(1)}, u32[]{:S(2)}, u32[]{:S(2)}) collective-permute-start(f32[16,16]{1,0:T(8,128)S(1)} %bitcast.19), channel_id=1, source_target_pairs={{0,8},{8,16},{16,24},{24,0},{1,9},{9,17},{17,25},{25,1},{2,10},{10... | collective-permute-start | bytes 3080 | tf_op jit(solution)/shard_map/ppermute | solution.py:47
  18.3 9.0 %collective-permute-start.7 = (bf16[2,128,128]{2,1,0:T(8,128)(2,1)S(1)}, bf16[2,128,128]{2,1,0:T(8,128)(2,1)S(1)}, u32[]{:S(2)}, u32[]{:S(2)}) collective-permute-start(bf16[2,128,128]{2,1,0:T(8,128)(2,1)S(1)} %get-tuple-element.45), channel_id=1, source_target_pairs={{0,1},{1,2},{2,3},{3,4},{4,5},{5,6},{6,7},{7,0},{8,9},{9,10},{10,1... | collective-permute-start | bytes 196616 | tf_op jit(solution)/shard_map/ppermute | solution.py:47
  18.3 9.0 %collective-permute-start.8 = (bf16[2,128,128]{2,1,0:T(8,128)(2,1)S(1)}, bf16[2,128,128]{2,1,0:T(8,128)(2,1)S(1)}, u32[]{:S(2)}, u32[]{:S(2)}) collective-permute-start(bf16[2,128,128]{2,1,0:T(8,128)(2,1)S(1)} %get-tuple-element.46), channel_id=1, source_target_pairs={{0,7},{1,0},{2,1},{3,2},{4,3},{5,4},{6,5},{7,6},{8,15},{9,8},{10,9... | collective-permute-start | bytes 196616 | tf_op jit(solution)/shard_map/ppermute | solution.py:47
  27.4 6.7 %collective-permute-start.9 = (bf16[20,16,128]{2,1,0:T(8,128)(2,1)S(1)}, bf16[20,16,128]{2,1,0:T(8,128)(2,1)S(1)}, u32[]{:S(2)}, u32[]{:S(2)}) collective-permute-start(bf16[20,16,128]{2,1,0:T(8,128)(2,1)S(1)} %pad_maximum_fusion), channel_id=1, source_target_pairs={{0,8},{8,16},{16,24},{24,0},{1,9},{9,17},{17,25},{25,1},{2,10},{10... | collective-permute-start | bytes 245768 | tf_op jit(solution)/shard_map/ppermute | solution.py:47
  29.8 4.5 %collective-permute-start.10 = (bf16[20,16,128]{2,1,0:T(8,128)(2,1)S(1)}, bf16[20,16,128]{2,1,0:T(8,128)(2,1)S(1)}, u32[]{:S(2)}, u32[]{:S(2)}) collective-permute-start(bf16[20,16,128]{2,1,0:T(8,128)(2,1)S(1)} %pad_maximum_fusion.1), channel_id=1, source_target_pairs={{0,24},{8,0},{16,8},{24,16},{1,25},{9,1},{17,9},{25,17},{2,26},{10... | collective-permute-start | bytes 245768 | tf_op jit(solution)/shard_map/ppermute | solution.py:47
  34.0 3.9 %copy-start.4 = (f32[4,64,128]{2,1,0:T(8,128)S(1)}, f32[4,64,128]{2,1,0:T(8,128)}, u32[]{:S(2)}) copy-start(f32[4,64,128]{2,1,0:T(8,128)} %constant.18.clone.refs_0_) | copy-start | bytes 393220
  37.3 8.6 %copy-start.1 = (f32[16,128,128]{2,1,0:T(8,128)S(1)}, f32[16,128,128]{2,1,0:T(8,128)}, u32[]{:S(2)}) copy-start(f32[16,128,128]{2,1,0:T(8,128)} %a_ref.9) | copy-start | bytes 3145732
  37.3 5.6 %collective-permute-start.15 = (bf16[2,128,128]{2,1,0:T(8,128)(2,1)S(1)}, bf16[2,128,128]{2,1,0:T(8,128)(2,1)S(1)}, u32[]{:S(2)}, u32[]{:S(2)}) collective-permute-start(bf16[2,128,128]{2,1,0:T(8,128)(2,1)S(1)} %get-tuple-element.51), channel_id=1, source_target_pairs={{0,7},{1,0},{2,1},{3,2},{4,3},{5,4},{6,5},{7,6},{8,15},{9,8},{10,9... | collective-permute-start | bytes 196616 | tf_op jit(solution)/shard_map/ppermute | solution.py:47
  37.4 5.5 %collective-permute-start.14 = (bf16[2,128,128]{2,1,0:T(8,128)(2,1)S(1)}, bf16[2,128,128]{2,1,0:T(8,128)(2,1)S(1)}, u32[]{:S(2)}, u32[]{:S(2)}) collective-permute-start(bf16[2,128,128]{2,1,0:T(8,128)(2,1)S(1)} %get-tuple-element.57), channel_id=1, source_target_pairs={{0,1},{1,2},{2,3},{3,4},{4,5},{5,6},{6,7},{7,0},{8,9},{9,10},{10,1... | collective-permute-start | bytes 196616 | tf_op jit(solution)/shard_map/ppermute | solution.py:47
  42.9 6.6 %collective-permute-start.16 = (bf16[20,16,128]{2,1,0:T(8,128)(2,1)S(1)}, bf16[20,16,128]{2,1,0:T(8,128)(2,1)S(1)}, u32[]{:S(2)}, u32[]{:S(2)}) collective-permute-start(bf16[20,16,128]{2,1,0:T(8,128)(2,1)S(1)} %pad_maximum_fusion.2), channel_id=1, source_target_pairs={{0,8},{8,16},{16,24},{24,0},{1,9},{9,17},{17,25},{25,1},{2,10},{10... | collective-permute-start | bytes 245768 | tf_op jit(solution)/shard_map/ppermute | solution.py:47
  44.2 5.3 %collective-permute-start.17 = (bf16[20,16,128]{2,1,0:T(8,128)(2,1)S(1)}, bf16[20,16,128]{2,1,0:T(8,128)(2,1)S(1)}, u32[]{:S(2)}, u32[]{:S(2)}) collective-permute-start(bf16[20,16,128]{2,1,0:T(8,128)(2,1)S(1)} %pad_maximum_fusion.3), channel_id=1, source_target_pairs={{0,24},{8,0},{16,8},{24,16},{1,25},{9,1},{17,9},{25,17},{2,26},{10... | collective-permute-start | bytes 245768 | tf_op jit(solution)/shard_map/ppermute | solution.py:47
  52.5 5.7 %collective-permute-start.18 = (bf16[2,128,128]{2,1,0:T(8,128)(2,1)S(1)}, bf16[2,128,128]{2,1,0:T(8,128)(2,1)S(1)}, u32[]{:S(2)}, u32[]{:S(2)}) collective-permute-start(bf16[2,128,128]{2,1,0:T(8,128)(2,1)S(1)} %get-tuple-element.65), channel_id=1, source_target_pairs={{0,1},{1,2},{2,3},{3,4},{4,5},{5,6},{6,7},{7,0},{8,9},{9,10},{10,1... | collective-permute-start | bytes 196616 | tf_op jit(solution)/shard_map/ppermute | solution.py:47
  52.6 5.7 %collective-permute-start.19 = (bf16[2,128,128]{2,1,0:T(8,128)(2,1)S(1)}, bf16[2,128,128]{2,1,0:T(8,128)(2,1)S(1)}, u32[]{:S(2)}, u32[]{:S(2)}) collective-permute-start(bf16[2,128,128]{2,1,0:T(8,128)(2,1)S(1)} %get-tuple-element.66), channel_id=1, source_target_pairs={{0,7},{1,0},{2,1},{3,2},{4,3},{5,4},{6,5},{7,6},{8,15},{9,8},{10,9... | collective-permute-start | bytes 196616 | tf_op jit(solution)/shard_map/ppermute | solution.py:47
  58.3 6.6 %collective-permute-start.20 = (bf16[20,16,128]{2,1,0:T(8,128)(2,1)S(1)}, bf16[20,16,128]{2,1,0:T(8,128)(2,1)S(1)}, u32[]{:S(2)}, u32[]{:S(2)}) collective-permute-start(bf16[20,16,128]{2,1,0:T(8,128)(2,1)S(1)} %pad_maximum_fusion.4), channel_id=1, source_target_pairs={{0,8},{8,16},{16,24},{24,0},{1,9},{9,17},{17,25},{25,1},{2,10},{10... | collective-permute-start | bytes 245768 | tf_op jit(solution)/shard_map/ppermute | solution.py:47
  59.6 5.3 %collective-permute-start.21 = (bf16[20,16,128]{2,1,0:T(8,128)(2,1)S(1)}, bf16[20,16,128]{2,1,0:T(8,128)(2,1)S(1)}, u32[]{:S(2)}, u32[]{:S(2)}) collective-permute-start(bf16[20,16,128]{2,1,0:T(8,128)(2,1)S(1)} %pad_maximum_fusion.5), channel_id=1, source_target_pairs={{0,24},{8,0},{16,8},{24,16},{1,25},{9,1},{17,9},{25,17},{2,26},{10... | collective-permute-start | bytes 245768 | tf_op jit(solution)/shard_map/ppermute | solution.py:47
  67.9 6.1 %collective-permute-start.22 = (bf16[2,128,128]{2,1,0:T(8,128)(2,1)S(1)}, bf16[2,128,128]{2,1,0:T(8,128)(2,1)S(1)}, u32[]{:S(2)}, u32[]{:S(2)}) collective-permute-start(bf16[2,128,128]{2,1,0:T(8,128)(2,1)S(1)} %get-tuple-element.72), channel_id=1, source_target_pairs={{0,1},{1,2},{2,3},{3,4},{4,5},{5,6},{6,7},{7,0},{8,9},{9,10},{10,1... | collective-permute-start | bytes 196616 | tf_op jit(solution)/shard_map/ppermute | solution.py:47
  67.9 6.1 %collective-permute-start.23 = (bf16[2,128,128]{2,1,0:T(8,128)(2,1)S(1)}, bf16[2,128,128]{2,1,0:T(8,128)(2,1)S(1)}, u32[]{:S(2)}, u32[]{:S(2)}) collective-permute-start(bf16[2,128,128]{2,1,0:T(8,128)(2,1)S(1)} %get-tuple-element.73), channel_id=1, source_target_pairs={{0,7},{1,0},{2,1},{3,2},{4,3},{5,4},{6,5},{7,6},{8,15},{9,8},{10,9... | collective-permute-start | bytes 196616 | tf_op jit(solution)/shard_map/ppermute | solution.py:47
  74.1 6.4 %collective-permute-start.24 = (bf16[20,16,128]{2,1,0:T(8,128)(2,1)S(1)}, bf16[20,16,128]{2,1,0:T(8,128)(2,1)S(1)}, u32[]{:S(2)}, u32[]{:S(2)}) collective-permute-start(bf16[20,16,128]{2,1,0:T(8,128)(2,1)S(1)} %pad_maximum_fusion.6), channel_id=1, source_target_pairs={{0,8},{8,16},{16,24},{24,0},{1,9},{9,17},{17,25},{25,1},{2,10},{10... | collective-permute-start | bytes 245768 | tf_op jit(solution)/shard_map/ppermute | solution.py:47
  75.1 5.4 %collective-permute-start.25 = (bf16[20,16,128]{2,1,0:T(8,128)(2,1)S(1)}, bf16[20,16,128]{2,1,0:T(8,128)(2,1)S(1)}, u32[]{:S(2)}, u32[]{:S(2)}) collective-permute-start(bf16[20,16,128]{2,1,0:T(8,128)(2,1)S(1)} %pad_maximum_fusion.7), channel_id=1, source_target_pairs={{0,24},{8,0},{16,8},{24,16},{1,25},{9,1},{17,9},{25,17},{2,26},{10... | collective-permute-start | bytes 245768 | tf_op jit(solution)/shard_map/ppermute | solution.py:47

commit v2 on v1

v2 whole, which is shorter than its diff:
```python
import functools

import jax
import jax.numpy as jnp
import numpy as np
from jax import lax
from jax.experimental import pallas as pl
from jax.experimental.pallas import tpu as pltpu
from jax.sharding import PartitionSpec as P

ITERS = 2
F32 = jnp.float32
BF16 = jnp.bfloat16
HIGHEST = lax.Precision.HIGHEST
VMEM = pl.BlockSpec(memory_space=pltpu.VMEM)
SMEM = pl.BlockSpec(memory_space=pltpu.SMEM)

TILE = 128
HALO = 16
PACK = TILE // HALO
TAP_ROWS = 48


def lanes(shape):
    return lax.broadcasted_iota(jnp.int32, shape, len(shape) - 1)


def sublanes(shape):
    return lax.broadcasted_iota(jnp.int32, shape, len(shape) - 2)


def call(body, outs, specs, scratch=(), name=None, flops=0, mib=16):
    return pl.pallas_call(
        body,
        out_shape=outs,
        in_specs=specs,
        out_specs=jax.tree.map(lambda _: VMEM, outs),
        scratch_shapes=list(scratch),
        compiler_params=pltpu.CompilerParams(vmem_limit_bytes=mib * 1024 * 1024),
        cost_estimate=pl.CostEstimate(flops=flops, bytes_accessed=1 << 20, transcendentals=0),
        name=name,
    )


def shift(cells, axis, by):
    count = lax.axis_size(axis)
    return lax.ppermute(cells, axis, [(i, (i + by) % count) for i in range(count)])


def swap(cells, axis, pairs):
    return lax.ppermute(cells, axis, pairs + [(j, i) for i, j in pairs])


def gathered(piece, axis):
    count = lax.axis_size(axis)
    if count <= 8:
        return [piece] + [shift(piece, axis, s) for s in range(1, count)]
    every = lax.all_gather(piece, axis, axis=0)
    me = lax.axis_index(axis)
    return [lax.dynamic_index_in_dim(every, (me - s) % count, 0, False) for s in range(count)]


def swap_pairs(cells, axis):
    return swap(cells, axis, [(i, i + 1) for i in range(0, lax.axis_size(axis), 2)])


def bank_kernel(bank_ref, ids_ref, mix_ref, out_ref, keys_ref):
    rows, taps = bank_ref.shape
    for block in range(rows // TILE):
        part = bank_ref[block * TILE : (block + 1) * TILE, :]
        part = jnp.concatenate([part, jnp.zeros((TILE, TILE - taps), F32)], axis=1)
        out_ref[:, block * TILE : (block + 1) * TILE] = part.T[:TAP_ROWS].astype(BF16)
    spread = (lanes((ids_ref.shape[1], TILE)) >> 3 == sublanes((ids_ref.shape[1], TILE))).astype(F32)
    both = jnp.concatenate([ids_ref[...].astype(F32), mix_ref[...]], axis=0)
    keys_ref[...] = jnp.dot(both, spread, precision=HIGHEST, preferred_element_type=F32)


def pick_kernel(cols, meta_ref, mine_ref, other_ref, *refs):
    pieces, outs = refs[:-2], refs[-2:]
    zones = pieces[0].shape[1] // TILE
    for keys_ref, out_ref in zip((mine_ref, other_ref), outs):
        ids = (keys_ref[...] + 0.5).astype(jnp.int32)
        for k in range(out_ref.shape[0]):
            got = jnp.zeros((TAP_ROWS, TILE), F32)
            for s, piece in enumerate(pieces):
                first = lax.rem(meta_ref[5] + cols - 2 * s, cols) * zones
                for m in range(zones):
                    got = jnp.where(
                        ids[k : k + 1] == first + m, piece[:, m * TILE : (m + 1) * TILE].astype(F32), got
                    )
            out_ref[k] = got.astype(BF16)


def taps_kernel(taps, keys_ref, mine_ref, other_ref, uv_ref):
    blended = mine_ref.shape[0]
    lane = lanes((1, TILE))
    is_row = (lane & 7) < 4
    picked = []
    total = jnp.zeros((1, TILE), F32)
    mix = keys_ref[blended:, :]
    for k in range(blended):
        got = mine_ref[k].astype(F32) + other_ref[k].astype(F32)
        sums = jnp.sum(got, axis=0, keepdims=True)
        both = sums * pltpu.roll(sums, TILE - 4, 1)
        total = total + jnp.where(is_row, both * mix[k : k + 1], 0.0)
        picked.append(got)
    group = (lanes((TILE, TILE)) >> 3) == (sublanes((TILE, TILE)) >> 3)
    total = jnp.dot(
        jnp.broadcast_to(total, (8, TILE)),
        group.astype(F32),
        precision=HIGHEST,
        preferred_element_type=F32,
    )[:1]
    tap = sublanes((TAP_ROWS, 2 * TILE))
    at = lanes((TAP_ROWS, 2 * TILE))
    half = taps // 2
    goes = jnp.where(at < TILE, (tap - half) & (TILE - 1), TILE + ((half - tap) & (TILE - 1)))
    place = ((goes == at) & (tap < taps)).astype(F32).astype(BF16)
    for k in range(blended):
        got = picked[k]
        scaled = mix[k : k + 1] * got / total
        chosen = jnp.where(is_row, scaled, got).astype(BF16)
        uv_ref[k] = lax.dot_general(
            chosen, place, (((0,), (0,)), ((), ())), preferred_element_type=F32
        ).reshape(uv_ref.shape[1:])


def turned(uv_ref, z, k, r, part, rows, by):
    line = uv_ref[k, z, r : r + 1, part * TILE : (part + 1) * TILE]
    return pltpu.roll(
        jnp.broadcast_to(line, (rows, TILE)), by % TILE, 1, stride=1, stride_axis=0
    )


def bands_kernel(part, rows, meta_ref, uv_ref, *refs):
    *refs, shifts_ref = refs
    if part == 0:
        (ct_ref,) = refs
    else:
        inverse_ref, illum, (ct_ref, inv_ref) = refs[0], refs[1 : 1 + rows], refs[1 + rows :]
        coarse = illum[0].shape[2]
        smooth = jnp.zeros((TILE, illum[0].shape[0]), F32)
        for s in range(rows):
            first = pl.multiple_of(lax.rem(meta_ref[4] + rows - s, rows) * coarse, coarse)
            smooth = smooth + lax.dot_general(
                inverse_ref[meta_ref[4], pl.ds(first, coarse), :],
                illum[s][:, 0, :].T,
                (((0,), (0,)), ((), ())),
                precision=HIGHEST,
                preferred_element_type=F32,
            )
        inv = 1.0 / smooth
        for g in range(inv_ref.shape[0]):
            inv_ref[g] = inv[:, g * PACK : (g + 1) * PACK]
    low_all = lanes((TILE, TILE)) < TILE // 2
    none = jnp.zeros((TILE, TILE), BF16)
    for t in range(PACK):
        to = (sublanes((TILE, TILE)) + t * HALO) & (TILE - 1)
        shifts_ref[:, t * TILE : (t + 1) * TILE] = (to == lanes((TILE, TILE))).astype(F32).astype(BF16)
    ct_ref[:, TILE:, :] = jnp.zeros((ct_ref.shape[0], TILE, 8 * TILE), BF16)

    def group(g8, carry):
        for i in range(PACK):
            z = g8 * PACK + i
            left, right = TILE + i * HALO, TILE + (i + 4) % PACK * HALO
            base = [turned(uv_ref, z, j // 4, 4 + j % 4, 1 - part, HALO, 0) for j in range(8)]
            base = jnp.concatenate(base, axis=0).astype(BF16)
            for t in range(0, PACK, 2):
                got = jnp.dot(
                    base, shifts_ref[:, t * TILE : (t + 2) * TILE], preferred_element_type=F32
                ).astype(BF16)
                first, second = got[:, :TILE], got[:, TILE:]
                if t == 0:
                    first, after = jnp.where(low_all, first, none), jnp.where(low_all, none, first)
                elif t == PACK - 2:
                    second, before = jnp.where(low_all, none, second), jnp.where(low_all, second, none)
                for j in range(8):
                    here, rows = slice(j * TILE, (j + 1) * TILE), slice(j * HALO, (j + 1) * HALO)
                    ct_ref[z, t * HALO : (t + 1) * HALO, here] = first[rows]
                    ct_ref[z, (t + 1) * HALO : (t + 2) * HALO, here] = second[rows]
                    if t == 0:
                        ct_ref[z, right : right + HALO, here] = after[rows]
                    elif t == PACK - 2:
                        ct_ref[z, left : left + HALO, here] = before[rows]
        return carry

    lax.fori_loop(0, ct_ref.shape[0] // PACK, group, 0)


def other_bands(part, uv_ref, ct_ref, z, i, cw_ref, rt_ref, edge_ref):
    low = lanes((HALO, TILE)) < TILE // 2
    lane = lanes((HALO, TILE)) >> 4
    none = jnp.zeros((HALO, TILE), F32)
    above, below = [none] * 2, [none] * 2
    for j in range(8):
        here = slice(j * TILE, (j + 1) * TILE)
        full = turned(uv_ref, z, j // 4, j % 4, part, TILE, 0)
        first, last = full[:HALO], full[TILE - HALO :]
        rt_ref[z, :HALO, here] = jnp.where(low, first, none).astype(BF16)
        rt_ref[z, HALO : TILE - HALO, here] = full[HALO : TILE - HALO].astype(BF16)
        rt_ref[z, TILE - HALO :, here] = jnp.where(low, none, last).astype(BF16)
        spot = (j % 4) * 2
        above[j // 4] = jnp.where(lane == spot, full[(spot + 1) * HALO : (spot + 2) * HALO], above[j // 4])
        below[j // 4] = jnp.where(lane == spot + 1, full[spot * HALO : (spot + 1) * HALO], below[j // 4])
    edge_ref[z] = jnp.concatenate(
        [jnp.concatenate(above, axis=1), jnp.concatenate(below, axis=1)], axis=0
    ).astype(BF16)
    before, after = TILE + i * HALO, TILE + (i + 4) % PACK * HALO
    cw_ref[z, TILE - 2 * HALO :, :] = jnp.zeros((2 * HALO, 4 * TILE), BF16)
    for j in range(0, 8, 2):
        this, other = slice(j * TILE, (j + 1) * TILE), slice((j + 1) * TILE, (j + 2) * TILE)
        for t in range(6):
            a = before if t == 0 else (t - 1) * HALO
            b = after if t == 5 else (t + 3) * HALO
            cw_ref[z, t * HALO : (t + 1) * HALO, j * TILE // 2 : j * TILE // 2 + TILE] = jnp.where(
                low, ct_ref[z, a : a + HALO, this], ct_ref[z, b : b + HALO, other]
            )


def sides_of(left, right, meta_ref):
    left = jnp.where(meta_ref[0] > 0, left, jnp.zeros_like(left))
    right = jnp.where(meta_ref[1] > 0, right, jnp.zeros_like(right))
    return left, right


def joined(left, right, parity):
    low = lanes(left.shape) < TILE // 2
    return jnp.where(low, left, right) if parity == 0 else jnp.where(low, right, left)


def windows(field, left, right, i):
    lane = lanes(field.shape)
    left = pltpu.roll(left, -i * HALO % TILE, 1)
    right = pltpu.roll(right, (80 - (i + 4) % PACK * HALO) % TILE, 1)
    first = jnp.where(lane < HALO, left, pltpu.roll(field, HALO, 1))
    second = jnp.where(lane < 80, pltpu.roll(field, 80, 1), right)
    return first, second


def column_pass(wide, cw_ref, z, q_ref, slot):
    rows = wide.shape[0] // 2
    low = lanes((rows, TILE)) < TILE // 2
    for n in range(2):
        got = jnp.dot(
            wide, cw_ref[z, :, n * 256 : (n + 1) * 256], preferred_element_type=F32
        ).astype(BF16)
        for p in range(2):
            first, second = got[:rows, p * TILE : (p + 1) * TILE], got[rows:, p * TILE : (p + 1) * TILE]
            at = (n * 4 + p * 2) * rows
            q_ref[slot, at : at + rows, :] = jnp.where(low, first, pltpu.roll(second, TILE // 2, 1))
            q_ref[slot, at + rows : at + 2 * rows, :] = jnp.where(low, pltpu.roll(first, TILE // 2, 1), second)


def pack_strips(value, i, g8, rows, right_ref, left_ref):
    lane = lanes(value.shape) >> 4
    at = (i + 4) % PACK
    to_right = pltpu.roll(value, (i * HALO - 112) % TILE, 1)
    to_left = pltpu.roll(value, at * HALO, 1)
    if i == 0:
        right_ref[g8, rows] = to_right
        left_ref[g8, rows] = to_left
    else:
        right_ref[g8, rows] = jnp.where(lane == i, to_right, right_ref[g8, rows])
        left_ref[g8, rows] = jnp.where(lane == at, to_left, left_ref[g8, rows])


def finish(part, blurred, g8, i, rows, a_ref, inv_ref, outs):
    z = g8 * PACK + i
    if part == 0:
        value = a_ref[z, rows] / blurred
    else:
        value = a_ref[z, rows] * blurred * inv_ref[g8, rows, i : i + 1]
        outs[0][z, rows] = value
        outs = outs[1:]
    if outs:
        b_ref, right_ref, left_ref = outs
        value = value.astype(BF16)
        b_ref[z, rows] = value
        pack_strips(value, i, g8, rows, right_ref, left_ref)


def main_kernel(part, making, meta_ref, ct_ref, rt_ref, field_ref, left_ref, right_ref, a_ref, inv_ref, rim_ref, *refs):
    outs, q_ref = refs[:-1], refs[-1]
    if making:
        outs, made, uv_ref, rt_ref = outs[:-3], outs[-3:], rt_ref, outs[-2]
    inner = slice(HALO, TILE - HALO)

    def group(g8, carry):
        sides = sides_of(left_ref[g8], right_ref[g8], meta_ref)
        halos = [joined(*sides, parity) for parity in range(2)]

        def columns(i):
            if making:
                other_bands(part, uv_ref, ct_ref, g8 * PACK + i, i, *made)
            wide = jnp.concatenate([field_ref[g8 * PACK + i], halos[i // 4]], axis=1)
            for n in range(4):
                got = jnp.dot(
                    wide, ct_ref[g8 * PACK + i, :, n * 256 : (n + 1) * 256], preferred_element_type=F32
                ).astype(BF16)
                q_ref[i % 4, n * 256 : n * 256 + TILE, :] = got[:, :TILE]
                q_ref[i % 4, n * 256 + TILE : (n + 1) * 256, :] = got[:, TILE:]

        def rows(i):
            z = g8 * PACK + i
            blurred = jnp.dot(rt_ref[z], q_ref[i % 4], preferred_element_type=F32)
            rim_ref[z, :HALO] = blurred[:HALO]
            rim_ref[z, HALO:] = blurred[TILE - HALO :]
            finish(part, blurred[inner], g8, i, inner, a_ref, inv_ref, outs)

        columns(0)
        columns(1)
        for i in range(PACK):
            if i + 2 < PACK:
                columns(i + 2)
            rows(i)
        return carry

    for g8 in range(field_ref.shape[0] // PACK):
        group(g8, 0)


def edge_kernel(part, meta_ref, cw_ref, edge_ref, rim_ref, top_ref, bot_ref, a_ref, inv_ref, *refs):
    count = len(refs) // 2
    made, outs, q_ref = refs[:count], refs[count:-1], refs[-1]
    depth = rim_ref.shape[0]
    inner = slice(HALO, TILE - HALO)

    def group(g8, carry):
        halos = [sides_of(ref[depth + g8], ref[depth + 2 + g8], meta_ref) for ref in (top_ref, bot_ref)]
        for old, new in zip(made, outs):
            each = pl.ds(g8 * (new.shape[0] // (depth // PACK)), new.shape[0] // (depth // PACK))
            new[each, inner] = old[each, inner]

        def columns(i):
            z = g8 * PACK + i
            pairs = []
            for s, ref in enumerate((top_ref, bot_ref)):
                both = windows(ref[z], *halos[s], i)
                pairs.append([jnp.where(meta_ref[2 + s] > 0, w, jnp.zeros_like(w)) for w in both])
            wide = jnp.concatenate([pairs[0][0], pairs[1][0], pairs[0][1], pairs[1][1]], axis=0)
            column_pass(wide, cw_ref, z, q_ref, i)

        def rows(i):
            z = g8 * PACK + i
            blurred = rim_ref[z] + jnp.dot(edge_ref[z], q_ref[i], preferred_element_type=F32)
            for s, at in enumerate((slice(0, HALO), slice(TILE - HALO, TILE))):
                finish(part, blurred[s * HALO : (s + 1) * HALO], g8, i, at, a_ref, inv_ref, outs)

        for i in range(PACK):
            columns(i)
        for i in range(PACK):
            rows(i)
        return carry

    for g8 in range(depth // PACK):
        group(g8, 0)


def first_kernel(est_ref, b_ref, right_ref, left_ref):
    def group(g8, carry):
        for i in range(PACK):
            value = est_ref[g8 * PACK + i].astype(BF16)
            b_ref[g8 * PACK + i] = value
            pack_strips(value, i, g8, slice(0, TILE), right_ref, left_ref)
        return carry

    lax.fori_loop(0, est_ref.shape[0] // PACK, group, 0)


def smoothing(length, rows):
    stiffness = float(length * length) / 16.0
    d = np.diff(np.eye(length), axis=0)
    inverse = np.linalg.inv(np.eye(length) + stiffness * d.T @ d)
    wide = np.repeat(inverse, TILE * rows // length, axis=0)
    return jnp.asarray(wide.reshape(rows, TILE, length).transpose(0, 2, 1), F32)


def shards(observed, estimate, psf_bank, zone_ids, mix_weights, illumination):
    depth = estimate.shape[0]
    zones_here, _, _, rank, taps = psf_bank.shape
    n_row, n_col = lax.axis_size("row"), lax.axis_size("col")
    row, col = lax.axis_index("row"), lax.axis_index("col")
    groups = depth // PACK
    flag = lambda x: x.astype(jnp.int32)
    meta = jnp.stack(
        [flag(col > 0), flag(col < n_col - 1), flag(row > 0), flag(row < n_row - 1), flag(row), flag(col)]
    )
    volume = jax.ShapeDtypeStruct((depth, TILE, TILE), F32)
    narrow = jax.ShapeDtypeStruct((depth, TILE, TILE), BF16)
    strip = jax.ShapeDtypeStruct((groups, TILE, TILE), BF16)


    def exchanged(to_right, to_left):
        return shift(to_right, "col", 1), shift(to_left, "col", -1)

    blended = zone_ids.shape[-1]
    flat = (zones_here * depth * 2 * rank, taps)
    bank, keys = call(
        bank_kernel,
        (
            jax.ShapeDtypeStruct((TAP_ROWS, zones_here * TILE), BF16),
            jax.ShapeDtypeStruct((2 * blended, TILE), F32),
        ),
        [VMEM] * 3,
        name="bank",
    )(psf_bank.reshape(flat), zone_ids[0, 0].T, mix_weights[0, 0].T)
    pieces = [bank] + [shift(bank, "col", s) for s in range(2, n_col, 2)]
    other_keys = swap_pairs(keys, "col")
    field, to_right, to_left = call(
        first_kernel, (narrow, strip, strip), [VMEM], name="first"
    )(estimate)
    left, right = exchanged(to_right, to_left)
    inverse = smoothing(illumination.shape[1] * n_row, n_row)
    factors = jax.ShapeDtypeStruct((blended, TAP_ROWS, TILE), BF16)
    mine, others = call(
        functools.partial(pick_kernel, n_col),
        (factors, factors),
        [SMEM] + [VMEM] * (2 + len(pieces)),
        name="pick",
    )(meta, keys, other_keys, *pieces)
    uv = call(
        functools.partial(taps_kernel, taps),
        jax.ShapeDtypeStruct((blended, depth, 2 * rank, 2 * TILE), F32),
        [VMEM] * 3,
        name="taps",
    )(keys, mine, swap_pairs(others, "col"))

    shape = lambda *s: jax.ShapeDtypeStruct((depth,) + s, BF16)

    def bands(part, uv):
        outs = (shape(2 * TILE, 8 * TILE),)
        args = [meta, uv]
        if part == 1:
            outs = outs + (jax.ShapeDtypeStruct((groups, TILE, PACK), F32),)
            args = args + [inverse] + profiles
        return call(
            functools.partial(bands_kernel, part, n_row),
            outs,
            [SMEM] + [VMEM] * (len(args) - 1),
            [pltpu.VMEM((TILE, 8 * TILE), BF16)],
            name="bands",
            flops=4 * 10**9,
        )(*args)

    def ends_of(field, left, right):
        return [
            jnp.concatenate([field[:, rows], left[:, rows], right[:, rows]], axis=0)
            for rows in (slice(0, HALO), slice(TILE - HALO, TILE))
        ]

    def blur(part, last, made, field, left, right, ends, other):
        ct, inv, *ready = made
        making = () if ready else (shape(TILE, 4 * TILE), shape(TILE, 8 * TILE), shape(2 * HALO, 2 * TILE))
        bot, top = shift(ends[0], "row", -1), shift(ends[1], "row", 1)
        rim = jax.ShapeDtypeStruct((depth, 2 * HALO, TILE), F32)
        outs = ((volume,) if part == 1 else ()) + (() if last else (narrow, strip, strip))
        main, *got = call(
            functools.partial(main_kernel, part, bool(making)),
            (rim,) + outs + making,
            [SMEM] + [VMEM] * 7,
            [pltpu.VMEM((4, 8 * TILE, TILE), BF16)],
            name="main",
            flops=4 * 10**9,
        )(meta, ct, uv if making else ready[1], field, left, right, other, inv)
        if making:
            got, ready = got[:-3], got[-3:]
        cw, rt, edge = ready
        done = call(
            functools.partial(edge_kernel, part),
            outs,
            [SMEM] + [VMEM] * (7 + len(outs)),
            [pltpu.VMEM((PACK, 2 * TILE, TILE), BF16)],
            name="edge",
            flops=2 * 10**9,
        )(meta, cw, edge, main, top, bot, other, inv, *got)
        return done, (ct, inv, cw, rt, edge)

    current = estimate
    ends = ends_of(field, left, right)
    first_end, last_end, profile, uv = lax.optimization_barrier((*ends, illumination.transpose(0, 2, 1), uv))
    ends = [first_end, last_end]
    profiles = gathered(profile, "row")
    forward = (*bands(0, uv), jnp.zeros((groups, TILE, PACK), F32))
    backward = None
    for step in range(ITERS):
        last = step == ITERS - 1
        (ratio, *strips), forward = blur(0, False, forward, field, left, right, ends, observed)
        left, right = exchanged(*strips)
        ends = ends_of(ratio, left, right)
        if backward is None:
            backward = bands(1, lax.optimization_barrier((uv, strips[0]))[0])
        (current, *rest), backward = blur(1, last, backward, ratio, left, right, ends, current)
        if not last:
            field, (left, right) = rest[0], exchanged(*rest[1:])
            ends = ends_of(field, left, right)
    return current


def solution(mesh):
    placed = (
        P(None, "row", "col"),
        P(None, "row", "col"),
        P(("row", "col"), None, None, None, None),
        P("row", "col", None, None),
        P("row", "col", None, None),
        P(None, "row", "col"),
    )
    return jax.shard_map(
        shards, mesh=mesh, in_specs=placed, out_specs=P(None, "row", "col"), check_vma=False
    )
```

time: 84.6 us -> 74.7 us (0.88)
  Pallas kernels: 37.7 us -> 28.5 us
  local copies, waits for them, and re-layouts: 4.79 us -> 3.71 us
    pallas_call x4, Pallas kernels: 12.9 us -> 7.67 us  [blur(): call(functools.partial(edge_kernel, part), outs, [SMEM] + [VMEM] * (7 + l...]
    pallas_call x2, Pallas kernels: 9.07 us -> 5.43 us  [bands(): call(functools.partial(bands_kernel, part, n_row), outs, [SMEM] + [VMEM]...]
    broadcast_in_dim x3 -> x1, local copies, waits for them, and re-layouts: 1.51 us -> 0.01 us  [shards(): forward = (*bands(0, uv), jnp.zeros((groups, TILE, PACK), F32))]
    unnamed x11 -> x16, local copies, waits for them, and re-layouts: 2.96 us -> 3.55 us
    pallas_call x6 -> x7, Pallas kernels: 15.3 us -> 14.9 us  [the longest x4 13.6 us: blur(): call(functools.partial(main_kernel, part, bool(making)), (rim,) + outs +...]
    ppermute x26 -> x22, waiting for transfers between devices: 5.24 us -> 5.58 us  [shift(): lax.ppermute(cells, axis, [(i, (i + by) % count) for i in range(count)])]
    ppermute x26 -> x22, starting transfers between devices: 36.2 us -> 36.2 us  [shift(): lax.ppermute(cells, axis, [(i, (i + by) % count) for i in range(count)])]
  transfers between devices with their start and end apart: 26 -> 24, of which waited for: 4 -> 4; matrix products, arithmetic and copies ran while one was open for 3% -> 0% of each run, Pallas kernels for 33% -> 29%
where the time goes in v2:
time: 74.7 us; the launch traced here: 74.5 us
  starting transfers between devices  36.3 us (49%)
  Pallas kernels  28.5 us (38%)
  waiting for transfers between devices  5.62 us (8%)
  local copies, waits for them, and re-layouts  3.71 us (5%)
    ppermute x22, starting transfers between devices, shift(): lax.ppermute(cells, axis, [(i, (i + by) % count) for i in range(count)])  36.2 us
    pallas_call x4, Pallas kernels, blur(): call(functools.partial(main_kernel, part, bool(making)), (rim,) + outs +...  13.6 us
    pallas_call x4, Pallas kernels, blur(): call(functools.partial(edge_kernel, part), outs, [SMEM] + [VMEM] * (7 + l...  7.67 us
    ppermute x22, waiting for transfers between devices, shift(): lax.ppermute(cells, axis, [(i, (i + by) % count) for i in range(count)])  5.58 us
    pallas_call x2, Pallas kernels, bands(): call(functools.partial(bands_kernel, part, n_row), outs, [SMEM] + [VMEM]...  5.43 us
    unnamed x16, local copies, waits for them, and re-layouts  3.55 us
  transfers between devices with their start and end apart: 24, of which 4 were waited for; matrix products, arithmetic and copies ran while one was open for 0% of the time, Pallas kernels for 29%

profile of v2, /device:TPU:0, one launch (start us, length us, event | category | flops | bytes accessed | tf_op | source)
XLA Modules:
  0.0 74.5 jit_solution(10097323107422245059)
XLA Ops:
  0.0 0.9 %copy-done.2 = f32[4,16,2,4,33]{4,3,2,1,0:T(4,128)S(1)} copy-done((f32[4,16,2,4,33]{4,3,2,1,0:T(4,128)S(1)}, f32[4,16,2,4,33]{4,3,2,1,0:T(4,128)}, u32[]{:S(2)}) %copy-start.2) | copy-done | bytes 67608
  1.0 0.7 copy-done.3
  1.6 0.7 copy-done.4
  2.3 0.1 bank.1
  2.4 5.1 %collective-permute-start.5 = (bf16[48,512]{1,0:T(8,128)(2,1)S(1)}, bf16[48,512]{1,0:T(8,128)(2,1)S(1)}, u32[]{:S(2)}, u32[]{:S(2)}) collective-permute-start(bf16[48,512]{1,0:T(8,128)(2,1)S(1)} %get-tuple-element.54.refs_0_), channel_id=1, source_target_pairs={{0,6},{1,7},{2,0},{3,1},{4,2},{5,3},{6,4},{7,5},{8,14},{9,15},{10,... | collective-permute-start | bytes 147464 | tf_op jit(solution)/shard_map/ppermute | solution.py:47
  7.5 0.0 collective-permute-start.4
  7.5 1.0 %collective-permute-start.3 = (bf16[48,512]{1,0:T(8,128)(2,1)S(1)}, bf16[48,512]{1,0:T(8,128)(2,1)S(1)}, u32[]{:S(2)}, u32[]{:S(2)}) collective-permute-start(bf16[48,512]{1,0:T(8,128)(2,1)S(1)} %get-tuple-element.54.refs_0_), channel_id=1, source_target_pairs={{0,2},{1,3},{2,4},{3,5},{4,6},{5,7},{6,0},{7,1},{8,10},{9,11},{10,... | collective-permute-start | bytes 147464 | tf_op jit(solution)/shard_map/ppermute | solution.py:47
  8.5 0.0 collective-permute-start.2
  8.5 1.2 %copy-done = f32[16,128,128]{2,1,0:T(8,128)S(1)} copy-done((f32[16,128,128]{2,1,0:T(8,128)S(1)}, f32[16,128,128]{2,1,0:T(8,128)}, u32[]{:S(2)}) %copy-start) | copy-done | bytes 1048600
  9.8 0.4 first.1
  10.2 0.6 collective-permute-start
  10.8 0.1 stack.43.meta_ref
  10.9 3.1 %collective-permute-start.1 = (bf16[2,128,128]{2,1,0:T(8,128)(2,1)S(1)}, bf16[2,128,128]{2,1,0:T(8,128)(2,1)S(1)}, u32[]{:S(2)}, u32[]{:S(2)}) collective-permute-start(bf16[2,128,128]{2,1,0:T(8,128)(2,1)S(1)} %get-tuple-element.52), channel_id=1, source_target_pairs={{0,7},{1,0},{2,1},{3,2},{4,3},{5,4},{6,5},{7,6},{8,15},{9,8},{10,9... | collective-permute-start | bytes 196616 | tf_op jit(solution)/shard_map/ppermute | solution.py:47
  13.9 0.0 collective-permute-done.5.refs_3_
  13.9 0.0 collective-permute-done.4.refs_2_
  13.9 0.0 collective-permute-done.3.refs_1_
  13.9 0.7 pick.1
  14.6 0.1 collective-permute-start.6
  14.7 1.0 %collective-permute-done.left_ref = bf16[2,128,128]{2,1,0:T(8,128)(2,1)S(1)} collective-permute-done((bf16[2,128,128]{2,1,0:T(8,128)(2,1)S(1)}, bf16[2,128,128]{2,1,0:T(8,128)(2,1)S(1)}, u32[]{:S(2)}, u32[]{:S(2)}) %collective-permute-start) | collective-permute-done | bytes 65568 | tf_op jit(solution)/shard_map/ppermute | solution.py:47
  15.7 0.1 collective-permute-done.1.right_ref
  15.9 0.0 collective-permute-done.6.other_ref
  15.9 0.5 taps.1.uv_ref.rt_ref
  16.4 0.0 copy-start.5
  16.4 2.5 %collective-permute-start.11 = (f32[16,1,16]{2,1,0:T(1,128)}, f32[16,1,16]{2,1,0:T(1,128)S(1)}, u32[]{:S(2)}, u32[]{:S(2)}) collective-permute-start(f32[16,1,16]{2,1,0:T(1,128)} %bitcast.17), channel_id=1, source_target_pairs={{0,24},{8,0},{16,8},{24,16},{1,25},{9,1},{17,9},{25,17},{2,26},{10... | collective-permute-start | bytes 3080 | tf_op jit(solution)/shard_map/ppermute | solution.py:47
  18.9 0.5 collective-permute-start.10
  19.4 0.6 collective-permute-start.9
  20.0 2.4 %collective-permute-start.7 = (bf16[20,16,128]{2,1,0:T(8,128)(2,1)S(1)}, bf16[20,16,128]{2,1,0:T(8,128)(2,1)S(1)}, u32[]{:S(2)}, u32[]{:S(2)}) collective-permute-start(bf16[20,16,128]{2,1,0:T(8,128)(2,1)S(1)} %get-tuple-element.61), channel_id=1, source_target_pairs={{0,8},{8,16},{16,24},{24,0},{1,9},{9,17},{17,25},{25,1},{2,10},{10... | collective-permute-start | bytes 245768 | tf_op jit(solution)/shard_map/ppermute | solution.py:47
  22.4 0.5 collective-permute-start.8
  22.9 2.5 %bands.2.ct_ref = bf16[16,256,1024]{2,1,0:T(8,128)(2,1)S(1)} custom-call(s32[6]{0:T(128)S(1)} %stack.43.meta_ref, f32[2,16,8,256]{3,2,1,0:T(8,128)S(1)} %taps.1.uv_ref.rt_ref), custom_call_target="tpu_custom_call" | custom-call | flops 4000000000 | bytes 1048576 | tf_op jit(solution)/shard_map/bands/pallas_call | solution.py:436
  25.5 3.9 %main.4 = (f32[16,32,128]{2,1,0:T(8,128)S(1)}, bf16[16,128,128]{2,1,0:T(8,128)(2,1)S(1)}, bf16[2,128,128]{2,1,0:T(8,128)(2,1)S(1)}, bf16[2,128,128]{2,1,0:T(8,12...) custom-call(s32[6]{0:T(128)S(1)} %stack.43.meta_ref, ...), custom_call_target="tpu_custom_call" | custom-call | flops 4000000000 | bytes 1048576 | tf_op jit(solution)/shard_map/main/pallas_call | solution.py:457
  29.4 0.0 copy-start.7
  29.4 0.0 collective-permute-done.7.top_ref
  29.4 1.7 %edge.4 = (bf16[16,128,128]{2,1,0:T(8,128)(2,1)S(1)}, bf16[2,128,128]{2,1,0:T(8,128)(2,1)S(1)}, bf16[2,128,128]{2,1,0:T(8,128)(2,1)S(1)}) custom-call(s32[6]{0:T(128)S(1)} %stack.43.meta_ref, bf16[16,128,512]{2,1,0:T(8,128)(2,1)S(1)} %get-tuple-element.58.cw_ref, bf16[16,32,256]{2,1,0:T(8,128)(2,1)S(1)} %get-tuple-element.59.edge_ref, ...), custom_call_target="tpu_custom_call" | custom-call | flops 2000000000 | bytes 1048576 | tf_op jit(solution)/shard_map/edge/pallas_call | solution.py:468
  31.1 0.1 collective-permute-start.12
  31.1 0.0 copy-start.1
  31.1 3.5 %collective-permute-start.13 = (bf16[2,128,128]{2,1,0:T(8,128)(2,1)S(1)}, bf16[2,128,128]{2,1,0:T(8,128)(2,1)S(1)}, u32[]{:S(2)}, u32[]{:S(2)}) collective-permute-start(bf16[2,128,128]{2,1,0:T(8,128)(2,1)S(1)} %get-tuple-element.71), channel_id=1, source_target_pairs={{0,7},{1,0},{2,1},{3,2},{4,3},{5,4},{6,5},{7,6},{8,15},{9,8},{10,9... | collective-permute-start | bytes 196616 | tf_op jit(solution)/shard_map/ppermute | solution.py:47
  34.7 0.0 collective-permute-done.11.refs_4_
  34.7 0.0 collective-permute-done.10.refs_3_
  34.7 2.9 %bands.3 = (bf16[16,256,1024]{2,1,0:T(8,128)(2,1)S(1)}, f32[2,128,8]{2,1,0:T(8,128)S(1)}) custom-call(s32[6]{0:T(128)S(1)} %stack.43.meta_ref, f32[2,16,8,256]{3,2,1,0:T(8,128)S(1)} %taps.1.uv_ref.rt_ref, f32[4,64,128]{2,1,0:T(8,128)S(1)} %copy-done.7, f32[16,1,16]{2,1,0:T(1,128)S(1)} %bitcast.20, f32[16,1,16]{2,1,0:T(1,128)S(1)} %collective-permute-done.9.refs_2_, ...), custom_call_target="tpu_custom_call" | custom-call | flops 4000000000 | bytes 1048576 | tf_op jit(solution)/shard_map/bands/pallas_call | solution.py:436
  37.6 0.0 collective-permute-done.13.right_ref
  37.7 1.5 %collective-permute-start.14 = (bf16[20,16,128]{2,1,0:T(8,128)(2,1)S(1)}, bf16[20,16,128]{2,1,0:T(8,128)(2,1)S(1)}, u32[]{:S(2)}, u32[]{:S(2)}) collective-permute-start(bf16[20,16,128]{2,1,0:T(8,128)(2,1)S(1)} %pad_maximum_fusion.2), channel_id=1, source_target_pairs={{0,8},{8,16},{16,24},{24,0},{1,9},{9,17},{17,25},{25,1},{2,10},{10... | collective-permute-start | bytes 245768 | tf_op jit(solution)/shard_map/ppermute | solution.py:47
  39.2 1.7 %collective-permute-start.15 = (bf16[20,16,128]{2,1,0:T(8,128)(2,1)S(1)}, bf16[20,16,128]{2,1,0:T(8,128)(2,1)S(1)}, u32[]{:S(2)}, u32[]{:S(2)}) collective-permute-start(bf16[20,16,128]{2,1,0:T(8,128)(2,1)S(1)} %pad_maximum_fusion.3), channel_id=1, source_target_pairs={{0,24},{8,0},{16,8},{24,16},{1,25},{9,1},{17,9},{25,17},{2,26},{10... | collective-permute-start | bytes 245768 | tf_op jit(solution)/shard_map/ppermute | solution.py:47
  40.9 3.8 %main.5 = (f32[16,32,128]{2,1,0:T(8,128)S(1)}, f32[16,128,128]{2,1,0:T(8,128)S(1)}, bf16[16,128,128]{2,1,0:T(8,128)(2,1)S(1)}, bf16[2,128,128]{2,1,0:T(8,128)(2,...) custom-call(s32[6]{0:T(128)S(1)} %stack.43.meta_ref, ...), custom_call_target="tpu_custom_call" | custom-call | flops 4000000000 | bytes 1048576 | tf_op jit(solution)/shard_map/main/pallas_call | solution.py:457
  44.7 0.0 collective-permute-done.15.bot_ref
  44.7 1.8 %edge.5 = (f32[16,128,128]{2,1,0:T(8,128)S(1)}, bf16[16,128,128]{2,1,0:T(8,128)(2,1)S(1)}, bf16[2,128,128]{2,1,0:T(8,128)(2,1)S(1)}, bf16[2,128,128]{2,1,0:T(8,128)(2,1)S(1)}) custom-call(s32[6]{0:T(128)S(1)} %stack.43.meta_ref, bf16[16,128,512]{2,1,0:T(8,128)(2,1)S(1)} %get-tuple-element.73.cw_ref, bf16[16,32,256]{2,1,0:T(8,128)(2,1)S(1)} %get-tuple-element.74.edge_ref, ...), custom_call_target="tpu_custom_call" | custom-call | flops 2000000000 | bytes 1048576 | tf_op jit(solution)/shard_map/edge/pallas_call | solution.py:468
  46.5 0.0 collective-permute-start.16
  46.6 3.5 %collective-permute-start.17 = (bf16[2,128,128]{2,1,0:T(8,128)(2,1)S(1)}, bf16[2,128,128]{2,1,0:T(8,128)(2,1)S(1)}, u32[]{:S(2)}, u32[]{:S(2)}) collective-permute-start(bf16[2,128,128]{2,1,0:T(8,128)(2,1)S(1)} %get-tuple-element.84), channel_id=1, source_target_pairs={{0,7},{1,0},{2,1},{3,2},{4,3},{5,4},{6,5},{7,6},{8,15},{9,8},{10,9... | collective-permute-start | bytes 196616 | tf_op jit(solution)/shard_map/ppermute | solution.py:47
  50.1 1.9 %collective-permute-done.16.left_ref = bf16[2,128,128]{2,1,0:T(8,128)(2,1)S(1)} collective-permute-done((bf16[2,128,128]{2,1,0:T(8,128)(2,1)S(1)}, bf16[2,128,128]{2,1,0:T(8,128)(2,1)S(1)}, u32[]{:S(2)}, u32[]{:S(2)}) %collective-permute-start.16) | collective-permute-done | bytes 65568 | tf_op jit(solution)/shard_map/ppermute | solution.py:47
  52.0 0.0 collective-permute-done.17.right_ref
  52.1 1.1 %collective-permute-start.18 = (bf16[20,16,128]{2,1,0:T(8,128)(2,1)S(1)}, bf16[20,16,128]{2,1,0:T(8,128)(2,1)S(1)}, u32[]{:S(2)}, u32[]{:S(2)}) collective-permute-start(bf16[20,16,128]{2,1,0:T(8,128)(2,1)S(1)} %pad_maximum_fusion.4), channel_id=1, source_target_pairs={{0,8},{8,16},{16,24},{24,0},{1,9},{9,17},{17,25},{25,1},{2,10},{10... | collective-permute-start | bytes 245768 | tf_op jit(solution)/shard_map/ppermute | solution.py:47
  53.2 1.9 %collective-permute-start.19 = (bf16[20,16,128]{2,1,0:T(8,128)(2,1)S(1)}, bf16[20,16,128]{2,1,0:T(8,128)(2,1)S(1)}, u32[]{:S(2)}, u32[]{:S(2)}) collective-permute-start(bf16[20,16,128]{2,1,0:T(8,128)(2,1)S(1)} %pad_maximum_fusion.5), channel_id=1, source_target_pairs={{0,24},{8,0},{16,8},{24,16},{1,25},{9,1},{17,9},{25,17},{2,26},{10... | collective-permute-start | bytes 245768 | tf_op jit(solution)/shard_map/ppermute | solution.py:47
  55.1 3.0 %main.6 = (f32[16,32,128]{2,1,0:T(8,128)S(1)}, bf16[16,128,128]{2,1,0:T(8,128)(2,1)S(1)}, bf16[2,128,128]{2,1,0:T(8,128)(2,1)S(1)}, bf16[2,128,128]{2,1,0:T(8,128)(2,1)S(1)}) custom-call(s32[6]{0:T(128)S(1)} %stack.43.meta_ref, bf16[16,256,1024]{2,1,0:T(8,128)(2,1)S(1)} %bands.2.ct_ref, bf16[16,128,1024]{2,1,0:T(8,128)(2,1)S(1)} %get-tuple-element.76.rt_ref, ...), custom_call_target="tpu_custom_call" | custom-call | flops 4000000000 | bytes 1048576 | tf_op jit(solution)/shard_map/main/pallas_call | solution.py:457
  58.2 0.0 collective-permute-done.18.top_ref
  58.2 0.0 collective-permute-done.19.bot_ref
  58.2 1.7 %edge.6 = (bf16[16,128,128]{2,1,0:T(8,128)(2,1)S(1)}, bf16[2,128,128]{2,1,0:T(8,128)(2,1)S(1)}, bf16[2,128,128]{2,1,0:T(8,128)(2,1)S(1)}) custom-call(s32[6]{0:T(128)S(1)} %stack.43.meta_ref, bf16[16,128,512]{2,1,0:T(8,128)(2,1)S(1)} %get-tuple-element.58.cw_ref, bf16[16,32,256]{2,1,0:T(8,128)(2,1)S(1)} %get-tuple-element.59.edge_ref, ...), custom_call_target="tpu_custom_call" | custom-call | flops 2000000000 | bytes 1048576 | tf_op jit(solution)/shard_map/edge/pallas_call | solution.py:468
  59.8 0.1 collective-permute-start.20
  59.9 3.5 %collective-permute-start.21 = (bf16[2,128,128]{2,1,0:T(8,128)(2,1)S(1)}, bf16[2,128,128]{2,1,0:T(8,128)(2,1)S(1)}, u32[]{:S(2)}, u32[]{:S(2)}) collective-permute-start(bf16[2,128,128]{2,1,0:T(8,128)(2,1)S(1)} %get-tuple-element.91), channel_id=1, source_target_pairs={{0,7},{1,0},{2,1},{3,2},{4,3},{5,4},{6,5},{7,6},{8,15},{9,8},{10,9... | collective-permute-start | bytes 196616 | tf_op jit(solution)/shard_map/ppermute | solution.py:47
  63.4 2.5 %collective-permute-done.20.left_ref = bf16[2,128,128]{2,1,0:T(8,128)(2,1)S(1)} collective-permute-done((bf16[2,128,128]{2,1,0:T(8,128)(2,1)S(1)}, bf16[2,128,128]{2,1,0:T(8,128)(2,1)S(1)}, u32[]{:S(2)}, u32[]{:S(2)}) %collective-permute-start.20) | collective-permute-done | bytes 65568 | tf_op jit(solution)/shard_map/ppermute | solution.py:47
  65.9 0.0 collective-permute-done.21.right_ref
  66.0 1.3 %collective-permute-start.22 = (bf16[20,16,128]{2,1,0:T(8,128)(2,1)S(1)}, bf16[20,16,128]{2,1,0:T(8,128)(2,1)S(1)}, u32[]{:S(2)}, u32[]{:S(2)}) collective-permute-start(bf16[20,16,128]{2,1,0:T(8,128)(2,1)S(1)} %pad_maximum_fusion.6), channel_id=1, source_target_pairs={{0,8},{8,16},{16,24},{24,0},{1,9},{9,17},{17,25},{25,1},{2,10},{10... | collective-permute-start | bytes 245768 | tf_op jit(solution)/shard_map/ppermute | solution.py:47
  67.3 1.7 %collective-permute-start.23 = (bf16[20,16,128]{2,1,0:T(8,128)(2,1)S(1)}, bf16[20,16,128]{2,1,0:T(8,128)(2,1)S(1)}, u32[]{:S(2)}, u32[]{:S(2)}) collective-permute-start(bf16[20,16,128]{2,1,0:T(8,128)(2,1)S(1)} %pad_maximum_fusion.7), channel_id=1, source_target_pairs={{0,24},{8,0},{16,8},{24,16},{1,25},{9,1},{17,9},{25,17},{2,26},{10... | collective-permute-start | bytes 245768 | tf_op jit(solution)/shard_map/ppermute | solution.py:47
  69.0 3.0 %main.7 = (f32[16,32,128]{2,1,0:T(8,128)S(1)}, f32[16,128,128]{2,1,0:T(8,128)S(1)}) custom-call(s32[6]{0:T(128)S(1)} %stack.43.meta_ref, bf16[16,256,1024]{2,1,0:T(8,128)(2,1)S(1)} %get-tuple-element.69.ct_ref, bf16[16,128,1024]{2,1,0:T(8,128)(2,1)S(1)} %get-tuple-element.75.rt_ref, bf16[16,128,128]{2,1,0:T(8,128)(2,1)S(1)} %get-tuple-element.89.field_ref, ...), custom_call_target="tpu_custom_call" | custom-call | flops 4000000000 | bytes 1048576 | tf_op jit(solution)/shard_map/main/pallas_call | solution.py:457
  72.0 0.0 collective-permute-done.23.bot_ref
  72.0 2.5 %edge.7 = f32[16,128,128]{2,1,0:T(8,128)} custom-call(s32[6]{0:T(128)S(1)} %stack.43.meta_ref, bf16[16,128,512]{2,1,0:T(8,128)(2,1)S(1)} %get-tuple-element.73.cw_ref, bf16[16,32,256]{2,1,0:T(8,128)(2,1)S(1)} %get-tuple-element.74.edge_ref, f32[16,32,128]{2,1,0:T(8,128)S(1)} %get-tuple-element.93.rim_ref, ...), custom_call_target="tpu_custom_call" | custom-call | flops 2000000000 | bytes 1048576 | tf_op jit(solution)/shard_map/edge/pallas_call | solution.py:468
  (35 shorter events, 0.2 us)
Async XLA Ops:
  0.0 0.9 %copy-start.2 = (f32[4,16,2,4,33]{4,3,2,1,0:T(4,128)S(1)}, f32[4,16,2,4,33]{4,3,2,1,0:T(4,128)}, u32[]{:S(2)}) copy-start(f32[4,16,2,4,33]{4,3,2,1,0:T(4,128)} %param.9) | copy-start | bytes 202756
  1.0 0.7 copy-start.3
  1.6 0.7 copy-start.4
  2.4 11.5 %collective-permute-start.5 = (bf16[48,512]{1,0:T(8,128)(2,1)S(1)}, bf16[48,512]{1,0:T(8,128)(2,1)S(1)}, u32[]{:S(2)}, u32[]{:S(2)}) collective-permute-start(bf16[48,512]{1,0:T(8,128)(2,1)S(1)} %get-tuple-element.54.refs_0_), channel_id=1, source_target_pairs={{0,6},{1,7},{2,0},{3,1},{4,2},{5,3},{6,4},{7,5},{8,14},{9,15},{10,... | collective-permute-start | bytes 147464 | tf_op jit(solution)/shard_map/ppermute | solution.py:47
  7.5 6.4 %collective-permute-start.4 = (bf16[48,512]{1,0:T(8,128)(2,1)S(1)}, bf16[48,512]{1,0:T(8,128)(2,1)S(1)}, u32[]{:S(2)}, u32[]{:S(2)}) collective-permute-start(bf16[48,512]{1,0:T(8,128)(2,1)S(1)} %get-tuple-element.54.refs_0_), channel_id=1, source_target_pairs={{0,4},{1,5},{2,6},{3,7},{4,0},{5,1},{6,2},{7,3},{8,12},{9,13},{10,... | collective-permute-start | bytes 147464 | tf_op jit(solution)/shard_map/ppermute | solution.py:47
  7.5 6.4 %collective-permute-start.3 = (bf16[48,512]{1,0:T(8,128)(2,1)S(1)}, bf16[48,512]{1,0:T(8,128)(2,1)S(1)}, u32[]{:S(2)}, u32[]{:S(2)}) collective-permute-start(bf16[48,512]{1,0:T(8,128)(2,1)S(1)} %get-tuple-element.54.refs_0_), channel_id=1, source_target_pairs={{0,2},{1,3},{2,4},{3,5},{4,6},{5,7},{6,0},{7,1},{8,10},{9,11},{10,... | collective-permute-start | bytes 147464 | tf_op jit(solution)/shard_map/ppermute | solution.py:47
  8.5 2.3 %collective-permute-start.2 = (f32[4,128]{1,0:T(4,128)S(1)}, f32[4,128]{1,0:T(4,128)S(1)}, u32[]{:S(2)}, u32[]{:S(2)}) collective-permute-start(f32[4,128]{1,0:T(4,128)S(1)} %get-tuple-element.53.mine_ref.keys_ref), channel_id=1, source_target_pairs={{0,1},{2,3},{4,5},{6,7},{1,0},{3,2},{5,4},{7,6},{8,9},{10,11},{12,... | collective-permute-start | bytes 6152 | tf_op jit(solution)/shard_map/ppermute | solution.py:51
  8.5 1.2 %copy-start = (f32[16,128,128]{2,1,0:T(8,128)S(1)}, f32[16,128,128]{2,1,0:T(8,128)}, u32[]{:S(2)}) copy-start(f32[16,128,128]{2,1,0:T(8,128)} %a_ref.9) | copy-start | bytes 3145732
  10.2 5.5 %collective-permute-start = (bf16[2,128,128]{2,1,0:T(8,128)(2,1)S(1)}, bf16[2,128,128]{2,1,0:T(8,128)(2,1)S(1)}, u32[]{:S(2)}, u32[]{:S(2)}) collective-permute-start(bf16[2,128,128]{2,1,0:T(8,128)(2,1)S(1)} %get-tuple-element.51), channel_id=1, source_target_pairs={{0,1},{1,2},{2,3},{3,4},{4,5},{5,6},{6,7},{7,0},{8,9},{9,10},{10,1... | collective-permute-start | bytes 196616 | tf_op jit(solution)/shard_map/ppermute | solution.py:47
  10.9 5.0 %collective-permute-start.1 = (bf16[2,128,128]{2,1,0:T(8,128)(2,1)S(1)}, bf16[2,128,128]{2,1,0:T(8,128)(2,1)S(1)}, u32[]{:S(2)}, u32[]{:S(2)}) collective-permute-start(bf16[2,128,128]{2,1,0:T(8,128)(2,1)S(1)} %get-tuple-element.52), channel_id=1, source_target_pairs={{0,7},{1,0},{2,1},{3,2},{4,3},{5,4},{6,5},{7,6},{8,15},{9,8},{10,9... | collective-permute-start | bytes 196616 | tf_op jit(solution)/shard_map/ppermute | solution.py:47
  14.6 1.3 %collective-permute-start.6 = (bf16[2,48,128]{2,1,0:T(8,128)(2,1)S(1)}, bf16[2,48,128]{2,1,0:T(8,128)(2,1)S(1)}, u32[]{:S(2)}, u32[]{:S(2)}) collective-permute-start(bf16[2,48,128]{2,1,0:T(8,128)(2,1)S(1)} %get-tuple-element.56), channel_id=1, source_target_pairs={{0,1},{2,3},{4,5},{6,7},{1,0},{3,2},{5,4},{7,6},{8,9},{10,11},{12,... | collective-permute-start | bytes 73736 | tf_op jit(solution)/shard_map/ppermute | solution.py:51
  16.4 9.1 %copy-start.5 = (f32[16,128,128]{2,1,0:T(8,128)S(1)}, f32[16,128,128]{2,1,0:T(8,128)}, u32[]{:S(2)}) copy-start(f32[16,128,128]{2,1,0:T(8,128)} %a_ref.11) | copy-start | bytes 3145732
  16.4 18.2 %collective-permute-start.11 = (f32[16,1,16]{2,1,0:T(1,128)}, f32[16,1,16]{2,1,0:T(1,128)S(1)}, u32[]{:S(2)}, u32[]{:S(2)}) collective-permute-start(f32[16,1,16]{2,1,0:T(1,128)} %bitcast.17), channel_id=1, source_target_pairs={{0,24},{8,0},{16,8},{24,16},{1,25},{9,1},{17,9},{25,17},{2,26},{10... | collective-permute-start | bytes 3080 | tf_op jit(solution)/shard_map/ppermute | solution.py:47
  18.9 15.7 %collective-permute-start.10 = (f32[16,1,16]{2,1,0:T(1,128)}, f32[16,1,16]{2,1,0:T(1,128)S(1)}, u32[]{:S(2)}, u32[]{:S(2)}) collective-permute-start(f32[16,1,16]{2,1,0:T(1,128)} %bitcast.18), channel_id=1, source_target_pairs={{0,16},{8,24},{16,0},{24,8},{1,17},{9,25},{17,1},{25,9},{2,18},{10... | collective-permute-start | bytes 3080 | tf_op jit(solution)/shard_map/ppermute | solution.py:47
  19.4 15.2 %collective-permute-start.9 = (f32[16,1,16]{2,1,0:T(1,128)}, f32[16,1,16]{2,1,0:T(1,128)S(1)}, u32[]{:S(2)}, u32[]{:S(2)}) collective-permute-start(f32[16,1,16]{2,1,0:T(1,128)} %bitcast.19), channel_id=1, source_target_pairs={{0,8},{8,16},{16,24},{24,0},{1,9},{9,17},{17,25},{25,1},{2,10},{10... | collective-permute-start | bytes 3080 | tf_op jit(solution)/shard_map/ppermute | solution.py:47
  20.0 9.4 %collective-permute-start.7 = (bf16[20,16,128]{2,1,0:T(8,128)(2,1)S(1)}, bf16[20,16,128]{2,1,0:T(8,128)(2,1)S(1)}, u32[]{:S(2)}, u32[]{:S(2)}) collective-permute-start(bf16[20,16,128]{2,1,0:T(8,128)(2,1)S(1)} %get-tuple-element.61), channel_id=1, source_target_pairs={{0,8},{8,16},{16,24},{24,0},{1,9},{9,17},{17,25},{25,1},{2,10},{10... | collective-permute-start | bytes 245768 | tf_op jit(solution)/shard_map/ppermute | solution.py:47
  22.4 7.0 %collective-permute-start.8 = (bf16[20,16,128]{2,1,0:T(8,128)(2,1)S(1)}, bf16[20,16,128]{2,1,0:T(8,128)(2,1)S(1)}, u32[]{:S(2)}, u32[]{:S(2)}) collective-permute-start(bf16[20,16,128]{2,1,0:T(8,128)(2,1)S(1)} %get-tuple-element.62), channel_id=1, source_target_pairs={{0,24},{8,0},{16,8},{24,16},{1,25},{9,1},{17,9},{25,17},{2,26},{10... | collective-permute-start | bytes 245768 | tf_op jit(solution)/shard_map/ppermute | solution.py:47
  29.4 5.3 %copy-start.6 = (f32[16,16,1]{1,2,0:T(1,128)S(1)}, f32[16,16,1]{1,2,0:T(1,128)}, u32[]{:S(2)}) copy-start(f32[16,16,1]{1,2,0:T(1,128)} %param.12) | copy-start | bytes 3076
  29.4 5.3 %copy-start.7 = (f32[4,64,128]{2,1,0:T(8,128)S(1)}, f32[4,64,128]{2,1,0:T(8,128)}, u32[]{:S(2)}) copy-start(f32[4,64,128]{2,1,0:T(8,128)} %constant.18.clone.refs_0_) | copy-start | bytes 393220
  31.1 6.6 %collective-permute-start.12 = (bf16[2,128,128]{2,1,0:T(8,128)(2,1)S(1)}, bf16[2,128,128]{2,1,0:T(8,128)(2,1)S(1)}, u32[]{:S(2)}, u32[]{:S(2)}) collective-permute-start(bf16[2,128,128]{2,1,0:T(8,128)(2,1)S(1)} %get-tuple-element.66), channel_id=1, source_target_pairs={{0,1},{1,2},{2,3},{3,4},{4,5},{5,6},{6,7},{7,0},{8,9},{9,10},{10,1... | collective-permute-start | bytes 196616 | tf_op jit(solution)/shard_map/ppermute | solution.py:47
  31.1 9.8 %copy-start.1 = (f32[16,128,128]{2,1,0:T(8,128)S(1)}, f32[16,128,128]{2,1,0:T(8,128)}, u32[]{:S(2)}) copy-start(f32[16,128,128]{2,1,0:T(8,128)} %a_ref.9) | copy-start | bytes 3145732
  31.1 6.5 %collective-permute-start.13 = (bf16[2,128,128]{2,1,0:T(8,128)(2,1)S(1)}, bf16[2,128,128]{2,1,0:T(8,128)(2,1)S(1)}, u32[]{:S(2)}, u32[]{:S(2)}) collective-permute-start(bf16[2,128,128]{2,1,0:T(8,128)(2,1)S(1)} %get-tuple-element.71), channel_id=1, source_target_pairs={{0,7},{1,0},{2,1},{3,2},{4,3},{5,4},{6,5},{7,6},{8,15},{9,8},{10,9... | collective-permute-start | bytes 196616 | tf_op jit(solution)/shard_map/ppermute | solution.py:47
  37.7 7.0 %collective-permute-start.14 = (bf16[20,16,128]{2,1,0:T(8,128)(2,1)S(1)}, bf16[20,16,128]{2,1,0:T(8,128)(2,1)S(1)}, u32[]{:S(2)}, u32[]{:S(2)}) collective-permute-start(bf16[20,16,128]{2,1,0:T(8,128)(2,1)S(1)} %pad_maximum_fusion.2), channel_id=1, source_target_pairs={{0,8},{8,16},{16,24},{24,0},{1,9},{9,17},{17,25},{25,1},{2,10},{10... | collective-permute-start | bytes 245768 | tf_op jit(solution)/shard_map/ppermute | solution.py:47
  39.2 5.4 %collective-permute-start.15 = (bf16[20,16,128]{2,1,0:T(8,128)(2,1)S(1)}, bf16[20,16,128]{2,1,0:T(8,128)(2,1)S(1)}, u32[]{:S(2)}, u32[]{:S(2)}) collective-permute-start(bf16[20,16,128]{2,1,0:T(8,128)(2,1)S(1)} %pad_maximum_fusion.3), channel_id=1, source_target_pairs={{0,24},{8,0},{16,8},{24,16},{1,25},{9,1},{17,9},{25,17},{2,26},{10... | collective-permute-start | bytes 245768 | tf_op jit(solution)/shard_map/ppermute | solution.py:47
  46.5 5.5 %collective-permute-start.16 = (bf16[2,128,128]{2,1,0:T(8,128)(2,1)S(1)}, bf16[2,128,128]{2,1,0:T(8,128)(2,1)S(1)}, u32[]{:S(2)}, u32[]{:S(2)}) collective-permute-start(bf16[2,128,128]{2,1,0:T(8,128)(2,1)S(1)} %get-tuple-element.83), channel_id=1, source_target_pairs={{0,1},{1,2},{2,3},{3,4},{4,5},{5,6},{6,7},{7,0},{8,9},{9,10},{10,1... | collective-permute-start | bytes 196616 | tf_op jit(solution)/shard_map/ppermute | solution.py:47
  46.6 5.5 %collective-permute-start.17 = (bf16[2,128,128]{2,1,0:T(8,128)(2,1)S(1)}, bf16[2,128,128]{2,1,0:T(8,128)(2,1)S(1)}, u32[]{:S(2)}, u32[]{:S(2)}) collective-permute-start(bf16[2,128,128]{2,1,0:T(8,128)(2,1)S(1)} %get-tuple-element.84), channel_id=1, source_target_pairs={{0,7},{1,0},{2,1},{3,2},{4,3},{5,4},{6,5},{7,6},{8,15},{9,8},{10,9... | collective-permute-start | bytes 196616 | tf_op jit(solution)/shard_map/ppermute | solution.py:47
  52.1 6.1 %collective-permute-start.18 = (bf16[20,16,128]{2,1,0:T(8,128)(2,1)S(1)}, bf16[20,16,128]{2,1,0:T(8,128)(2,1)S(1)}, u32[]{:S(2)}, u32[]{:S(2)}) collective-permute-start(bf16[20,16,128]{2,1,0:T(8,128)(2,1)S(1)} %pad_maximum_fusion.4), channel_id=1, source_target_pairs={{0,8},{8,16},{16,24},{24,0},{1,9},{9,17},{17,25},{25,1},{2,10},{10... | collective-permute-start | bytes 245768 | tf_op jit(solution)/shard_map/ppermute | solution.py:47
  53.2 5.0 %collective-permute-start.19 = (bf16[20,16,128]{2,1,0:T(8,128)(2,1)S(1)}, bf16[20,16,128]{2,1,0:T(8,128)(2,1)S(1)}, u32[]{:S(2)}, u32[]{:S(2)}) collective-permute-start(bf16[20,16,128]{2,1,0:T(8,128)(2,1)S(1)} %pad_maximum_fusion.5), channel_id=1, source_target_pairs={{0,24},{8,0},{16,8},{24,16},{1,25},{9,1},{17,9},{25,17},{2,26},{10... | collective-permute-start | bytes 245768 | tf_op jit(solution)/shard_map/ppermute | solution.py:47
  59.8 6.1 %collective-permute-start.20 = (bf16[2,128,128]{2,1,0:T(8,128)(2,1)S(1)}, bf16[2,128,128]{2,1,0:T(8,128)(2,1)S(1)}, u32[]{:S(2)}, u32[]{:S(2)}) collective-permute-start(bf16[2,128,128]{2,1,0:T(8,128)(2,1)S(1)} %get-tuple-element.90), channel_id=1, source_target_pairs={{0,1},{1,2},{2,3},{3,4},{4,5},{5,6},{6,7},{7,0},{8,9},{9,10},{10,1... | collective-permute-start | bytes 196616 | tf_op jit(solution)/shard_map/ppermute | solution.py:47
  59.9 6.0 %collective-permute-start.21 = (bf16[2,128,128]{2,1,0:T(8,128)(2,1)S(1)}, bf16[2,128,128]{2,1,0:T(8,128)(2,1)S(1)}, u32[]{:S(2)}, u32[]{:S(2)}) collective-permute-start(bf16[2,128,128]{2,1,0:T(8,128)(2,1)S(1)} %get-tuple-element.91), channel_id=1, source_target_pairs={{0,7},{1,0},{2,1},{3,2},{4,3},{5,4},{6,5},{7,6},{8,15},{9,8},{10,9... | collective-permute-start | bytes 196616 | tf_op jit(solution)/shard_map/ppermute | solution.py:47
  66.0 6.0 %collective-permute-start.22 = (bf16[20,16,128]{2,1,0:T(8,128)(2,1)S(1)}, bf16[20,16,128]{2,1,0:T(8,128)(2,1)S(1)}, u32[]{:S(2)}, u32[]{:S(2)}) collective-permute-start(bf16[20,16,128]{2,1,0:T(8,128)(2,1)S(1)} %pad_maximum_fusion.6), channel_id=1, source_target_pairs={{0,8},{8,16},{16,24},{24,0},{1,9},{9,17},{17,25},{25,1},{2,10},{10... | collective-permute-start | bytes 245768 | tf_op jit(solution)/shard_map/ppermute | solution.py:47
  67.3 4.7 %collective-permute-start.23 = (bf16[20,16,128]{2,1,0:T(8,128)(2,1)S(1)}, bf16[20,16,128]{2,1,0:T(8,128)(2,1)S(1)}, u32[]{:S(2)}, u32[]{:S(2)}) collective-permute-start(bf16[20,16,128]{2,1,0:T(8,128)(2,1)S(1)} %pad_maximum_fusion.7), channel_id=1, source_target_pairs={{0,24},{8,0},{16,8},{24,16},{1,25},{9,1},{17,9},{25,17},{2,26},{10... | collective-permute-start | bytes 245768 | tf_op jit(solution)/shard_map/ppermute | solution.py:47

commit v3 on v2

--- a/solution.py
+++ b/solution.py
@@ -51,28 +51,16 @@
     return lax.ppermute(cells, axis, pairs + [(j, i) for i, j in pairs])
 
 
-def gathered(piece, axis):
-    count = lax.axis_size(axis)
-    if count <= 8:
-        return [piece] + [shift(piece, axis, s) for s in range(1, count)]
-    every = lax.all_gather(piece, axis, axis=0)
-    me = lax.axis_index(axis)
-    return [lax.dynamic_index_in_dim(every, (me - s) % count, 0, False) for s in range(count)]
-
-
 def swap_pairs(cells, axis):
     return swap(cells, axis, [(i, i + 1) for i in range(0, lax.axis_size(axis), 2)])
 
 
-def bank_kernel(bank_ref, ids_ref, mix_ref, out_ref, keys_ref):
+def bank_kernel(bank_ref, out_ref):
     rows, taps = bank_ref.shape
     for block in range(rows // TILE):
         part = bank_ref[block * TILE : (block + 1) * TILE, :]
         part = jnp.concatenate([part, jnp.zeros((TILE, TILE - taps), F32)], axis=1)
         out_ref[:, block * TILE : (block + 1) * TILE] = part.T[:TAP_ROWS].astype(BF16)
-    spread = (lanes((ids_ref.shape[1], TILE)) >> 3 == sublanes((ids_ref.shape[1], TILE))).astype(F32)
-    both = jnp.concatenate([ids_ref[...].astype(F32), mix_ref[...]], axis=0)
-    keys_ref[...] = jnp.dot(both, spread, precision=HIGHEST, preferred_element_type=F32)
 
 
 def pick_kernel(cols, meta_ref, mine_ref, other_ref, *refs):
@@ -138,13 +126,14 @@
         (ct_ref,) = refs
     else:
         inverse_ref, illum, (ct_ref, inv_ref) = refs[0], refs[1 : 1 + rows], refs[1 + rows :]
-        coarse = illum[0].shape[2]
-        smooth = jnp.zeros((TILE, illum[0].shape[0]), F32)
+        coarse = inverse_ref.shape[1] // rows
+        smooth = jnp.zeros((TILE, illum[0].shape[1]), F32)
         for s in range(rows):
             first = pl.multiple_of(lax.rem(meta_ref[4] + rows - s, rows) * coarse, coarse)
+            profile = sum(illum[s][n].astype(F32) for n in range(3))
             smooth = smooth + lax.dot_general(
                 inverse_ref[meta_ref[4], pl.ds(first, coarse), :],
-                illum[s][:, 0, :].T,
+                profile.T[:coarse],
                 (((0,), (0,)), ((), ())),
                 precision=HIGHEST,
                 preferred_element_type=F32,
@@ -152,39 +141,46 @@
         inv = 1.0 / smooth
         for g in range(inv_ref.shape[0]):
             inv_ref[g] = inv[:, g * PACK : (g + 1) * PACK]
-    low_all = lanes((TILE, TILE)) < TILE // 2
-    none = jnp.zeros((TILE, TILE), BF16)
+    start_shifts(shifts_ref)
+    ct_ref[:, TILE:, :] = jnp.zeros((ct_ref.shape[0], TILE, 8 * TILE), BF16)
+
+    def group(g8, carry):
+        for i in range(PACK):
+            column_bands(part, uv_ref, shifts_ref, g8 * PACK + i, i, ct_ref)
+        return carry
+
+    lax.fori_loop(0, ct_ref.shape[0] // PACK, group, 0)
+
+
+def start_shifts(shifts_ref):
     for t in range(PACK):
         to = (sublanes((TILE, TILE)) + t * HALO) & (TILE - 1)
         shifts_ref[:, t * TILE : (t + 1) * TILE] = (to == lanes((TILE, TILE))).astype(F32).astype(BF16)
-    ct_ref[:, TILE:, :] = jnp.zeros((ct_ref.shape[0], TILE, 8 * TILE), BF16)
-
-    def group(g8, carry):
-        for i in range(PACK):
-            z = g8 * PACK + i
-            left, right = TILE + i * HALO, TILE + (i + 4) % PACK * HALO
-            base = [turned(uv_ref, z, j // 4, 4 + j % 4, 1 - part, HALO, 0) for j in range(8)]
-            base = jnp.concatenate(base, axis=0).astype(BF16)
-            for t in range(0, PACK, 2):
-                got = jnp.dot(
-                    base, shifts_ref[:, t * TILE : (t + 2) * TILE], preferred_element_type=F32
-                ).astype(BF16)
-                first, second = got[:, :TILE], got[:, TILE:]
-                if t == 0:
-                    first, after = jnp.where(low_all, first, none), jnp.where(low_all, none, first)
-                elif t == PACK - 2:
-                    second, before = jnp.where(low_all, none, second), jnp.where(low_all, second, none)
-                for j in range(8):
-                    here, rows = slice(j * TILE, (j + 1) * TILE), slice(j * HALO, (j + 1) * HALO)
-                    ct_ref[z, t * HALO : (t + 1) * HALO, here] = first[rows]
-                    ct_ref[z, (t + 1) * HALO : (t + 2) * HALO, here] = second[rows]
-                    if t == 0:
-                        ct_ref[z, right : right + HALO, here] = after[rows]
-                    elif t == PACK - 2:
-                        ct_ref[z, left : left + HALO, here] = before[rows]
-        return carry
-
-    lax.fori_loop(0, ct_ref.shape[0] // PACK, group, 0)
+
+
+def column_bands(part, uv_ref, shifts_ref, z, i, ct_ref):
+    low_all = lanes((TILE, TILE)) < TILE // 2
+    none = jnp.zeros((TILE, TILE), BF16)
+    left, right = TILE + i * HALO, TILE + (i + 4) % PACK * HALO
+    base = [turned(uv_ref, z, j // 4, 4 + j % 4, 1 - part, HALO, 0) for j in range(8)]
+    base = jnp.concatenate(base, axis=0).astype(BF16)
+    for t in range(0, PACK, 2):
+        got = jnp.dot(
+            base, shifts_ref[:, t * TILE : (t + 2) * TILE], preferred_element_type=F32
+        ).astype(BF16)
+        first, second = got[:, :TILE], got[:, TILE:]
+        if t == 0:
+            first, after = jnp.where(low_all, first, none), jnp.where(low_all, none, first)
+        elif t == PACK - 2:
+            second, before = jnp.where(low_all, none, second), jnp.where(low_all, second, none)
+        for j in range(8):
+            here, rows = slice(j * TILE, (j + 1) * TILE), slice(j * HALO, (j + 1) * HALO)
+            ct_ref[z, t * HALO : (t + 1) * HALO, here] = first[rows]
+            ct_ref[z, (t + 1) * HALO : (t + 2) * HALO, here] = second[rows]
+            if t == 0:
+                ct_ref[z, right : right + HALO, here] = after[rows]
+            elif t == PACK - 2:
+                ct_ref[z, left : left + HALO, here] = before[rows]
 
 
 def other_bands(part, uv_ref, ct_ref, z, i, cw_ref, rt_ref, edge_ref):
@@ -283,6 +279,15 @@
     outs, q_ref = refs[:-1], refs[-1]
     if making:
         outs, made, uv_ref, rt_ref = outs[:-3], outs[-3:], rt_ref, outs[-2]
+    if making == 2:
+        shifts_ref, q_ref = refs[-1], refs[-2]
+        *outs, ct_ref, cw_ref, rt_ref, edge_ref = refs[:-2]
+        made = cw_ref, rt_ref, edge_ref
+        start_shifts(shifts_ref)
+        for z in range(ct_ref.shape[0]):
+            for t in range(PACK):
+                if t % 4 != z % 4:
+                    ct_ref[z, TILE + t * HALO : TILE + (t + 1) * HALO, :] = jnp.zeros((HALO, 8 * TILE), BF16)
     inner = slice(HALO, TILE - HALO)
 
     def group(g8, carry):
@@ -290,8 +295,6 @@
         halos = [joined(*sides, parity) for parity in range(2)]
 
         def columns(i):
-            if making:
-                other_bands(part, uv_ref, ct_ref, g8 * PACK + i, i, *made)
             wide = jnp.concatenate([field_ref[g8 * PACK + i], halos[i // 4]], axis=1)
             for n in range(4):
                 got = jnp.dot(
@@ -307,9 +310,20 @@
             rim_ref[z, HALO:] = blurred[TILE - HALO :]
             finish(part, blurred[inner], g8, i, inner, a_ref, inv_ref, outs)
 
+        def bands(i):
+            if making == 2:
+                column_bands(part, uv_ref, shifts_ref, g8 * PACK + i, i, ct_ref)
+            if making:
+                other_bands(part, uv_ref, ct_ref, g8 * PACK + i, i, *made)
+
+        bands(0)
+        bands(1)
         columns(0)
+        bands(2)
         columns(1)
         for i in range(PACK):
+            if i + 3 < PACK:
+                bands(i + 3)
             if i + 2 < PACK:
                 columns(i + 2)
             rows(i)
@@ -354,6 +368,21 @@
 
     for g8 in range(depth // PACK):
         group(g8, 0)
+
+
+def keys_kernel(ids_ref, mix_ref, illum_ref, keys_ref, plane_ref):
+    spread = (lanes((ids_ref.shape[1], TILE)) >> 3 == sublanes((ids_ref.shape[1], TILE))).astype(F32)
+    both = jnp.concatenate([ids_ref[...].astype(F32), mix_ref[...]], axis=0)
+    keys_ref[...] = jnp.dot(both, spread, precision=HIGHEST, preferred_element_type=F32)
+    rest = illum_ref[:, 0, :]
+    depth, coarse = rest.shape
+    parts = []
+    for _ in range(3):
+        part = rest.astype(BF16)
+        rest = rest - part.astype(F32)
+        parts.append(jnp.concatenate([part, jnp.zeros((depth, TILE - coarse), BF16)], axis=1))
+    for n in range(3):
+        plane_ref[n] = parts[n]
 
 
 def first_kernel(est_ref, b_ref, right_ref, left_ref):
@@ -390,25 +419,35 @@
     strip = jax.ShapeDtypeStruct((groups, TILE, TILE), BF16)
 
 
+    def ends_of(field, left, right, *more):
+        return [
+            jnp.concatenate([field[:, rows], left[:, rows], right[:, rows], *more], axis=0)
+            for rows in (slice(0, HALO), slice(TILE - HALO, TILE))
+        ]
+
     def exchanged(to_right, to_left):
         return shift(to_right, "col", 1), shift(to_left, "col", -1)
 
     blended = zone_ids.shape[-1]
     flat = (zones_here * depth * 2 * rank, taps)
-    bank, keys = call(
+    bank = call(
         bank_kernel,
-        (
-            jax.ShapeDtypeStruct((TAP_ROWS, zones_here * TILE), BF16),
-            jax.ShapeDtypeStruct((2 * blended, TILE), F32),
-        ),
+        jax.ShapeDtypeStruct((TAP_ROWS, zones_here * TILE), BF16),
+        [VMEM],
+        name="bank",
+        flops=4 * 10**9,
+    )(psf_bank.reshape(flat))
+    pieces = [bank] + [shift(bank, "col", s) for s in range(2, n_col, 2)]
+    field, to_right, to_left = call(
+        first_kernel, (narrow, strip, strip), [VMEM], name="first", flops=10**9
+    )(estimate)
+    keys, plane = call(
+        keys_kernel,
+        (jax.ShapeDtypeStruct((2 * blended, TILE), F32), jax.ShapeDtypeStruct((3, depth, TILE), BF16)),
         [VMEM] * 3,
-        name="bank",
-    )(psf_bank.reshape(flat), zone_ids[0, 0].T, mix_weights[0, 0].T)
-    pieces = [bank] + [shift(bank, "col", s) for s in range(2, n_col, 2)]
+        name="keys",
+    )(zone_ids[0, 0].T, mix_weights[0, 0].T, illumination.transpose(0, 2, 1))
     other_keys = swap_pairs(keys, "col")
-    field, to_right, to_left = call(
-        first_kernel, (narrow, strip, strip), [VMEM], name="first"
-    )(estimate)
     left, right = exchanged(to_right, to_left)
     inverse = smoothing(illumination.shape[1] * n_row, n_row)
     factors = jax.ShapeDtypeStruct((blended, TAP_ROWS, TILE), BF16)
@@ -418,6 +457,7 @@
         [SMEM] + [VMEM] * (2 + len(pieces)),
         name="pick",
     )(meta, keys, other_keys, *pieces)
+    ends = ends_of(field, left, right, plane)
     uv = call(
         functools.partial(taps_kernel, taps),
         jax.ShapeDtypeStruct((blended, depth, 2 * rank, 2 * TILE), F32),
@@ -427,12 +467,12 @@
 
     shape = lambda *s: jax.ShapeDtypeStruct((depth,) + s, BF16)
 
-    def bands(part, uv):
+    def bands(part, uv, *profiles):
         outs = (shape(2 * TILE, 8 * TILE),)
         args = [meta, uv]
         if part == 1:
             outs = outs + (jax.ShapeDtypeStruct((groups, TILE, PACK), F32),)
-            args = args + [inverse] + profiles
+            args = [*args, inverse, *profiles]
         return call(
             functools.partial(bands_kernel, part, n_row),
             outs,
@@ -442,28 +482,26 @@
             flops=4 * 10**9,
         )(*args)
 
-    def ends_of(field, left, right):
-        return [
-            jnp.concatenate([field[:, rows], left[:, rows], right[:, rows]], axis=0)
-            for rows in (slice(0, HALO), slice(TILE - HALO, TILE))
-        ]
-
     def blur(part, last, made, field, left, right, ends, other):
         ct, inv, *ready = made
         making = () if ready else (shape(TILE, 4 * TILE), shape(TILE, 8 * TILE), shape(2 * HALO, 2 * TILE))
+        making = making if ct is not None else (shape(2 * TILE, 8 * TILE), *making)
+        scratch = [pltpu.VMEM((4, 8 * TILE, TILE), BF16)]
         bot, top = shift(ends[0], "row", -1), shift(ends[1], "row", 1)
         rim = jax.ShapeDtypeStruct((depth, 2 * HALO, TILE), F32)
         outs = ((volume,) if part == 1 else ()) + (() if last else (narrow, strip, strip))
         main, *got = call(
-            functools.partial(main_kernel, part, bool(making)),
+            functools.partial(main_kernel, part, len(making) - 2 if making else 0),
             (rim,) + outs + making,
             [SMEM] + [VMEM] * 7,
-            [pltpu.VMEM((4, 8 * TILE, TILE), BF16)],
+            scratch if ct is not None else scratch + [pltpu.VMEM((TILE, 8 * TILE), BF16)],
             name="main",
             flops=4 * 10**9,
-        )(meta, ct, uv if making else ready[1], field, left, right, other, inv)
+        )(meta, uv if ct is None else ct, uv if making else ready[1], field, left, right, other, inv)
         if making:
             got, ready = got[:-3], got[-3:]
+        if ct is None:
+            *got, ct = got
         cw, rt, edge = ready
         done = call(
             functools.partial(edge_kernel, part),
@@ -473,23 +511,21 @@
             name="edge",
             flops=2 * 10**9,
         )(meta, cw, edge, main, top, bot, other, inv, *got)
-        return done, (ct, inv, cw, rt, edge)
+        return done, (ct, inv, cw, rt, edge), (top, bot)
 
     current = estimate
-    ends = ends_of(field, left, right)
-    first_end, last_end, profile, uv = lax.optimization_barrier((*ends, illumination.transpose(0, 2, 1), uv))
-    ends = [first_end, last_end]
-    profiles = gathered(profile, "row")
-    forward = (*bands(0, uv), jnp.zeros((groups, TILE, PACK), F32))
+    far = [shift(plane, "row", s) for s in range(2, n_row - 1)]
+    forward = (None, jnp.zeros((groups, TILE, PACK), F32))
     backward = None
     for step in range(ITERS):
         last = step == ITERS - 1
-        (ratio, *strips), forward = blur(0, False, forward, field, left, right, ends, observed)
+        (ratio, *strips), forward, ends = blur(0, False, forward, field, left, right, ends, observed)
         left, right = exchanged(*strips)
+        if backward is None:
+            above, below = (end[-3:] for end in ends)
+            backward = bands(1, lax.optimization_barrier((uv, strips[0]))[0], plane, above, *far, below)
         ends = ends_of(ratio, left, right)
-        if backward is None:
-            backward = bands(1, lax.optimization_barrier((uv, strips[0]))[0])
-        (current, *rest), backward = blur(1, last, backward, ratio, left, right, ends, current)
+        (current, *rest), backward, _ = blur(1, last, backward, ratio, left, right, ends, current)
         if not last:
             field, (left, right) = rest[0], exchanged(*rest[1:])
             ends = ends_of(field, left, right)

time: 74.7 us -> 68.3 us (0.914)
  starting transfers between devices: 36.3 us -> 33.1 us
  local copies, waits for them, and re-layouts: 3.71 us -> 1.13 us
    ppermute x22 -> x20, starting transfers between devices: 36.2 us -> 33.1 us  [shift(): lax.ppermute(cells, axis, [(i, (i + by) % count) for i in range(count)])]
    unnamed x16 -> x14, local copies, waits for them, and re-layouts: 3.55 us -> 0.97 us
    pallas_call x2 -> x1, Pallas kernels: 5.43 us -> 2.97 us  [bands(): call(functools.partial(bands_kernel, part, n_row), outs, [SMEM] + [VMEM]...]
    pallas_call x6 -> x7, Pallas kernels: 14.2 us -> 16 us  [the longest x4 15.3 us: blur(): call(functools.partial(main_kernel, part, len(making) - 2 if making else...]
    ppermute x22 -> x20, waiting for transfers between devices: 5.58 us -> 5.68 us  [shift(): lax.ppermute(cells, axis, [(i, (i + by) % count) for i in range(count)])]
  transfers between devices with their start and end apart: 24 -> 22, of which waited for: 4 -> 4; matrix products, arithmetic and copies ran while one was open for 0% -> 0% of each run, Pallas kernels for 29% -> 32%
where the time goes in v3:
time: 68.3 us; the launch traced here: 68.2 us
  starting transfers between devices  33.1 us (48%)
  Pallas kernels  27.8 us (41%)
  waiting for transfers between devices  5.72 us (8%)
  local copies, waits for them, and re-layouts  1.13 us (2%)
    ppermute x20, starting transfers between devices, shift(): lax.ppermute(cells, axis, [(i, (i + by) % count) for i in range(count)])  33.1 us
    pallas_call x4, Pallas kernels, blur(): call(functools.partial(main_kernel, part, len(making) - 2 if making else...  15.3 us
    pallas_call x4, Pallas kernels, blur(): call(functools.partial(edge_kernel, part), outs, [SMEM] + [VMEM] * (7 + l...  7.64 us
    ppermute x20, waiting for transfers between devices, shift(): lax.ppermute(cells, axis, [(i, (i + by) % count) for i in range(count)])  5.68 us
    pallas_call x1, Pallas kernels, bands(): call(functools.partial(bands_kernel, part, n_row), outs, [SMEM] + [VMEM]...  2.97 us
  transfers between devices with their start and end apart: 22, of which 4 were waited for; matrix products, arithmetic and copies ran while one was open for 0% of the time, Pallas kernels for 32%

profile of v3, /device:TPU:0, one launch (start us, length us, event | category | flops | bytes accessed | tf_op | source)
XLA Modules:
  0.0 68.2 jit_solution(6175803971143362472)
XLA Ops:
  0.0 0.9 %copy-done.5 = f32[4,16,2,4,33]{4,3,2,1,0:T(4,128)S(1)} copy-done((f32[4,16,2,4,33]{4,3,2,1,0:T(4,128)S(1)}, f32[4,16,2,4,33]{4,3,2,1,0:T(4,128)}, u32[]{:S(2)}) %copy-start.5) | copy-done | bytes 67608
  1.0 0.1 bank.1.refs_0_
  1.1 0.0 copy-start.4
  1.1 5.1 %collective-permute-start.3 = (bf16[48,512]{1,0:T(8,128)(2,1)S(1)}, bf16[48,512]{1,0:T(8,128)(2,1)S(1)}, u32[]{:S(2)}, u32[]{:S(2)}) collective-permute-start(bf16[48,512]{1,0:T(8,128)(2,1)S(1)} %bank.1.refs_0_), channel_id=1, source_target_pairs={{0,6},{1,7},{2,0},{3,1},{4,2},{5,3},{6,4},{7,5},{8,14},{9,15},{10,... | collective-permute-start | bytes 147464 | tf_op jit(solution)/shard_map/ppermute | solution.py:47
  6.2 0.0 collective-permute-start.2
  6.2 1.0 %collective-permute-start.1 = (bf16[48,512]{1,0:T(8,128)(2,1)S(1)}, bf16[48,512]{1,0:T(8,128)(2,1)S(1)}, u32[]{:S(2)}, u32[]{:S(2)}) collective-permute-start(bf16[48,512]{1,0:T(8,128)(2,1)S(1)} %bank.1.refs_0_), channel_id=1, source_target_pairs={{0,2},{1,3},{2,4},{3,5},{4,6},{5,7},{6,0},{7,1},{8,10},{9,11},{10,... | collective-permute-start | bytes 147464 | tf_op jit(solution)/shard_map/ppermute | solution.py:47
  7.2 0.0 copy-done
  7.2 0.0 copy-done.1
  7.2 0.2 keys.1
  7.3 0.0 collective-permute-start
  7.3 0.4 first.1
  7.8 0.6 collective-permute-start.5
  8.4 0.1 stack.43.meta_ref
  8.5 0.0 collective-permute-done.other_ref
  8.5 1.5 %collective-permute-start.9 = (bf16[3,16,128]{2,1,0:T(8,128)(2,1)S(1)}, bf16[3,16,128]{2,1,0:T(8,128)(2,1)S(1)}, u32[]{:S(2)}, u32[]{:S(2)}) collective-permute-start(bf16[3,16,128]{2,1,0:T(8,128)(2,1)S(1)} %get-tuple-element.56.refs_1_), channel_id=1, source_target_pairs={{0,16},{8,24},{16,0},{24,8},{1,17},{9,25},{17,1},{25,9},{2,18},{10... | collective-permute-start | bytes 36872 | tf_op jit(solution)/shard_map/ppermute | solution.py:47
  10.0 0.0 collective-permute-done.3.refs_3_
  10.0 2.8 %collective-permute-start.6 = (bf16[2,128,128]{2,1,0:T(8,128)(2,1)S(1)}, bf16[2,128,128]{2,1,0:T(8,128)(2,1)S(1)}, u32[]{:S(2)}, u32[]{:S(2)}) collective-permute-start(bf16[2,128,128]{2,1,0:T(8,128)(2,1)S(1)} %get-tuple-element.52), channel_id=1, source_target_pairs={{0,7},{1,0},{2,1},{3,2},{4,3},{5,4},{6,5},{7,6},{8,15},{9,8},{10,9... | collective-permute-start | bytes 196616 | tf_op jit(solution)/shard_map/ppermute | solution.py:47
  12.8 0.0 collective-permute-done.2.refs_2_
  12.8 0.0 collective-permute-done.1.refs_1_
  12.8 0.7 %pick.1 = (bf16[2,48,128]{2,1,0:T(8,128)(2,1)S(1)}, bf16[2,48,128]{2,1,0:T(8,128)(2,1)S(1)}) custom-call(s32[6]{0:T(128)S(1)} %stack.43.meta_ref, f32[4,128]{1,0:T(4,128)S(1)} %get-tuple-element.47.mine_ref.keys_ref, f32[4,128]{1,0:T(4,128)S(1)} %collective-permute-done.other_ref, bf16[48,512]{1,0:T(8,128)(2,1)S(1)} %bank.1.refs_0_, ...), custom_call_target="tpu_custom_call" | custom-call | bytes 1048576 | tf_op jit(solution)/shard_map/pick/pallas_call | solution.py:454
  13.5 0.1 collective-permute-start.4
  13.6 0.0 collective-permute-done.5.left_ref
  13.6 1.1 %collective-permute-done.6.right_ref = bf16[2,128,128]{2,1,0:T(8,128)(2,1)S(1)} collective-permute-done((bf16[2,128,128]{2,1,0:T(8,128)(2,1)S(1)}, bf16[2,128,128]{2,1,0:T(8,128)(2,1)S(1)}, u32[]{:S(2)}, u32[]{:S(2)}) %collective-permute-start.6) | collective-permute-done | bytes 65568 | tf_op jit(solution)/shard_map/ppermute | solution.py:47
  14.7 1.5 %collective-permute-start.8 = (bf16[23,16,128]{2,1,0:T(8,128)(2,1)S(1)}, bf16[23,16,128]{2,1,0:T(8,128)(2,1)S(1)}, u32[]{:S(2)}, u32[]{:S(2)}) collective-permute-start(bf16[23,16,128]{2,1,0:T(8,128)(2,1)S(1)} %get-tuple-element.113), channel_id=1, source_target_pairs={{0,24},{8,0},{16,8},{24,16},{1,25},{9,1},{17,9},{25,17},{2,26},{10... | collective-permute-start | bytes 282632 | tf_op jit(solution)/shard_map/ppermute | solution.py:47
  16.2 0.6 collective-permute-start.7
  16.8 0.0 collective-permute-done.4.other_ref
  16.8 0.5 taps.1.ct_ref.rt_ref.uv_ref
  17.4 5.5 %main.4 = (f32[16,32,128]{2,1,0:T(8,128)S(1)}, bf16[16,128,128]{2,1,0:T(8,128)(2,1)S(1)}, bf16[2,128,128]{2,1,0:T(8,128)(2,1)S(1)}, bf16[2,128,128]{2,1,0:T(8,12...) custom-call(s32[6]{0:T(128)S(1)} %stack.43.meta_ref, ...), custom_call_target="tpu_custom_call" | custom-call | flops 4000000000 | bytes 1048576 | tf_op jit(solution)/shard_map/main/pallas_call | solution.py:493
  22.8 0.0 collective-permute-done.8.bot_ref
  22.8 0.0 collective-permute-done.7.top_ref
  22.8 1.6 %edge.4 = (bf16[16,128,128]{2,1,0:T(8,128)(2,1)S(1)}, bf16[2,128,128]{2,1,0:T(8,128)(2,1)S(1)}, bf16[2,128,128]{2,1,0:T(8,128)(2,1)S(1)}) custom-call(s32[6]{0:T(128)S(1)} %stack.43.meta_ref, bf16[16,128,512]{2,1,0:T(8,128)(2,1)S(1)} %get-tuple-element.53.cw_ref, bf16[16,32,256]{2,1,0:T(8,128)(2,1)S(1)} %get-tuple-element.54.edge_ref, ...), custom_call_target="tpu_custom_call" | custom-call | flops 2000000000 | bytes 1048576 | tf_op jit(solution)/shard_map/edge/pallas_call | solution.py:506
  24.5 0.3 collective-permute-start.10
  24.8 3.3 %collective-permute-start.11 = (bf16[2,128,128]{2,1,0:T(8,128)(2,1)S(1)}, bf16[2,128,128]{2,1,0:T(8,128)(2,1)S(1)}, u32[]{:S(2)}, u32[]{:S(2)}) collective-permute-start(bf16[2,128,128]{2,1,0:T(8,128)(2,1)S(1)} %get-tuple-element.64), channel_id=1, source_target_pairs={{0,7},{1,0},{2,1},{3,2},{4,3},{5,4},{6,5},{7,6},{8,15},{9,8},{10,9... | collective-permute-start | bytes 196616 | tf_op jit(solution)/shard_map/ppermute | solution.py:47
  28.1 0.0 collective-permute-done.9.refs_3_
  28.1 0.0 copy-done.6
  28.1 3.0 %bands.1 = (bf16[16,256,1024]{2,1,0:T(8,128)(2,1)S(1)}, f32[2,128,8]{2,1,0:T(8,128)S(1)}) custom-call(s32[6]{0:T(128)S(1)} %stack.43.meta_ref, f32[2,16,8,256]{3,2,1,0:T(8,128)S(1)} %taps.1.ct_ref.rt_ref.uv_ref, f32[4,64,128]{2,1,0:T(8,128)S(1)} %copy-done.6, bf16[3,16,128]{2,1,0:T(8,128)(2,1)S(1)} %get-tuple-element.56.refs_1_, ...), custom_call_target="tpu_custom_call" | custom-call | flops 4000000000 | bytes 1048576 | tf_op jit(solution)/shard_map/bands/pallas_call | solution.py:476
  31.1 0.0 collective-permute-done.11.right_ref
  31.1 0.0 collective-permute-done.10.left_ref
  31.2 2.4 %collective-permute-start.12 = (bf16[20,16,128]{2,1,0:T(8,128)(2,1)S(1)}, bf16[20,16,128]{2,1,0:T(8,128)(2,1)S(1)}, u32[]{:S(2)}, u32[]{:S(2)}) collective-permute-start(bf16[20,16,128]{2,1,0:T(8,128)(2,1)S(1)} %pad_maximum_fusion.2), channel_id=1, source_target_pairs={{0,8},{8,16},{16,24},{24,0},{1,9},{9,17},{17,25},{25,1},{2,10},{10... | collective-permute-start | bytes 245768 | tf_op jit(solution)/shard_map/ppermute | solution.py:47
  33.6 0.8 %collective-permute-start.13 = (bf16[20,16,128]{2,1,0:T(8,128)(2,1)S(1)}, bf16[20,16,128]{2,1,0:T(8,128)(2,1)S(1)}, u32[]{:S(2)}, u32[]{:S(2)}) collective-permute-start(bf16[20,16,128]{2,1,0:T(8,128)(2,1)S(1)} %pad_maximum_fusion.3), channel_id=1, source_target_pairs={{0,24},{8,0},{16,8},{24,16},{1,25},{9,1},{17,9},{25,17},{2,26},{10... | collective-permute-start | bytes 245768 | tf_op jit(solution)/shard_map/ppermute | solution.py:47
  34.4 3.8 %main.5 = (f32[16,32,128]{2,1,0:T(8,128)S(1)}, f32[16,128,128]{2,1,0:T(8,128)S(1)}, bf16[16,128,128]{2,1,0:T(8,128)(2,1)S(1)}, bf16[2,128,128]{2,1,0:T(8,128)(2,...) custom-call(s32[6]{0:T(128)S(1)} %stack.43.meta_ref, ...), custom_call_target="tpu_custom_call" | custom-call | flops 4000000000 | bytes 1048576 | tf_op jit(solution)/shard_map/main/pallas_call | solution.py:493
  38.2 0.0 collective-permute-done.12.top_ref
  38.2 0.1 collective-permute-done.13.bot_ref
  38.3 1.8 %edge.5 = (f32[16,128,128]{2,1,0:T(8,128)S(1)}, bf16[16,128,128]{2,1,0:T(8,128)(2,1)S(1)}, bf16[2,128,128]{2,1,0:T(8,128)(2,1)S(1)}, bf16[2,128,128]{2,1,0:T(8,128)(2,1)S(1)}) custom-call(s32[6]{0:T(128)S(1)} %stack.43.meta_ref, bf16[16,128,512]{2,1,0:T(8,128)(2,1)S(1)} %get-tuple-element.66.cw_ref, bf16[16,32,256]{2,1,0:T(8,128)(2,1)S(1)} %get-tuple-element.67.edge_ref, ...), custom_call_target="tpu_custom_call" | custom-call | flops 2000000000 | bytes 1048576 | tf_op jit(solution)/shard_map/edge/pallas_call | solution.py:506
  40.1 0.0 collective-permute-start.14
  40.2 3.5 %collective-permute-start.15 = (bf16[2,128,128]{2,1,0:T(8,128)(2,1)S(1)}, bf16[2,128,128]{2,1,0:T(8,128)(2,1)S(1)}, u32[]{:S(2)}, u32[]{:S(2)}) collective-permute-start(bf16[2,128,128]{2,1,0:T(8,128)(2,1)S(1)} %get-tuple-element.78), channel_id=1, source_target_pairs={{0,7},{1,0},{2,1},{3,2},{4,3},{5,4},{6,5},{7,6},{8,15},{9,8},{10,9... | collective-permute-start | bytes 196616 | tf_op jit(solution)/shard_map/ppermute | solution.py:47
  43.7 1.9 %collective-permute-done.14.left_ref = bf16[2,128,128]{2,1,0:T(8,128)(2,1)S(1)} collective-permute-done((bf16[2,128,128]{2,1,0:T(8,128)(2,1)S(1)}, bf16[2,128,128]{2,1,0:T(8,128)(2,1)S(1)}, u32[]{:S(2)}, u32[]{:S(2)}) %collective-permute-start.14) | collective-permute-done | bytes 65568 | tf_op jit(solution)/shard_map/ppermute | solution.py:47
  45.7 0.0 collective-permute-done.15.right_ref
  45.7 1.5 %collective-permute-start.16 = (bf16[20,16,128]{2,1,0:T(8,128)(2,1)S(1)}, bf16[20,16,128]{2,1,0:T(8,128)(2,1)S(1)}, u32[]{:S(2)}, u32[]{:S(2)}) collective-permute-start(bf16[20,16,128]{2,1,0:T(8,128)(2,1)S(1)} %pad_maximum_fusion.4), channel_id=1, source_target_pairs={{0,8},{8,16},{16,24},{24,0},{1,9},{9,17},{17,25},{25,1},{2,10},{10... | collective-permute-start | bytes 245768 | tf_op jit(solution)/shard_map/ppermute | solution.py:47
  47.2 1.6 %collective-permute-start.17 = (bf16[20,16,128]{2,1,0:T(8,128)(2,1)S(1)}, bf16[20,16,128]{2,1,0:T(8,128)(2,1)S(1)}, u32[]{:S(2)}, u32[]{:S(2)}) collective-permute-start(bf16[20,16,128]{2,1,0:T(8,128)(2,1)S(1)} %pad_maximum_fusion.5), channel_id=1, source_target_pairs={{0,24},{8,0},{16,8},{24,16},{1,25},{9,1},{17,9},{25,17},{2,26},{10... | collective-permute-start | bytes 245768 | tf_op jit(solution)/shard_map/ppermute | solution.py:47
  48.7 3.1 %main.6 = (f32[16,32,128]{2,1,0:T(8,128)S(1)}, bf16[16,128,128]{2,1,0:T(8,128)(2,1)S(1)}, bf16[2,128,128]{2,1,0:T(8,128)(2,1)S(1)}, bf16[2,128,128]{2,1,0:T(8,128)(2,1)S(1)}) custom-call(s32[6]{0:T(128)S(1)} %stack.43.meta_ref, bf16[16,256,1024]{2,1,0:T(8,128)(2,1)S(1)} %get-tuple-element.69.ct_ref, bf16[16,128,1024]{2,1,0:T(8,128)(2,1)S(1)} %get-tuple-element.70.rt_ref, ...), custom_call_target="tpu_custom_call" | custom-call | flops 4000000000 | bytes 1048576 | tf_op jit(solution)/shard_map/main/pallas_call | solution.py:493
  51.8 0.0 collective-permute-done.16.top_ref
  51.8 0.0 collective-permute-done.17.bot_ref
  51.8 1.6 %edge.6 = (bf16[16,128,128]{2,1,0:T(8,128)(2,1)S(1)}, bf16[2,128,128]{2,1,0:T(8,128)(2,1)S(1)}, bf16[2,128,128]{2,1,0:T(8,128)(2,1)S(1)}) custom-call(s32[6]{0:T(128)S(1)} %stack.43.meta_ref, bf16[16,128,512]{2,1,0:T(8,128)(2,1)S(1)} %get-tuple-element.53.cw_ref, bf16[16,32,256]{2,1,0:T(8,128)(2,1)S(1)} %get-tuple-element.54.edge_ref, ...), custom_call_target="tpu_custom_call" | custom-call | flops 2000000000 | bytes 1048576 | tf_op jit(solution)/shard_map/edge/pallas_call | solution.py:506
  53.4 0.1 collective-permute-start.18
  53.5 3.5 %collective-permute-start.19 = (bf16[2,128,128]{2,1,0:T(8,128)(2,1)S(1)}, bf16[2,128,128]{2,1,0:T(8,128)(2,1)S(1)}, u32[]{:S(2)}, u32[]{:S(2)}) collective-permute-start(bf16[2,128,128]{2,1,0:T(8,128)(2,1)S(1)} %get-tuple-element.85), channel_id=1, source_target_pairs={{0,7},{1,0},{2,1},{3,2},{4,3},{5,4},{6,5},{7,6},{8,15},{9,8},{10,9... | collective-permute-start | bytes 196616 | tf_op jit(solution)/shard_map/ppermute | solution.py:47
  57.1 2.5 %collective-permute-done.18.left_ref = bf16[2,128,128]{2,1,0:T(8,128)(2,1)S(1)} collective-permute-done((bf16[2,128,128]{2,1,0:T(8,128)(2,1)S(1)}, bf16[2,128,128]{2,1,0:T(8,128)(2,1)S(1)}, u32[]{:S(2)}, u32[]{:S(2)}) %collective-permute-start.18) | collective-permute-done | bytes 65568 | tf_op jit(solution)/shard_map/ppermute | solution.py:47
  59.6 0.0 collective-permute-done.19.right_ref
  59.6 1.2 %collective-permute-start.20 = (bf16[20,16,128]{2,1,0:T(8,128)(2,1)S(1)}, bf16[20,16,128]{2,1,0:T(8,128)(2,1)S(1)}, u32[]{:S(2)}, u32[]{:S(2)}) collective-permute-start(bf16[20,16,128]{2,1,0:T(8,128)(2,1)S(1)} %pad_maximum_fusion.6), channel_id=1, source_target_pairs={{0,8},{8,16},{16,24},{24,0},{1,9},{9,17},{17,25},{25,1},{2,10},{10... | collective-permute-start | bytes 245768 | tf_op jit(solution)/shard_map/ppermute | solution.py:47
  60.8 1.9 %collective-permute-start.21 = (bf16[20,16,128]{2,1,0:T(8,128)(2,1)S(1)}, bf16[20,16,128]{2,1,0:T(8,128)(2,1)S(1)}, u32[]{:S(2)}, u32[]{:S(2)}) collective-permute-start(bf16[20,16,128]{2,1,0:T(8,128)(2,1)S(1)} %pad_maximum_fusion.7), channel_id=1, source_target_pairs={{0,24},{8,0},{16,8},{24,16},{1,25},{9,1},{17,9},{25,17},{2,26},{10... | collective-permute-start | bytes 245768 | tf_op jit(solution)/shard_map/ppermute | solution.py:47
  62.6 2.9 %main.7 = (f32[16,32,128]{2,1,0:T(8,128)S(1)}, f32[16,128,128]{2,1,0:T(8,128)S(1)}) custom-call(s32[6]{0:T(128)S(1)} %stack.43.meta_ref, bf16[16,256,1024]{2,1,0:T(8,128)(2,1)S(1)} %get-tuple-element.62.ct_ref, bf16[16,128,1024]{2,1,0:T(8,128)(2,1)S(1)} %get-tuple-element.68.rt_ref, bf16[16,128,128]{2,1,0:T(8,128)(2,1)S(1)} %get-tuple-element.83.field_ref, ...), custom_call_target="tpu_custom_call" | custom-call | flops 4000000000 | bytes 1048576 | tf_op jit(solution)/shard_map/main/pallas_call | solution.py:493
  65.6 0.0 collective-permute-done.20.top_ref
  65.6 0.0 collective-permute-done.21.bot_ref
  65.6 2.5 %edge.7 = f32[16,128,128]{2,1,0:T(8,128)} custom-call(s32[6]{0:T(128)S(1)} %stack.43.meta_ref, bf16[16,128,512]{2,1,0:T(8,128)(2,1)S(1)} %get-tuple-element.66.cw_ref, bf16[16,32,256]{2,1,0:T(8,128)(2,1)S(1)} %get-tuple-element.67.edge_ref, f32[16,32,128]{2,1,0:T(8,128)S(1)} %get-tuple-element.87.rim_ref, ...), custom_call_target="tpu_custom_call" | custom-call | flops 2000000000 | bytes 1048576 | tf_op jit(solution)/shard_map/edge/pallas_call | solution.py:506
  (31 shorter events, 0.2 us)
Async XLA Ops:
  0.0 0.9 %copy-start.5 = (f32[4,16,2,4,33]{4,3,2,1,0:T(4,128)S(1)}, f32[4,16,2,4,33]{4,3,2,1,0:T(4,128)}, u32[]{:S(2)}) copy-start(f32[4,16,2,4,33]{4,3,2,1,0:T(4,128)} %param.9) | copy-start | bytes 202756
  1.0 6.2 %copy-start = (f32[16,16,1]{1,2,0:T(1,128)S(1)}, f32[16,16,1]{1,2,0:T(1,128)}, u32[]{:S(2)}) copy-start(f32[16,16,1]{1,2,0:T(1,128)} %param.12) | copy-start | bytes 3076
  1.0 6.2 %copy-start.1 = (s32[1,1,16,2]{2,3,1,0:T(2,128)S(1)}, s32[1,1,16,2]{2,3,1,0:T(2,128)}, u32[]{:S(2)}) copy-start(s32[1,1,16,2]{2,3,1,0:T(2,128)} %param.10) | copy-start | bytes 388
  1.0 6.2 %copy-start.2 = (f32[1,1,16,2]{2,3,1,0:T(2,128)S(1)}, f32[1,1,16,2]{2,3,1,0:T(2,128)}, u32[]{:S(2)}) copy-start(f32[1,1,16,2]{2,3,1,0:T(2,128)} %param.11) | copy-start | bytes 388
  1.0 6.4 %copy-start.3 = (f32[16,128,128]{2,1,0:T(8,128)S(1)}, f32[16,128,128]{2,1,0:T(8,128)}, u32[]{:S(2)}) copy-start(f32[16,128,128]{2,1,0:T(8,128)} %a_ref.9) | copy-start | bytes 3145732
  1.1 16.3 %copy-start.4 = (f32[16,128,128]{2,1,0:T(8,128)S(1)}, f32[16,128,128]{2,1,0:T(8,128)}, u32[]{:S(2)}) copy-start(f32[16,128,128]{2,1,0:T(8,128)} %a_ref.11) | copy-start | bytes 3145732
  1.1 9.0 %collective-permute-start.3 = (bf16[48,512]{1,0:T(8,128)(2,1)S(1)}, bf16[48,512]{1,0:T(8,128)(2,1)S(1)}, u32[]{:S(2)}, u32[]{:S(2)}) collective-permute-start(bf16[48,512]{1,0:T(8,128)(2,1)S(1)} %bank.1.refs_0_), channel_id=1, source_target_pairs={{0,6},{1,7},{2,0},{3,1},{4,2},{5,3},{6,4},{7,5},{8,14},{9,15},{10,... | collective-permute-start | bytes 147464 | tf_op jit(solution)/shard_map/ppermute | solution.py:47
  6.2 6.6 %collective-permute-start.2 = (bf16[48,512]{1,0:T(8,128)(2,1)S(1)}, bf16[48,512]{1,0:T(8,128)(2,1)S(1)}, u32[]{:S(2)}, u32[]{:S(2)}) collective-permute-start(bf16[48,512]{1,0:T(8,128)(2,1)S(1)} %bank.1.refs_0_), channel_id=1, source_target_pairs={{0,4},{1,5},{2,6},{3,7},{4,0},{5,1},{6,2},{7,3},{8,12},{9,13},{10,... | collective-permute-start | bytes 147464 | tf_op jit(solution)/shard_map/ppermute | solution.py:47
  6.2 6.6 %collective-permute-start.1 = (bf16[48,512]{1,0:T(8,128)(2,1)S(1)}, bf16[48,512]{1,0:T(8,128)(2,1)S(1)}, u32[]{:S(2)}, u32[]{:S(2)}) collective-permute-start(bf16[48,512]{1,0:T(8,128)(2,1)S(1)} %bank.1.refs_0_), channel_id=1, source_target_pairs={{0,2},{1,3},{2,4},{3,5},{4,6},{5,7},{6,0},{7,1},{8,10},{9,11},{10,... | collective-permute-start | bytes 147464 | tf_op jit(solution)/shard_map/ppermute | solution.py:47
  7.3 1.2 %collective-permute-start = (f32[4,128]{1,0:T(4,128)S(1)}, f32[4,128]{1,0:T(4,128)S(1)}, u32[]{:S(2)}, u32[]{:S(2)}) collective-permute-start(f32[4,128]{1,0:T(4,128)S(1)} %get-tuple-element.47.mine_ref.keys_ref), channel_id=1, source_target_pairs={{0,1},{2,3},{4,5},{6,7},{1,0},{3,2},{5,4},{7,6},{8,9},{10,11},{12,... | collective-permute-start | bytes 6152 | tf_op jit(solution)/shard_map/ppermute | solution.py:51
  7.8 5.8 %collective-permute-start.5 = (bf16[2,128,128]{2,1,0:T(8,128)(2,1)S(1)}, bf16[2,128,128]{2,1,0:T(8,128)(2,1)S(1)}, u32[]{:S(2)}, u32[]{:S(2)}) collective-permute-start(bf16[2,128,128]{2,1,0:T(8,128)(2,1)S(1)} %get-tuple-element.51), channel_id=1, source_target_pairs={{0,1},{1,2},{2,3},{3,4},{4,5},{5,6},{6,7},{7,0},{8,9},{9,10},{10,1... | collective-permute-start | bytes 196616 | tf_op jit(solution)/shard_map/ppermute | solution.py:47
  8.5 19.6 %collective-permute-start.9 = (bf16[3,16,128]{2,1,0:T(8,128)(2,1)S(1)}, bf16[3,16,128]{2,1,0:T(8,128)(2,1)S(1)}, u32[]{:S(2)}, u32[]{:S(2)}) collective-permute-start(bf16[3,16,128]{2,1,0:T(8,128)(2,1)S(1)} %get-tuple-element.56.refs_1_), channel_id=1, source_target_pairs={{0,16},{8,24},{16,0},{24,8},{1,17},{9,25},{17,1},{25,9},{2,18},{10... | collective-permute-start | bytes 36872 | tf_op jit(solution)/shard_map/ppermute | solution.py:47
  10.0 4.7 %collective-permute-start.6 = (bf16[2,128,128]{2,1,0:T(8,128)(2,1)S(1)}, bf16[2,128,128]{2,1,0:T(8,128)(2,1)S(1)}, u32[]{:S(2)}, u32[]{:S(2)}) collective-permute-start(bf16[2,128,128]{2,1,0:T(8,128)(2,1)S(1)} %get-tuple-element.52), channel_id=1, source_target_pairs={{0,7},{1,0},{2,1},{3,2},{4,3},{5,4},{6,5},{7,6},{8,15},{9,8},{10,9... | collective-permute-start | bytes 196616 | tf_op jit(solution)/shard_map/ppermute | solution.py:47
  13.5 3.3 %collective-permute-start.4 = (bf16[2,48,128]{2,1,0:T(8,128)(2,1)S(1)}, bf16[2,48,128]{2,1,0:T(8,128)(2,1)S(1)}, u32[]{:S(2)}, u32[]{:S(2)}) collective-permute-start(bf16[2,48,128]{2,1,0:T(8,128)(2,1)S(1)} %get-tuple-element.49), channel_id=1, source_target_pairs={{0,1},{2,3},{4,5},{6,7},{1,0},{3,2},{5,4},{7,6},{8,9},{10,11},{12,... | collective-permute-start | bytes 73736 | tf_op jit(solution)/shard_map/ppermute | solution.py:51
  14.7 8.1 %collective-permute-start.8 = (bf16[23,16,128]{2,1,0:T(8,128)(2,1)S(1)}, bf16[23,16,128]{2,1,0:T(8,128)(2,1)S(1)}, u32[]{:S(2)}, u32[]{:S(2)}) collective-permute-start(bf16[23,16,128]{2,1,0:T(8,128)(2,1)S(1)} %get-tuple-element.113), channel_id=1, source_target_pairs={{0,24},{8,0},{16,8},{24,16},{1,25},{9,1},{17,9},{25,17},{2,26},{10... | collective-permute-start | bytes 282632 | tf_op jit(solution)/shard_map/ppermute | solution.py:47
  16.2 6.6 %collective-permute-start.7 = (bf16[23,16,128]{2,1,0:T(8,128)(2,1)S(1)}, bf16[23,16,128]{2,1,0:T(8,128)(2,1)S(1)}, u32[]{:S(2)}, u32[]{:S(2)}) collective-permute-start(bf16[23,16,128]{2,1,0:T(8,128)(2,1)S(1)} %get-tuple-element.114), channel_id=1, source_target_pairs={{0,8},{8,16},{16,24},{24,0},{1,9},{9,17},{17,25},{25,1},{2,10},{10... | collective-permute-start | bytes 282632 | tf_op jit(solution)/shard_map/ppermute | solution.py:47
  22.8 5.3 %copy-start.6 = (f32[4,64,128]{2,1,0:T(8,128)S(1)}, f32[4,64,128]{2,1,0:T(8,128)}, u32[]{:S(2)}) copy-start(f32[4,64,128]{2,1,0:T(8,128)} %constant.18.clone.refs_0_) | copy-start | bytes 393220
  24.5 6.6 %collective-permute-start.10 = (bf16[2,128,128]{2,1,0:T(8,128)(2,1)S(1)}, bf16[2,128,128]{2,1,0:T(8,128)(2,1)S(1)}, u32[]{:S(2)}, u32[]{:S(2)}) collective-permute-start(bf16[2,128,128]{2,1,0:T(8,128)(2,1)S(1)} %get-tuple-element.60), channel_id=1, source_target_pairs={{0,1},{1,2},{2,3},{3,4},{4,5},{5,6},{6,7},{7,0},{8,9},{9,10},{10,1... | collective-permute-start | bytes 196616 | tf_op jit(solution)/shard_map/ppermute | solution.py:47
  24.8 6.3 %collective-permute-start.11 = (bf16[2,128,128]{2,1,0:T(8,128)(2,1)S(1)}, bf16[2,128,128]{2,1,0:T(8,128)(2,1)S(1)}, u32[]{:S(2)}, u32[]{:S(2)}) collective-permute-start(bf16[2,128,128]{2,1,0:T(8,128)(2,1)S(1)} %get-tuple-element.64), channel_id=1, source_target_pairs={{0,7},{1,0},{2,1},{3,2},{4,3},{5,4},{6,5},{7,6},{8,15},{9,8},{10,9... | collective-permute-start | bytes 196616 | tf_op jit(solution)/shard_map/ppermute | solution.py:47
  31.2 7.0 %collective-permute-start.12 = (bf16[20,16,128]{2,1,0:T(8,128)(2,1)S(1)}, bf16[20,16,128]{2,1,0:T(8,128)(2,1)S(1)}, u32[]{:S(2)}, u32[]{:S(2)}) collective-permute-start(bf16[20,16,128]{2,1,0:T(8,128)(2,1)S(1)} %pad_maximum_fusion.2), channel_id=1, source_target_pairs={{0,8},{8,16},{16,24},{24,0},{1,9},{9,17},{17,25},{25,1},{2,10},{10... | collective-permute-start | bytes 245768 | tf_op jit(solution)/shard_map/ppermute | solution.py:47
  33.6 4.7 %collective-permute-start.13 = (bf16[20,16,128]{2,1,0:T(8,128)(2,1)S(1)}, bf16[20,16,128]{2,1,0:T(8,128)(2,1)S(1)}, u32[]{:S(2)}, u32[]{:S(2)}) collective-permute-start(bf16[20,16,128]{2,1,0:T(8,128)(2,1)S(1)} %pad_maximum_fusion.3), channel_id=1, source_target_pairs={{0,24},{8,0},{16,8},{24,16},{1,25},{9,1},{17,9},{25,17},{2,26},{10... | collective-permute-start | bytes 245768 | tf_op jit(solution)/shard_map/ppermute | solution.py:47
  40.1 5.5 %collective-permute-start.14 = (bf16[2,128,128]{2,1,0:T(8,128)(2,1)S(1)}, bf16[2,128,128]{2,1,0:T(8,128)(2,1)S(1)}, u32[]{:S(2)}, u32[]{:S(2)}) collective-permute-start(bf16[2,128,128]{2,1,0:T(8,128)(2,1)S(1)} %get-tuple-element.77), channel_id=1, source_target_pairs={{0,1},{1,2},{2,3},{3,4},{4,5},{5,6},{6,7},{7,0},{8,9},{9,10},{10,1... | collective-permute-start | bytes 196616 | tf_op jit(solution)/shard_map/ppermute | solution.py:47
  40.2 5.5 %collective-permute-start.15 = (bf16[2,128,128]{2,1,0:T(8,128)(2,1)S(1)}, bf16[2,128,128]{2,1,0:T(8,128)(2,1)S(1)}, u32[]{:S(2)}, u32[]{:S(2)}) collective-permute-start(bf16[2,128,128]{2,1,0:T(8,128)(2,1)S(1)} %get-tuple-element.78), channel_id=1, source_target_pairs={{0,7},{1,0},{2,1},{3,2},{4,3},{5,4},{6,5},{7,6},{8,15},{9,8},{10,9... | collective-permute-start | bytes 196616 | tf_op jit(solution)/shard_map/ppermute | solution.py:47
  45.7 6.1 %collective-permute-start.16 = (bf16[20,16,128]{2,1,0:T(8,128)(2,1)S(1)}, bf16[20,16,128]{2,1,0:T(8,128)(2,1)S(1)}, u32[]{:S(2)}, u32[]{:S(2)}) collective-permute-start(bf16[20,16,128]{2,1,0:T(8,128)(2,1)S(1)} %pad_maximum_fusion.4), channel_id=1, source_target_pairs={{0,8},{8,16},{16,24},{24,0},{1,9},{9,17},{17,25},{25,1},{2,10},{10... | collective-permute-start | bytes 245768 | tf_op jit(solution)/shard_map/ppermute | solution.py:47
  47.2 4.6 %collective-permute-start.17 = (bf16[20,16,128]{2,1,0:T(8,128)(2,1)S(1)}, bf16[20,16,128]{2,1,0:T(8,128)(2,1)S(1)}, u32[]{:S(2)}, u32[]{:S(2)}) collective-permute-start(bf16[20,16,128]{2,1,0:T(8,128)(2,1)S(1)} %pad_maximum_fusion.5), channel_id=1, source_target_pairs={{0,24},{8,0},{16,8},{24,16},{1,25},{9,1},{17,9},{25,17},{2,26},{10... | collective-permute-start | bytes 245768 | tf_op jit(solution)/shard_map/ppermute | solution.py:47
  53.4 6.1 %collective-permute-start.18 = (bf16[2,128,128]{2,1,0:T(8,128)(2,1)S(1)}, bf16[2,128,128]{2,1,0:T(8,128)(2,1)S(1)}, u32[]{:S(2)}, u32[]{:S(2)}) collective-permute-start(bf16[2,128,128]{2,1,0:T(8,128)(2,1)S(1)} %get-tuple-element.84), channel_id=1, source_target_pairs={{0,1},{1,2},{2,3},{3,4},{4,5},{5,6},{6,7},{7,0},{8,9},{9,10},{10,1... | collective-permute-start | bytes 196616 | tf_op jit(solution)/shard_map/ppermute | solution.py:47
  53.5 6.1 %collective-permute-start.19 = (bf16[2,128,128]{2,1,0:T(8,128)(2,1)S(1)}, bf16[2,128,128]{2,1,0:T(8,128)(2,1)S(1)}, u32[]{:S(2)}, u32[]{:S(2)}) collective-permute-start(bf16[2,128,128]{2,1,0:T(8,128)(2,1)S(1)} %get-tuple-element.85), channel_id=1, source_target_pairs={{0,7},{1,0},{2,1},{3,2},{4,3},{5,4},{6,5},{7,6},{8,15},{9,8},{10,9... | collective-permute-start | bytes 196616 | tf_op jit(solution)/shard_map/ppermute | solution.py:47
  59.6 6.0 %collective-permute-start.20 = (bf16[20,16,128]{2,1,0:T(8,128)(2,1)S(1)}, bf16[20,16,128]{2,1,0:T(8,128)(2,1)S(1)}, u32[]{:S(2)}, u32[]{:S(2)}) collective-permute-start(bf16[20,16,128]{2,1,0:T(8,128)(2,1)S(1)} %pad_maximum_fusion.6), channel_id=1, source_target_pairs={{0,8},{8,16},{16,24},{24,0},{1,9},{9,17},{17,25},{25,1},{2,10},{10... | collective-permute-start | bytes 245768 | tf_op jit(solution)/shard_map/ppermute | solution.py:47
  60.8 4.8 %collective-permute-start.21 = (bf16[20,16,128]{2,1,0:T(8,128)(2,1)S(1)}, bf16[20,16,128]{2,1,0:T(8,128)(2,1)S(1)}, u32[]{:S(2)}, u32[]{:S(2)}) collective-permute-start(bf16[20,16,128]{2,1,0:T(8,128)(2,1)S(1)} %pad_maximum_fusion.7), channel_id=1, source_target_pairs={{0,24},{8,0},{16,8},{24,16},{1,25},{9,1},{17,9},{25,17},{2,26},{10... | collective-permute-start | bytes 245768 | tf_op jit(solution)/shard_map/ppermute | solution.py:47

commit v4 on v3

--- a/solution.py
+++ b/solution.py
@@ -55,6 +55,24 @@
     return swap(cells, axis, [(i, i + 1) for i in range(0, lax.axis_size(axis), 2)])
 
 
+def outer_columns(rows, cols):
+    pairs = []
+    for r in range(rows):
+        for c in range(cols):
+            to = c - 1 if c % 2 == 0 else c + 1
+            pairs.append((r * cols + c, r * cols + to if 0 <= to < cols else (r ^ 1) * cols + c))
+    return pairs
+
+
+def outer_rows(rows, cols):
+    pairs = []
+    for r in range(rows):
+        for c in range(cols):
+            to = r - 1 if r % 2 == 0 else r + 1
+            pairs.append((r * cols + c, to * cols + c if 0 <= to < rows else r * cols + (c ^ 1)))
+    return pairs
+
+
 def bank_kernel(bank_ref, out_ref):
     rows, taps = bank_ref.shape
     for block in range(rows // TILE):
@@ -71,7 +89,7 @@
         for k in range(out_ref.shape[0]):
             got = jnp.zeros((TAP_ROWS, TILE), F32)
             for s, piece in enumerate(pieces):
-                first = lax.rem(meta_ref[5] + cols - 2 * s, cols) * zones
+                first = (meta_ref[5] ^ (2 * s)) * zones
                 for m in range(zones):
                     got = jnp.where(
                         ids[k : k + 1] == first + m, piece[:, m * TILE : (m + 1) * TILE].astype(F32), got
@@ -129,7 +147,7 @@
         coarse = inverse_ref.shape[1] // rows
         smooth = jnp.zeros((TILE, illum[0].shape[1]), F32)
         for s in range(rows):
-            first = pl.multiple_of(lax.rem(meta_ref[4] + rows - s, rows) * coarse, coarse)
+            first = pl.multiple_of((meta_ref[4] ^ s) * coarse, coarse)
             profile = sum(illum[s][n].astype(F32) for n in range(3))
             smooth = smooth + lax.dot_general(
                 inverse_ref[meta_ref[4], pl.ds(first, coarse), :],
@@ -426,7 +444,10 @@
         ]
 
     def exchanged(to_right, to_left):
-        return shift(to_right, "col", 1), shift(to_left, "col", -1)
+        even = meta[5] % 2 == 0
+        near = swap_pairs(jnp.where(even, to_right, to_left), "col")
+        far = lax.ppermute(jnp.where(even, to_left, to_right), ("row", "col"), outer_columns(n_row, n_col))
+        return jnp.where(even, far, near), jnp.where(even, near, far)
 
     blended = zone_ids.shape[-1]
     flat = (zones_here * depth * 2 * rank, taps)
@@ -437,7 +458,7 @@
         name="bank",
         flops=4 * 10**9,
     )(psf_bank.reshape(flat))
-    pieces = [bank] + [shift(bank, "col", s) for s in range(2, n_col, 2)]
+    pieces = [bank] + [lax.ppermute(bank, "col", [(i, i ^ s) for i in range(n_col)]) for s in range(2, n_col, 2)]
     field, to_right, to_left = call(
         first_kernel, (narrow, strip, strip), [VMEM], name="first", flops=10**9
     )(estimate)
@@ -487,7 +508,10 @@
         making = () if ready else (shape(TILE, 4 * TILE), shape(TILE, 8 * TILE), shape(2 * HALO, 2 * TILE))
         making = making if ct is not None else (shape(2 * TILE, 8 * TILE), *making)
         scratch = [pltpu.VMEM((4, 8 * TILE, TILE), BF16)]
-        bot, top = shift(ends[0], "row", -1), shift(ends[1], "row", 1)
+        even = meta[4] % 2 == 0
+        near = swap_pairs(jnp.where(even, ends[1], ends[0]), "row")
+        far = lax.ppermute(jnp.where(even, ends[0], ends[1]), ("row", "col"), outer_rows(n_row, n_col))
+        bot, top = jnp.where(even, near, far), jnp.where(even, far, near)
         rim = jax.ShapeDtypeStruct((depth, 2 * HALO, TILE), F32)
         outs = ((volume,) if part == 1 else ()) + (() if last else (narrow, strip, strip))
         main, *got = call(
@@ -511,19 +535,18 @@
             name="edge",
             flops=2 * 10**9,
         )(meta, cw, edge, main, top, bot, other, inv, *got)
-        return done, (ct, inv, cw, rt, edge), (top, bot)
+        return done, (ct, inv, cw, rt, edge), near
 
     current = estimate
-    far = [shift(plane, "row", s) for s in range(2, n_row - 1)]
+    others = [lax.ppermute(plane, "row", [(i, i ^ s) for i in range(n_row)]) for s in range(2, n_row)]
     forward = (None, jnp.zeros((groups, TILE, PACK), F32))
     backward = None
     for step in range(ITERS):
         last = step == ITERS - 1
-        (ratio, *strips), forward, ends = blur(0, False, forward, field, left, right, ends, observed)
+        (ratio, *strips), forward, near = blur(0, False, forward, field, left, right, ends, observed)
         left, right = exchanged(*strips)
         if backward is None:
-            above, below = (end[-3:] for end in ends)
-            backward = bands(1, lax.optimization_barrier((uv, strips[0]))[0], plane, above, *far, below)
+            backward = bands(1, lax.optimization_barrier((uv, strips[0]))[0], plane, near[-3:], *others)
         ends = ends_of(ratio, left, right)
         (current, *rest), backward, _ = blur(1, last, backward, ratio, left, right, ends, current)
         if not last:

time: 68.3 us -> 60.4 us (0.88)
  starting transfers between devices: 33.1 us -> 25.5 us
  waiting for transfers between devices: 5.72 us -> 5.02 us
    ppermute x20 -> x13, starting transfers between devices: 33.1 us -> 16.6 us  [the longest x4 7.88 us: exchanged(): lax.ppermute(jnp.where(even, to_left, to_right), ('row', 'col'), outer_co...]
    ppermute x2 -> x10, starting transfers between devices: 0.07 us -> 8.84 us  [swap(): return lax.ppermute(cells, axis, pairs + [(j, i) for i, j in pairs])]
    ppermute x20 -> x13, waiting for transfers between devices: 5.68 us -> 4.47 us  [the longest x4 4.45 us: exchanged(): lax.ppermute(jnp.where(even, to_left, to_right), ('row', 'col'), outer_co...]
  transfers between devices with their start and end apart: 22 -> 23, of which waited for: 4 -> 5; matrix products, arithmetic and copies ran while one was open for 0% -> 0% of each run, Pallas kernels for 32% -> 36%
where the time goes in v4:
time: 60.4 us; the launch traced here: 60.3 us
  Pallas kernels  27.9 us (46%)
  starting transfers between devices  25.5 us (42%)
  waiting for transfers between devices  5.02 us (8%)
  local copies, waits for them, and re-layouts  1.14 us (2%)
    pallas_call x4, Pallas kernels, blur(): call(functools.partial(main_kernel, part, len(making) - 2 if making else...  15.3 us
    ppermute x10, starting transfers between devices, swap(): return lax.ppermute(cells, axis, pairs + [(j, i) for i, j in pairs])  8.84 us
    ppermute x4, starting transfers between devices, exchanged(): lax.ppermute(jnp.where(even, to_left, to_right), ('row', 'col'), outer_co...  7.88 us
    pallas_call x4, Pallas kernels, blur(): call(functools.partial(edge_kernel, part), outs, [SMEM] + [VMEM] * (7 + l...  7.66 us
    ppermute x3, starting transfers between devices, shards(): lax.ppermute(bank, 'col', [(i, i ^ s) for i in range(n_col)])  5.76 us
    ppermute x4, waiting for transfers between devices, exchanged(): lax.ppermute(jnp.where(even, to_left, to_right), ('row', 'col'), outer_co...  4.45 us
    pallas_call x1, Pallas kernels, bands(): call(functools.partial(bands_kernel, part, n_row), outs, [SMEM] + [VMEM]...  3.15 us
    ppermute x2, starting transfers between devices, shards(): lax.ppermute(plane, 'row', [(i, i ^ s) for i in range(n_row)])  2.77 us
  transfers between devices with their start and end apart: 23, of which 5 were waited for; matrix products, arithmetic and copies ran while one was open for 0% of the time, Pallas kernels for 36%

profile of v4, /device:TPU:0, one launch (start us, length us, event | category | flops | bytes accessed | tf_op | source)
XLA Modules:
  0.0 60.3 jit_solution(2207628022913914371)
XLA Ops:
  0.0 0.9 %copy-done.5 = f32[4,16,2,4,33]{4,3,2,1,0:T(4,128)S(1)} copy-done((f32[4,16,2,4,33]{4,3,2,1,0:T(4,128)S(1)}, f32[4,16,2,4,33]{4,3,2,1,0:T(4,128)}, u32[]{:S(2)}) %copy-start.5) | copy-done | bytes 67608
  1.0 0.1 bank.1.refs_0_
  1.1 0.0 copy-start.4
  1.1 5.1 %collective-permute-start.3 = (bf16[48,512]{1,0:T(8,128)(2,1)S(1)}, bf16[48,512]{1,0:T(8,128)(2,1)S(1)}, u32[]{:S(2)}, u32[]{:S(2)}) collective-permute-start(bf16[48,512]{1,0:T(8,128)(2,1)S(1)} %bank.1.refs_0_), channel_id=1, source_target_pairs={{0,6},{1,7},{2,4},{3,5},{4,2},{5,3},{6,0},{7,1},{8,14},{9,15},{10,... | collective-permute-start | bytes 147464 | tf_op jit(solution)/shard_map/ppermute | solution.py:461
  6.2 0.0 collective-permute-start.2
  6.2 0.6 %collective-permute-start.1 = (bf16[48,512]{1,0:T(8,128)(2,1)S(1)}, bf16[48,512]{1,0:T(8,128)(2,1)S(1)}, u32[]{:S(2)}, u32[]{:S(2)}) collective-permute-start(bf16[48,512]{1,0:T(8,128)(2,1)S(1)} %bank.1.refs_0_), channel_id=1, source_target_pairs={{0,2},{1,3},{2,0},{3,1},{4,6},{5,7},{6,4},{7,5},{8,10},{9,11},{10,... | collective-permute-start | bytes 147464 | tf_op jit(solution)/shard_map/ppermute | solution.py:461
  6.8 0.0 copy-done
  6.8 0.2 keys.1
  7.0 0.0 collective-permute-start
  7.0 0.4 first.1
  7.5 0.6 collective-permute-start.6
  8.0 0.1 collective-permute-done.other_ref
  8.1 1.6 %collective-permute-start.5 = (bf16[2,128,128]{2,1,0:T(8,128)(2,1)S(1)}, bf16[2,128,128]{2,1,0:T(8,128)(2,1)S(1)}, u32[]{:S(2)}, u32[]{:S(2)}) collective-permute-start(bf16[2,128,128]{2,1,0:T(8,128)(2,1)S(1)} %get-tuple-element.128), channel_id=1, source_target_pairs={{0,8},{1,2},{2,1},{3,4},{4,3},{5,6},{6,5},{7,15},{8,0},{9,10},{10,... | collective-permute-start | bytes 196616 | tf_op jit(solution)/shard_map/ppermute | solution.py:449
  9.8 0.1 stack.43.meta_ref
  9.9 0.0 collective-permute-done.3.refs_3_
  9.9 1.5 %collective-permute-start.10 = (bf16[3,16,128]{2,1,0:T(8,128)(2,1)S(1)}, bf16[3,16,128]{2,1,0:T(8,128)(2,1)S(1)}, u32[]{:S(2)}, u32[]{:S(2)}) collective-permute-start(bf16[3,16,128]{2,1,0:T(8,128)(2,1)S(1)} %get-tuple-element.56.refs_1_), channel_id=1, source_target_pairs={{0,24},{8,16},{16,8},{24,0},{1,25},{9,17},{17,9},{25,1},{2,26},{10... | collective-permute-start | bytes 36872 | tf_op jit(solution)/shard_map/ppermute | solution.py:541
  11.4 0.0 collective-permute-done.2.refs_2_
  11.4 1.3 %collective-permute-start.9 = (bf16[3,16,128]{2,1,0:T(8,128)(2,1)S(1)}, bf16[3,16,128]{2,1,0:T(8,128)(2,1)S(1)}, u32[]{:S(2)}, u32[]{:S(2)}) collective-permute-start(bf16[3,16,128]{2,1,0:T(8,128)(2,1)S(1)} %get-tuple-element.56.refs_1_), channel_id=1, source_target_pairs={{0,16},{8,24},{16,0},{24,8},{1,17},{9,25},{17,1},{25,9},{2,18},{10... | collective-permute-start | bytes 36872 | tf_op jit(solution)/shard_map/ppermute | solution.py:541
  12.7 0.0 collective-permute-done.1.refs_1_
  12.7 0.7 %pick.1 = (bf16[2,48,128]{2,1,0:T(8,128)(2,1)S(1)}, bf16[2,48,128]{2,1,0:T(8,128)(2,1)S(1)}) custom-call(s32[6]{0:T(128)S(1)} %stack.43.meta_ref, f32[4,128]{1,0:T(4,128)S(1)} %get-tuple-element.47.mine_ref.keys_ref, f32[4,128]{1,0:T(4,128)S(1)} %collective-permute-done.other_ref, bf16[48,512]{1,0:T(8,128)(2,1)S(1)} %bank.1.refs_0_, ...), custom_call_target="tpu_custom_call" | custom-call | bytes 1048576 | tf_op jit(solution)/shard_map/pick/pallas_call | solution.py:475
  13.4 0.1 collective-permute-start.4
  13.5 0.0 collective-permute-done.6
  13.5 0.0 collective-permute-done.5
  13.6 1.6 %collective-permute-start.8 = (bf16[23,16,128]{2,1,0:T(8,128)(2,1)S(1)}, bf16[23,16,128]{2,1,0:T(8,128)(2,1)S(1)}, u32[]{:S(2)}, u32[]{:S(2)}) collective-permute-start(bf16[23,16,128]{2,1,0:T(8,128)(2,1)S(1)} %get-tuple-element.99), channel_id=1, source_target_pairs={{0,8},{16,24},{8,0},{24,16},{1,9},{17,25},{9,1},{25,17},{2,10},{18... | collective-permute-start | bytes 282632 | tf_op jit(solution)/shard_map/ppermute | solution.py:51
  15.1 0.2 collective-permute-start.7
  15.3 0.0 collective-permute-done.4.other_ref
  15.3 0.5 taps.1.ct_ref.rt_ref.uv_ref
  15.9 5.5 %main.4 = (f32[16,32,128]{2,1,0:T(8,128)S(1)}, bf16[16,128,128]{2,1,0:T(8,128)(2,1)S(1)}, bf16[2,128,128]{2,1,0:T(8,128)(2,1)S(1)}, bf16[2,128,128]{2,1,0:T(8,12...) custom-call(s32[6]{0:T(128)S(1)} %stack.43.meta_ref, ...), custom_call_target="tpu_custom_call" | custom-call | flops 4000000000 | bytes 1048576 | tf_op jit(solution)/shard_map/main/pallas_call | solution.py:517
  21.3 0.0 collective-permute-done.8
  21.3 0.0 collective-permute-done.7
  21.4 1.7 %edge.4 = (bf16[16,128,128]{2,1,0:T(8,128)(2,1)S(1)}, bf16[2,128,128]{2,1,0:T(8,128)(2,1)S(1)}, bf16[2,128,128]{2,1,0:T(8,128)(2,1)S(1)}) custom-call(s32[6]{0:T(128)S(1)} %stack.43.meta_ref, bf16[16,128,512]{2,1,0:T(8,128)(2,1)S(1)} %get-tuple-element.53.cw_ref, bf16[16,32,256]{2,1,0:T(8,128)(2,1)S(1)} %get-tuple-element.54.edge_ref, ...), custom_call_target="tpu_custom_call" | custom-call | flops 2000000000 | bytes 1048576 | tf_op jit(solution)/shard_map/edge/pallas_call | solution.py:530
  23.1 0.4 collective-permute-start.12
  23.4 1.8 %collective-permute-start.11 = (bf16[2,128,128]{2,1,0:T(8,128)(2,1)S(1)}, bf16[2,128,128]{2,1,0:T(8,128)(2,1)S(1)}, u32[]{:S(2)}, u32[]{:S(2)}) collective-permute-start(bf16[2,128,128]{2,1,0:T(8,128)(2,1)S(1)} %get-tuple-element.124), channel_id=1, source_target_pairs={{0,8},{1,2},{2,1},{3,4},{4,3},{5,6},{6,5},{7,15},{8,0},{9,10},{10,... | collective-permute-start | bytes 196616 | tf_op jit(solution)/shard_map/ppermute | solution.py:449
  25.2 0.0 collective-permute-done.10.refs_4_
  25.2 0.0 collective-permute-done.9.refs_3_
  25.3 3.1 %bands.1 = (bf16[16,256,1024]{2,1,0:T(8,128)(2,1)S(1)}, f32[2,128,8]{2,1,0:T(8,128)S(1)}) custom-call(s32[6]{0:T(128)S(1)} %stack.43.meta_ref, f32[2,16,8,256]{3,2,1,0:T(8,128)S(1)} %taps.1.ct_ref.rt_ref.uv_ref, f32[4,64,128]{2,1,0:T(8,128)S(1)} %copy-done.6, bf16[3,16,128]{2,1,0:T(8,128)(2,1)S(1)} %get-tuple-element.56.refs_1_, ...), custom_call_target="tpu_custom_call" | custom-call | flops 4000000000 | bytes 1048576 | tf_op jit(solution)/shard_map/bands/pallas_call | solution.py:497
  28.4 0.0 collective-permute-done.12
  28.4 0.0 collective-permute-done.11
  28.5 1.1 %collective-permute-start.14 = (bf16[20,16,128]{2,1,0:T(8,128)(2,1)S(1)}, bf16[20,16,128]{2,1,0:T(8,128)(2,1)S(1)}, u32[]{:S(2)}, u32[]{:S(2)}) collective-permute-start(bf16[20,16,128]{2,1,0:T(8,128)(2,1)S(1)} %get-tuple-element.111), channel_id=1, source_target_pairs={{0,8},{16,24},{8,0},{24,16},{1,9},{17,25},{9,1},{25,17},{2,10},{18... | collective-permute-start | bytes 245768 | tf_op jit(solution)/shard_map/ppermute | solution.py:51
  29.6 0.0 collective-permute-start.13
  29.6 3.8 %main.5 = (f32[16,32,128]{2,1,0:T(8,128)S(1)}, f32[16,128,128]{2,1,0:T(8,128)S(1)}, bf16[16,128,128]{2,1,0:T(8,128)(2,1)S(1)}, bf16[2,128,128]{2,1,0:T(8,128)(2,...) custom-call(s32[6]{0:T(128)S(1)} %stack.43.meta_ref, ...), custom_call_target="tpu_custom_call" | custom-call | flops 4000000000 | bytes 1048576 | tf_op jit(solution)/shard_map/main/pallas_call | solution.py:517
  33.4 0.0 collective-permute-done.14
  33.5 0.0 collective-permute-done.13
  33.5 1.8 %edge.5 = (f32[16,128,128]{2,1,0:T(8,128)S(1)}, bf16[16,128,128]{2,1,0:T(8,128)(2,1)S(1)}, bf16[2,128,128]{2,1,0:T(8,128)(2,1)S(1)}, bf16[2,128,128]{2,1,0:T(8,128)(2,1)S(1)}) custom-call(s32[6]{0:T(128)S(1)} %stack.43.meta_ref, bf16[16,128,512]{2,1,0:T(8,128)(2,1)S(1)} %get-tuple-element.66.cw_ref, bf16[16,32,256]{2,1,0:T(8,128)(2,1)S(1)} %get-tuple-element.67.edge_ref, ...), custom_call_target="tpu_custom_call" | custom-call | flops 2000000000 | bytes 1048576 | tf_op jit(solution)/shard_map/edge/pallas_call | solution.py:530
  35.3 0.6 collective-permute-start.16
  35.9 2.1 %collective-permute-start.15 = (bf16[2,128,128]{2,1,0:T(8,128)(2,1)S(1)}, bf16[2,128,128]{2,1,0:T(8,128)(2,1)S(1)}, u32[]{:S(2)}, u32[]{:S(2)}) collective-permute-start(bf16[2,128,128]{2,1,0:T(8,128)(2,1)S(1)} %get-tuple-element.120), channel_id=1, source_target_pairs={{0,8},{1,2},{2,1},{3,4},{4,3},{5,6},{6,5},{7,15},{8,0},{9,10},{10,... | collective-permute-start | bytes 196616 | tf_op jit(solution)/shard_map/ppermute | solution.py:449
  38.0 0.0 collective-permute-done.16
  38.0 2.2 %collective-permute-done.15 = bf16[2,128,128]{2,1,0:T(8,128)(2,1)S(1)} collective-permute-done((bf16[2,128,128]{2,1,0:T(8,128)(2,1)S(1)}, bf16[2,128,128]{2,1,0:T(8,128)(2,1)S(1)}, u32[]{:S(2)}, u32[]{:S(2)}) %collective-permute-start.15) | collective-permute-done | bytes 65568 | tf_op jit(solution)/shard_map/ppermute | solution.py:449
  40.3 2.1 %collective-permute-start.18 = (bf16[20,16,128]{2,1,0:T(8,128)(2,1)S(1)}, bf16[20,16,128]{2,1,0:T(8,128)(2,1)S(1)}, u32[]{:S(2)}, u32[]{:S(2)}) collective-permute-start(bf16[20,16,128]{2,1,0:T(8,128)(2,1)S(1)} %get-tuple-element.107), channel_id=1, source_target_pairs={{0,8},{16,24},{8,0},{24,16},{1,9},{17,25},{9,1},{25,17},{2,10},{18... | collective-permute-start | bytes 245768 | tf_op jit(solution)/shard_map/ppermute | solution.py:51
  42.4 0.0 collective-permute-start.17
  42.4 3.1 %main.6 = (f32[16,32,128]{2,1,0:T(8,128)S(1)}, bf16[16,128,128]{2,1,0:T(8,128)(2,1)S(1)}, bf16[2,128,128]{2,1,0:T(8,128)(2,1)S(1)}, bf16[2,128,128]{2,1,0:T(8,128)(2,1)S(1)}) custom-call(s32[6]{0:T(128)S(1)} %stack.43.meta_ref, bf16[16,256,1024]{2,1,0:T(8,128)(2,1)S(1)} %get-tuple-element.69.ct_ref, bf16[16,128,1024]{2,1,0:T(8,128)(2,1)S(1)} %get-tuple-element.70.rt_ref, ...), custom_call_target="tpu_custom_call" | custom-call | flops 4000000000 | bytes 1048576 | tf_op jit(solution)/shard_map/main/pallas_call | solution.py:517
  45.5 0.2 collective-permute-done.18
  45.6 0.0 collective-permute-done.17
  45.6 1.6 %edge.6 = (bf16[16,128,128]{2,1,0:T(8,128)(2,1)S(1)}, bf16[2,128,128]{2,1,0:T(8,128)(2,1)S(1)}, bf16[2,128,128]{2,1,0:T(8,128)(2,1)S(1)}) custom-call(s32[6]{0:T(128)S(1)} %stack.43.meta_ref, bf16[16,128,512]{2,1,0:T(8,128)(2,1)S(1)} %get-tuple-element.53.cw_ref, bf16[16,32,256]{2,1,0:T(8,128)(2,1)S(1)} %get-tuple-element.54.edge_ref, ...), custom_call_target="tpu_custom_call" | custom-call | flops 2000000000 | bytes 1048576 | tf_op jit(solution)/shard_map/edge/pallas_call | solution.py:530
  47.3 0.4 collective-permute-start.20
  47.7 2.4 %collective-permute-start.19 = (bf16[2,128,128]{2,1,0:T(8,128)(2,1)S(1)}, bf16[2,128,128]{2,1,0:T(8,128)(2,1)S(1)}, u32[]{:S(2)}, u32[]{:S(2)}) collective-permute-start(bf16[2,128,128]{2,1,0:T(8,128)(2,1)S(1)} %get-tuple-element.116), channel_id=1, source_target_pairs={{0,8},{1,2},{2,1},{3,4},{4,3},{5,6},{6,5},{7,15},{8,0},{9,10},{10,... | collective-permute-start | bytes 196616 | tf_op jit(solution)/shard_map/ppermute | solution.py:449
  50.1 0.0 collective-permute-done.20
  50.1 2.2 %collective-permute-done.19 = bf16[2,128,128]{2,1,0:T(8,128)(2,1)S(1)} collective-permute-done((bf16[2,128,128]{2,1,0:T(8,128)(2,1)S(1)}, bf16[2,128,128]{2,1,0:T(8,128)(2,1)S(1)}, u32[]{:S(2)}, u32[]{:S(2)}) %collective-permute-start.19) | collective-permute-done | bytes 65568 | tf_op jit(solution)/shard_map/ppermute | solution.py:449
  52.4 2.1 %collective-permute-start.22 = (bf16[20,16,128]{2,1,0:T(8,128)(2,1)S(1)}, bf16[20,16,128]{2,1,0:T(8,128)(2,1)S(1)}, u32[]{:S(2)}, u32[]{:S(2)}) collective-permute-start(bf16[20,16,128]{2,1,0:T(8,128)(2,1)S(1)} %get-tuple-element.103), channel_id=1, source_target_pairs={{0,8},{16,24},{8,0},{24,16},{1,9},{17,25},{9,1},{25,17},{2,10},{18... | collective-permute-start | bytes 245768 | tf_op jit(solution)/shard_map/ppermute | solution.py:51
  54.5 0.0 collective-permute-start.21
  54.5 2.9 %main.7 = (f32[16,32,128]{2,1,0:T(8,128)S(1)}, f32[16,128,128]{2,1,0:T(8,128)S(1)}) custom-call(s32[6]{0:T(128)S(1)} %stack.43.meta_ref, bf16[16,256,1024]{2,1,0:T(8,128)(2,1)S(1)} %get-tuple-element.62.ct_ref, bf16[16,128,1024]{2,1,0:T(8,128)(2,1)S(1)} %get-tuple-element.68.rt_ref, bf16[16,128,128]{2,1,0:T(8,128)(2,1)S(1)} %get-tuple-element.83.field_ref, ...), custom_call_target="tpu_custom_call" | custom-call | flops 4000000000 | bytes 1048576 | tf_op jit(solution)/shard_map/main/pallas_call | solution.py:517
  57.5 0.2 collective-permute-done.22
  57.7 0.0 collective-permute-done.21
  57.7 2.5 %edge.7 = f32[16,128,128]{2,1,0:T(8,128)} custom-call(s32[6]{0:T(128)S(1)} %stack.43.meta_ref, bf16[16,128,512]{2,1,0:T(8,128)(2,1)S(1)} %get-tuple-element.66.cw_ref, bf16[16,32,256]{2,1,0:T(8,128)(2,1)S(1)} %get-tuple-element.67.edge_ref, f32[16,32,128]{2,1,0:T(8,128)S(1)} %get-tuple-element.87.rim_ref, ...), custom_call_target="tpu_custom_call" | custom-call | flops 2000000000 | bytes 1048576 | tf_op jit(solution)/shard_map/edge/pallas_call | solution.py:530
  (40 shorter events, 0.4 us)
Async XLA Ops:
  0.0 0.9 %copy-start.5 = (f32[4,16,2,4,33]{4,3,2,1,0:T(4,128)S(1)}, f32[4,16,2,4,33]{4,3,2,1,0:T(4,128)}, u32[]{:S(2)}) copy-start(f32[4,16,2,4,33]{4,3,2,1,0:T(4,128)} %param.9) | copy-start | bytes 202756
  1.0 5.9 %copy-start = (f32[16,16,1]{1,2,0:T(1,128)S(1)}, f32[16,16,1]{1,2,0:T(1,128)}, u32[]{:S(2)}) copy-start(f32[16,16,1]{1,2,0:T(1,128)} %param.12) | copy-start | bytes 3076
  1.0 5.9 %copy-start.1 = (s32[1,1,16,2]{2,3,1,0:T(2,128)S(1)}, s32[1,1,16,2]{2,3,1,0:T(2,128)}, u32[]{:S(2)}) copy-start(s32[1,1,16,2]{2,3,1,0:T(2,128)} %param.10) | copy-start | bytes 388
  1.0 5.9 %copy-start.2 = (f32[1,1,16,2]{2,3,1,0:T(2,128)S(1)}, f32[1,1,16,2]{2,3,1,0:T(2,128)}, u32[]{:S(2)}) copy-start(f32[1,1,16,2]{2,3,1,0:T(2,128)} %param.11) | copy-start | bytes 388
  1.0 6.0 %copy-start.3 = (f32[16,128,128]{2,1,0:T(8,128)S(1)}, f32[16,128,128]{2,1,0:T(8,128)}, u32[]{:S(2)}) copy-start(f32[16,128,128]{2,1,0:T(8,128)} %a_ref.9) | copy-start | bytes 3145732
  1.1 14.8 %copy-start.4 = (f32[16,128,128]{2,1,0:T(8,128)S(1)}, f32[16,128,128]{2,1,0:T(8,128)}, u32[]{:S(2)}) copy-start(f32[16,128,128]{2,1,0:T(8,128)} %a_ref.11) | copy-start | bytes 3145732
  1.1 8.8 %collective-permute-start.3 = (bf16[48,512]{1,0:T(8,128)(2,1)S(1)}, bf16[48,512]{1,0:T(8,128)(2,1)S(1)}, u32[]{:S(2)}, u32[]{:S(2)}) collective-permute-start(bf16[48,512]{1,0:T(8,128)(2,1)S(1)} %bank.1.refs_0_), channel_id=1, source_target_pairs={{0,6},{1,7},{2,4},{3,5},{4,2},{5,3},{6,0},{7,1},{8,14},{9,15},{10,... | collective-permute-start | bytes 147464 | tf_op jit(solution)/shard_map/ppermute | solution.py:461
  6.2 5.3 %collective-permute-start.2 = (bf16[48,512]{1,0:T(8,128)(2,1)S(1)}, bf16[48,512]{1,0:T(8,128)(2,1)S(1)}, u32[]{:S(2)}, u32[]{:S(2)}) collective-permute-start(bf16[48,512]{1,0:T(8,128)(2,1)S(1)} %bank.1.refs_0_), channel_id=1, source_target_pairs={{0,4},{1,5},{2,6},{3,7},{4,0},{5,1},{6,2},{7,3},{8,12},{9,13},{10,... | collective-permute-start | bytes 147464 | tf_op jit(solution)/shard_map/ppermute | solution.py:461
  6.2 6.5 %collective-permute-start.1 = (bf16[48,512]{1,0:T(8,128)(2,1)S(1)}, bf16[48,512]{1,0:T(8,128)(2,1)S(1)}, u32[]{:S(2)}, u32[]{:S(2)}) collective-permute-start(bf16[48,512]{1,0:T(8,128)(2,1)S(1)} %bank.1.refs_0_), channel_id=1, source_target_pairs={{0,2},{1,3},{2,0},{3,1},{4,6},{5,7},{6,4},{7,5},{8,10},{9,11},{10,... | collective-permute-start | bytes 147464 | tf_op jit(solution)/shard_map/ppermute | solution.py:461
  7.0 1.2 %collective-permute-start = (f32[4,128]{1,0:T(4,128)S(1)}, f32[4,128]{1,0:T(4,128)S(1)}, u32[]{:S(2)}, u32[]{:S(2)}) collective-permute-start(f32[4,128]{1,0:T(4,128)S(1)} %get-tuple-element.47.mine_ref.keys_ref), channel_id=1, source_target_pairs={{0,1},{2,3},{4,5},{6,7},{1,0},{3,2},{5,4},{7,6},{8,9},{10,11},{12,... | collective-permute-start | bytes 6152 | tf_op jit(solution)/shard_map/ppermute | solution.py:51
  7.5 6.0 %collective-permute-start.6 = (bf16[2,128,128]{2,1,0:T(8,128)(2,1)S(1)}, bf16[2,128,128]{2,1,0:T(8,128)(2,1)S(1)}, u32[]{:S(2)}, u32[]{:S(2)}) collective-permute-start(bf16[2,128,128]{2,1,0:T(8,128)(2,1)S(1)} %get-tuple-element.127), channel_id=1, source_target_pairs={{0,1},{2,3},{4,5},{6,7},{1,0},{3,2},{5,4},{7,6},{8,9},{10,11},{12,... | collective-permute-start | bytes 196616 | tf_op jit(solution)/shard_map/ppermute | solution.py:51
  8.1 5.3 %collective-permute-start.5 = (bf16[2,128,128]{2,1,0:T(8,128)(2,1)S(1)}, bf16[2,128,128]{2,1,0:T(8,128)(2,1)S(1)}, u32[]{:S(2)}, u32[]{:S(2)}) collective-permute-start(bf16[2,128,128]{2,1,0:T(8,128)(2,1)S(1)} %get-tuple-element.128), channel_id=1, source_target_pairs={{0,8},{1,2},{2,1},{3,4},{4,3},{5,6},{6,5},{7,15},{8,0},{9,10},{10,... | collective-permute-start | bytes 196616 | tf_op jit(solution)/shard_map/ppermute | solution.py:449
  9.9 15.3 %collective-permute-start.10 = (bf16[3,16,128]{2,1,0:T(8,128)(2,1)S(1)}, bf16[3,16,128]{2,1,0:T(8,128)(2,1)S(1)}, u32[]{:S(2)}, u32[]{:S(2)}) collective-permute-start(bf16[3,16,128]{2,1,0:T(8,128)(2,1)S(1)} %get-tuple-element.56.refs_1_), channel_id=1, source_target_pairs={{0,24},{8,16},{16,8},{24,0},{1,25},{9,17},{17,9},{25,1},{2,26},{10... | collective-permute-start | bytes 36872 | tf_op jit(solution)/shard_map/ppermute | solution.py:541
  11.4 13.8 %collective-permute-start.9 = (bf16[3,16,128]{2,1,0:T(8,128)(2,1)S(1)}, bf16[3,16,128]{2,1,0:T(8,128)(2,1)S(1)}, u32[]{:S(2)}, u32[]{:S(2)}) collective-permute-start(bf16[3,16,128]{2,1,0:T(8,128)(2,1)S(1)} %get-tuple-element.56.refs_1_), channel_id=1, source_target_pairs={{0,16},{8,24},{16,0},{24,8},{1,17},{9,25},{17,1},{25,9},{2,18},{10... | collective-permute-start | bytes 36872 | tf_op jit(solution)/shard_map/ppermute | solution.py:541
  13.4 1.9 %collective-permute-start.4 = (bf16[2,48,128]{2,1,0:T(8,128)(2,1)S(1)}, bf16[2,48,128]{2,1,0:T(8,128)(2,1)S(1)}, u32[]{:S(2)}, u32[]{:S(2)}) collective-permute-start(bf16[2,48,128]{2,1,0:T(8,128)(2,1)S(1)} %get-tuple-element.49), channel_id=1, source_target_pairs={{0,1},{2,3},{4,5},{6,7},{1,0},{3,2},{5,4},{7,6},{8,9},{10,11},{12,... | collective-permute-start | bytes 73736 | tf_op jit(solution)/shard_map/ppermute | solution.py:51
  13.6 7.8 %collective-permute-start.8 = (bf16[23,16,128]{2,1,0:T(8,128)(2,1)S(1)}, bf16[23,16,128]{2,1,0:T(8,128)(2,1)S(1)}, u32[]{:S(2)}, u32[]{:S(2)}) collective-permute-start(bf16[23,16,128]{2,1,0:T(8,128)(2,1)S(1)} %get-tuple-element.99), channel_id=1, source_target_pairs={{0,8},{16,24},{8,0},{24,16},{1,9},{17,25},{9,1},{25,17},{2,10},{18... | collective-permute-start | bytes 282632 | tf_op jit(solution)/shard_map/ppermute | solution.py:51
  15.1 6.2 %collective-permute-start.7 = (bf16[23,16,128]{2,1,0:T(8,128)(2,1)S(1)}, bf16[23,16,128]{2,1,0:T(8,128)(2,1)S(1)}, u32[]{:S(2)}, u32[]{:S(2)}) collective-permute-start(bf16[23,16,128]{2,1,0:T(8,128)(2,1)S(1)} %get-tuple-element.100), channel_id=1, source_target_pairs={{0,1},{1,0},{2,3},{3,2},{4,5},{5,4},{6,7},{7,6},{8,16},{9,17},{10,... | collective-permute-start | bytes 282632 | tf_op jit(solution)/shard_map/ppermute | solution.py:513
  21.3 3.9 %copy-start.6 = (f32[4,64,128]{2,1,0:T(8,128)S(1)}, f32[4,64,128]{2,1,0:T(8,128)}, u32[]{:S(2)}) copy-start(f32[4,64,128]{2,1,0:T(8,128)} %constant.46.clone.refs_0_) | copy-start | bytes 393220
  23.1 5.4 %collective-permute-start.12 = (bf16[2,128,128]{2,1,0:T(8,128)(2,1)S(1)}, bf16[2,128,128]{2,1,0:T(8,128)(2,1)S(1)}, u32[]{:S(2)}, u32[]{:S(2)}) collective-permute-start(bf16[2,128,128]{2,1,0:T(8,128)(2,1)S(1)} %get-tuple-element.123), channel_id=1, source_target_pairs={{0,1},{2,3},{4,5},{6,7},{1,0},{3,2},{5,4},{7,6},{8,9},{10,11},{12,... | collective-permute-start | bytes 196616 | tf_op jit(solution)/shard_map/ppermute | solution.py:51
  23.4 5.0 %collective-permute-start.11 = (bf16[2,128,128]{2,1,0:T(8,128)(2,1)S(1)}, bf16[2,128,128]{2,1,0:T(8,128)(2,1)S(1)}, u32[]{:S(2)}, u32[]{:S(2)}) collective-permute-start(bf16[2,128,128]{2,1,0:T(8,128)(2,1)S(1)} %get-tuple-element.124), channel_id=1, source_target_pairs={{0,8},{1,2},{2,1},{3,4},{4,3},{5,6},{6,5},{7,15},{8,0},{9,10},{10,... | collective-permute-start | bytes 196616 | tf_op jit(solution)/shard_map/ppermute | solution.py:449
  28.5 4.9 %collective-permute-start.14 = (bf16[20,16,128]{2,1,0:T(8,128)(2,1)S(1)}, bf16[20,16,128]{2,1,0:T(8,128)(2,1)S(1)}, u32[]{:S(2)}, u32[]{:S(2)}) collective-permute-start(bf16[20,16,128]{2,1,0:T(8,128)(2,1)S(1)} %get-tuple-element.111), channel_id=1, source_target_pairs={{0,8},{16,24},{8,0},{24,16},{1,9},{17,25},{9,1},{25,17},{2,10},{18... | collective-permute-start | bytes 245768 | tf_op jit(solution)/shard_map/ppermute | solution.py:51
  29.6 3.8 %collective-permute-start.13 = (bf16[20,16,128]{2,1,0:T(8,128)(2,1)S(1)}, bf16[20,16,128]{2,1,0:T(8,128)(2,1)S(1)}, u32[]{:S(2)}, u32[]{:S(2)}) collective-permute-start(bf16[20,16,128]{2,1,0:T(8,128)(2,1)S(1)} %get-tuple-element.112), channel_id=1, source_target_pairs={{0,1},{1,0},{2,3},{3,2},{4,5},{5,4},{6,7},{7,6},{8,16},{9,17},{10,... | collective-permute-start | bytes 245768 | tf_op jit(solution)/shard_map/ppermute | solution.py:513
  35.3 2.7 %collective-permute-start.16 = (bf16[2,128,128]{2,1,0:T(8,128)(2,1)S(1)}, bf16[2,128,128]{2,1,0:T(8,128)(2,1)S(1)}, u32[]{:S(2)}, u32[]{:S(2)}) collective-permute-start(bf16[2,128,128]{2,1,0:T(8,128)(2,1)S(1)} %get-tuple-element.119), channel_id=1, source_target_pairs={{0,1},{2,3},{4,5},{6,7},{1,0},{3,2},{5,4},{7,6},{8,9},{10,11},{12,... | collective-permute-start | bytes 196616 | tf_op jit(solution)/shard_map/ppermute | solution.py:51
  35.9 4.3 %collective-permute-start.15 = (bf16[2,128,128]{2,1,0:T(8,128)(2,1)S(1)}, bf16[2,128,128]{2,1,0:T(8,128)(2,1)S(1)}, u32[]{:S(2)}, u32[]{:S(2)}) collective-permute-start(bf16[2,128,128]{2,1,0:T(8,128)(2,1)S(1)} %get-tuple-element.120), channel_id=1, source_target_pairs={{0,8},{1,2},{2,1},{3,4},{4,3},{5,6},{6,5},{7,15},{8,0},{9,10},{10,... | collective-permute-start | bytes 196616 | tf_op jit(solution)/shard_map/ppermute | solution.py:449
  40.3 5.3 %collective-permute-start.18 = (bf16[20,16,128]{2,1,0:T(8,128)(2,1)S(1)}, bf16[20,16,128]{2,1,0:T(8,128)(2,1)S(1)}, u32[]{:S(2)}, u32[]{:S(2)}) collective-permute-start(bf16[20,16,128]{2,1,0:T(8,128)(2,1)S(1)} %get-tuple-element.107), channel_id=1, source_target_pairs={{0,8},{16,24},{8,0},{24,16},{1,9},{17,25},{9,1},{25,17},{2,10},{18... | collective-permute-start | bytes 245768 | tf_op jit(solution)/shard_map/ppermute | solution.py:51
  42.4 3.2 %collective-permute-start.17 = (bf16[20,16,128]{2,1,0:T(8,128)(2,1)S(1)}, bf16[20,16,128]{2,1,0:T(8,128)(2,1)S(1)}, u32[]{:S(2)}, u32[]{:S(2)}) collective-permute-start(bf16[20,16,128]{2,1,0:T(8,128)(2,1)S(1)} %get-tuple-element.108), channel_id=1, source_target_pairs={{0,1},{1,0},{2,3},{3,2},{4,5},{5,4},{6,7},{7,6},{8,16},{9,17},{10,... | collective-permute-start | bytes 245768 | tf_op jit(solution)/shard_map/ppermute | solution.py:513
  47.3 2.8 %collective-permute-start.20 = (bf16[2,128,128]{2,1,0:T(8,128)(2,1)S(1)}, bf16[2,128,128]{2,1,0:T(8,128)(2,1)S(1)}, u32[]{:S(2)}, u32[]{:S(2)}) collective-permute-start(bf16[2,128,128]{2,1,0:T(8,128)(2,1)S(1)} %get-tuple-element.115), channel_id=1, source_target_pairs={{0,1},{2,3},{4,5},{6,7},{1,0},{3,2},{5,4},{7,6},{8,9},{10,11},{12,... | collective-permute-start | bytes 196616 | tf_op jit(solution)/shard_map/ppermute | solution.py:51
  47.7 4.6 %collective-permute-start.19 = (bf16[2,128,128]{2,1,0:T(8,128)(2,1)S(1)}, bf16[2,128,128]{2,1,0:T(8,128)(2,1)S(1)}, u32[]{:S(2)}, u32[]{:S(2)}) collective-permute-start(bf16[2,128,128]{2,1,0:T(8,128)(2,1)S(1)} %get-tuple-element.116), channel_id=1, source_target_pairs={{0,8},{1,2},{2,1},{3,4},{4,3},{5,6},{6,5},{7,15},{8,0},{9,10},{10,... | collective-permute-start | bytes 196616 | tf_op jit(solution)/shard_map/ppermute | solution.py:449
  52.4 5.3 %collective-permute-start.22 = (bf16[20,16,128]{2,1,0:T(8,128)(2,1)S(1)}, bf16[20,16,128]{2,1,0:T(8,128)(2,1)S(1)}, u32[]{:S(2)}, u32[]{:S(2)}) collective-permute-start(bf16[20,16,128]{2,1,0:T(8,128)(2,1)S(1)} %get-tuple-element.103), channel_id=1, source_target_pairs={{0,8},{16,24},{8,0},{24,16},{1,9},{17,25},{9,1},{25,17},{2,10},{18... | collective-permute-start | bytes 245768 | tf_op jit(solution)/shard_map/ppermute | solution.py:51
  54.5 3.2 %collective-permute-start.21 = (bf16[20,16,128]{2,1,0:T(8,128)(2,1)S(1)}, bf16[20,16,128]{2,1,0:T(8,128)(2,1)S(1)}, u32[]{:S(2)}, u32[]{:S(2)}) collective-permute-start(bf16[20,16,128]{2,1,0:T(8,128)(2,1)S(1)} %get-tuple-element.104), channel_id=1, source_target_pairs={{0,1},{1,0},{2,3},{3,2},{4,5},{5,4},{6,7},{7,6},{8,16},{9,17},{10,... | collective-permute-start | bytes 245768 | tf_op jit(solution)/shard_map/ppermute | solution.py:513

commit v5 on v4

--- a/solution.py
+++ b/solution.py
@@ -167,7 +167,8 @@
             column_bands(part, uv_ref, shifts_ref, g8 * PACK + i, i, ct_ref)
         return carry
 
-    lax.fori_loop(0, ct_ref.shape[0] // PACK, group, 0)
+    for g8 in range(ct_ref.shape[0] // PACK):
+        group(g8, 0)
 
 
 def start_shifts(shifts_ref):
@@ -308,7 +309,7 @@
                     ct_ref[z, TILE + t * HALO : TILE + (t + 1) * HALO, :] = jnp.zeros((HALO, 8 * TILE), BF16)
     inner = slice(HALO, TILE - HALO)
 
-    def group(g8, carry):
+    def group(g8):
         sides = sides_of(left_ref[g8], right_ref[g8], meta_ref)
         halos = [joined(*sides, parity) for parity in range(2)]
 
@@ -334,21 +335,16 @@
             if making:
                 other_bands(part, uv_ref, ct_ref, g8 * PACK + i, i, *made)
 
-        bands(0)
-        bands(1)
-        columns(0)
-        bands(2)
-        columns(1)
-        for i in range(PACK):
-            if i + 3 < PACK:
-                bands(i + 3)
-            if i + 2 < PACK:
-                columns(i + 2)
-            rows(i)
-        return carry
-
-    for g8 in range(field_ref.shape[0] // PACK):
-        group(g8, 0)
+        return bands, columns, rows
+
+    count = field_ref.shape[0]
+    steps = [group(g8) for g8 in range(count // PACK)]
+    bands, columns, rows = ([(step[n], i) for step in steps for i in range(PACK)] for n in range(3))
+    for z in range(-3, count):
+        for kind, ahead in ((bands, 3), (columns, 2), (rows, 0)):
+            if 0 <= z + ahead < count:
+                do, i = kind[z + ahead]
+                do(i)
 
 
 def edge_kernel(part, meta_ref, cw_ref, edge_ref, rim_ref, top_ref, bot_ref, a_ref, inv_ref, *refs):
@@ -445,8 +441,8 @@
 
     def exchanged(to_right, to_left):
         even = meta[5] % 2 == 0
+        far = lax.ppermute(jnp.where(even, to_left, to_right), ("row", "col"), outer_columns(n_row, n_col))
         near = swap_pairs(jnp.where(even, to_right, to_left), "col")
-        far = lax.ppermute(jnp.where(even, to_left, to_right), ("row", "col"), outer_columns(n_row, n_col))
         return jnp.where(even, far, near), jnp.where(even, near, far)
 
     blended = zone_ids.shape[-1]
@@ -509,8 +505,8 @@
         making = making if ct is not None else (shape(2 * TILE, 8 * TILE), *making)
         scratch = [pltpu.VMEM((4, 8 * TILE, TILE), BF16)]
         even = meta[4] % 2 == 0
+        far = lax.ppermute(jnp.where(even, ends[0], ends[1]), ("row", "col"), outer_rows(n_row, n_col))
         near = swap_pairs(jnp.where(even, ends[1], ends[0]), "row")
-        far = lax.ppermute(jnp.where(even, ends[0], ends[1]), ("row", "col"), outer_rows(n_row, n_col))
         bot, top = jnp.where(even, near, far), jnp.where(even, far, near)
         rim = jax.ShapeDtypeStruct((depth, 2 * HALO, TILE), F32)
         outs = ((volume,) if part == 1 else ()) + (() if last else (narrow, strip, strip))

time: 60.4 us -> 60.2 us (level)
  waiting for transfers between devices: 5.02 us -> 5.89 us
  Pallas kernels: 27.9 us -> 27.1 us
    pallas_call x1, Pallas kernels: 3.15 us -> 2.33 us  [bands(): call(functools.partial(bands_kernel, part, n_row), outs, [SMEM] + [VMEM]...]
  transfers between devices with their start and end apart: 23 -> 23, of which waited for: 5 -> 6; matrix products, arithmetic and copies ran while one was open for 0% -> 0% of each run, Pallas kernels for 36% -> 35%
where the time goes in v5:
time: 60.2 us; the launch traced here: 60 us
  Pallas kernels  27.1 us (45%)
  starting transfers between devices  25.2 us (42%)
  waiting for transfers between devices  5.89 us (10%)
  local copies, waits for them, and re-layouts  1.14 us (2%)
    pallas_call x4, Pallas kernels, blur(): call(functools.partial(main_kernel, part, len(making) - 2 if making else...  15 us
    ppermute x10, starting transfers between devices, swap(): return lax.ppermute(cells, axis, pairs + [(j, i) for i, j in pairs])  8.86 us
    pallas_call x4, Pallas kernels, blur(): call(functools.partial(edge_kernel, part), outs, [SMEM] + [VMEM] * (7 + l...  7.83 us
    ppermute x4, starting transfers between devices, exchanged(): lax.ppermute(jnp.where(even, to_left, to_right), ('row', 'col'), outer_co...  7.65 us
    ppermute x3, starting transfers between devices, shards(): lax.ppermute(bank, 'col', [(i, i ^ s) for i in range(n_col)])  5.76 us
    ppermute x4, waiting for transfers between devices, exchanged(): lax.ppermute(jnp.where(even, to_left, to_right), ('row', 'col'), outer_co...  5.02 us
    ppermute x2, starting transfers between devices, shards(): lax.ppermute(plane, 'row', [(i, i ^ s) for i in range(n_row)])  2.77 us
    pallas_call x1, Pallas kernels, bands(): call(functools.partial(bands_kernel, part, n_row), outs, [SMEM] + [VMEM]...  2.33 us
  transfers between devices with their start and end apart: 23, of which 6 were waited for; matrix products, arithmetic and copies ran while one was open for 0% of the time, Pallas kernels for 35%

profile of v5, /device:TPU:0, one launch (start us, length us, event | category | flops | bytes accessed | tf_op | source)
XLA Modules:
  0.0 60.0 jit_solution(9875952019304154335)
XLA Ops:
  0.0 0.9 %copy-done.5 = f32[4,16,2,4,33]{4,3,2,1,0:T(4,128)S(1)} copy-done((f32[4,16,2,4,33]{4,3,2,1,0:T(4,128)S(1)}, f32[4,16,2,4,33]{4,3,2,1,0:T(4,128)}, u32[]{:S(2)}) %copy-start.5) | copy-done | bytes 67608
  1.0 0.1 bank.1.refs_0_
  1.1 0.0 copy-start.4
  1.1 5.1 %collective-permute-start.3 = (bf16[48,512]{1,0:T(8,128)(2,1)S(1)}, bf16[48,512]{1,0:T(8,128)(2,1)S(1)}, u32[]{:S(2)}, u32[]{:S(2)}) collective-permute-start(bf16[48,512]{1,0:T(8,128)(2,1)S(1)} %bank.1.refs_0_), channel_id=1, source_target_pairs={{0,6},{1,7},{2,4},{3,5},{4,2},{5,3},{6,0},{7,1},{8,14},{9,15},{10,... | collective-permute-start | bytes 147464 | tf_op jit(solution)/shard_map/ppermute | solution.py:457
  6.2 0.0 collective-permute-start.2
  6.2 0.6 %collective-permute-start.1 = (bf16[48,512]{1,0:T(8,128)(2,1)S(1)}, bf16[48,512]{1,0:T(8,128)(2,1)S(1)}, u32[]{:S(2)}, u32[]{:S(2)}) collective-permute-start(bf16[48,512]{1,0:T(8,128)(2,1)S(1)} %bank.1.refs_0_), channel_id=1, source_target_pairs={{0,2},{1,3},{2,0},{3,1},{4,6},{5,7},{6,4},{7,5},{8,10},{9,11},{10,... | collective-permute-start | bytes 147464 | tf_op jit(solution)/shard_map/ppermute | solution.py:457
  6.8 0.0 copy-done.1
  6.8 0.2 keys.1
  7.0 0.0 collective-permute-start
  7.0 0.4 first.1
  7.5 0.6 collective-permute-start.6
  8.0 0.1 collective-permute-done.other_ref
  8.1 1.6 %collective-permute-start.5 = (bf16[2,128,128]{2,1,0:T(8,128)(2,1)S(1)}, bf16[2,128,128]{2,1,0:T(8,128)(2,1)S(1)}, u32[]{:S(2)}, u32[]{:S(2)}) collective-permute-start(bf16[2,128,128]{2,1,0:T(8,128)(2,1)S(1)} %get-tuple-element.128), channel_id=1, source_target_pairs={{0,8},{1,2},{2,1},{3,4},{4,3},{5,6},{6,5},{7,15},{8,0},{9,10},{10,... | collective-permute-start | bytes 196616 | tf_op jit(solution)/shard_map/ppermute | solution.py:444
  9.8 0.1 stack.43.meta_ref
  9.9 0.0 collective-permute-done.3.refs_3_
  9.9 1.5 %collective-permute-start.10 = (bf16[3,16,128]{2,1,0:T(8,128)(2,1)S(1)}, bf16[3,16,128]{2,1,0:T(8,128)(2,1)S(1)}, u32[]{:S(2)}, u32[]{:S(2)}) collective-permute-start(bf16[3,16,128]{2,1,0:T(8,128)(2,1)S(1)} %get-tuple-element.56.refs_1_), channel_id=1, source_target_pairs={{0,24},{8,16},{16,8},{24,0},{1,25},{9,17},{17,9},{25,1},{2,26},{10... | collective-permute-start | bytes 36872 | tf_op jit(solution)/shard_map/ppermute | solution.py:537
  11.4 0.0 collective-permute-done.2.refs_2_
  11.4 1.3 %collective-permute-start.9 = (bf16[3,16,128]{2,1,0:T(8,128)(2,1)S(1)}, bf16[3,16,128]{2,1,0:T(8,128)(2,1)S(1)}, u32[]{:S(2)}, u32[]{:S(2)}) collective-permute-start(bf16[3,16,128]{2,1,0:T(8,128)(2,1)S(1)} %get-tuple-element.56.refs_1_), channel_id=1, source_target_pairs={{0,16},{8,24},{16,0},{24,8},{1,17},{9,25},{17,1},{25,9},{2,18},{10... | collective-permute-start | bytes 36872 | tf_op jit(solution)/shard_map/ppermute | solution.py:537
  12.7 0.0 collective-permute-done.1.refs_1_
  12.7 0.7 %pick.1 = (bf16[2,48,128]{2,1,0:T(8,128)(2,1)S(1)}, bf16[2,48,128]{2,1,0:T(8,128)(2,1)S(1)}) custom-call(s32[6]{0:T(128)S(1)} %stack.43.meta_ref, f32[4,128]{1,0:T(4,128)S(1)} %get-tuple-element.47.mine_ref.keys_ref, f32[4,128]{1,0:T(4,128)S(1)} %collective-permute-done.other_ref, bf16[48,512]{1,0:T(8,128)(2,1)S(1)} %bank.1.refs_0_, ...), custom_call_target="tpu_custom_call" | custom-call | bytes 1048576 | tf_op jit(solution)/shard_map/pick/pallas_call | solution.py:471
  13.4 0.1 collective-permute-start.4
  13.5 0.0 collective-permute-done.6
  13.5 0.0 collective-permute-done.5
  13.6 1.6 %collective-permute-start.8 = (bf16[23,16,128]{2,1,0:T(8,128)(2,1)S(1)}, bf16[23,16,128]{2,1,0:T(8,128)(2,1)S(1)}, u32[]{:S(2)}, u32[]{:S(2)}) collective-permute-start(bf16[23,16,128]{2,1,0:T(8,128)(2,1)S(1)} %get-tuple-element.99), channel_id=1, source_target_pairs={{0,8},{16,24},{8,0},{24,16},{1,9},{17,25},{9,1},{25,17},{2,10},{18... | collective-permute-start | bytes 282632 | tf_op jit(solution)/shard_map/ppermute | solution.py:51
  15.1 0.2 collective-permute-start.7
  15.3 0.0 collective-permute-done.4.other_ref
  15.3 0.5 taps.1.ct_ref.rt_ref.uv_ref
  15.9 5.3 %main.4 = (f32[16,32,128]{2,1,0:T(8,128)S(1)}, bf16[16,128,128]{2,1,0:T(8,128)(2,1)S(1)}, bf16[2,128,128]{2,1,0:T(8,128)(2,1)S(1)}, bf16[2,128,128]{2,1,0:T(8,12...) custom-call(s32[6]{0:T(128)S(1)} %stack.43.meta_ref, ...), custom_call_target="tpu_custom_call" | custom-call | flops 4000000000 | bytes 1048576 | tf_op jit(solution)/shard_map/main/pallas_call | solution.py:513
  21.2 0.0 collective-permute-done.8
  21.2 0.0 collective-permute-done.7
  21.2 1.7 %edge.4 = (bf16[16,128,128]{2,1,0:T(8,128)(2,1)S(1)}, bf16[2,128,128]{2,1,0:T(8,128)(2,1)S(1)}, bf16[2,128,128]{2,1,0:T(8,128)(2,1)S(1)}) custom-call(s32[6]{0:T(128)S(1)} %stack.43.meta_ref, bf16[16,128,512]{2,1,0:T(8,128)(2,1)S(1)} %get-tuple-element.53.cw_ref, bf16[16,32,256]{2,1,0:T(8,128)(2,1)S(1)} %get-tuple-element.54.edge_ref, ...), custom_call_target="tpu_custom_call" | custom-call | flops 2000000000 | bytes 1048576 | tf_op jit(solution)/shard_map/edge/pallas_call | solution.py:526
  22.9 0.4 collective-permute-start.12
  23.3 1.8 %collective-permute-start.11 = (bf16[2,128,128]{2,1,0:T(8,128)(2,1)S(1)}, bf16[2,128,128]{2,1,0:T(8,128)(2,1)S(1)}, u32[]{:S(2)}, u32[]{:S(2)}) collective-permute-start(bf16[2,128,128]{2,1,0:T(8,128)(2,1)S(1)} %get-tuple-element.124), channel_id=1, source_target_pairs={{0,8},{1,2},{2,1},{3,4},{4,3},{5,6},{6,5},{7,15},{8,0},{9,10},{10,... | collective-permute-start | bytes 196616 | tf_op jit(solution)/shard_map/ppermute | solution.py:444
  25.1 0.0 collective-permute-done.10.refs_4_
  25.1 0.0 collective-permute-done.9.refs_3_
  25.1 2.3 %bands.1 = (bf16[16,256,1024]{2,1,0:T(8,128)(2,1)S(1)}, f32[2,128,8]{2,1,0:T(8,128)S(1)}) custom-call(s32[6]{0:T(128)S(1)} %stack.43.meta_ref, f32[2,16,8,256]{3,2,1,0:T(8,128)S(1)} %taps.1.ct_ref.rt_ref.uv_ref, f32[4,64,128]{2,1,0:T(8,128)S(1)} %copy-done.6, bf16[3,16,128]{2,1,0:T(8,128)(2,1)S(1)} %get-tuple-element.56.refs_1_, ...), custom_call_target="tpu_custom_call" | custom-call | flops 4000000000 | bytes 1048576 | tf_op jit(solution)/shard_map/bands/pallas_call | solution.py:493
  27.5 0.0 collective-permute-done.12
  27.5 0.1 collective-permute-done.11
  27.6 1.9 %collective-permute-start.14 = (bf16[20,16,128]{2,1,0:T(8,128)(2,1)S(1)}, bf16[20,16,128]{2,1,0:T(8,128)(2,1)S(1)}, u32[]{:S(2)}, u32[]{:S(2)}) collective-permute-start(bf16[20,16,128]{2,1,0:T(8,128)(2,1)S(1)} %get-tuple-element.111), channel_id=1, source_target_pairs={{0,8},{16,24},{8,0},{24,16},{1,9},{17,25},{9,1},{25,17},{2,10},{18... | collective-permute-start | bytes 245768 | tf_op jit(solution)/shard_map/ppermute | solution.py:51
  29.5 0.0 collective-permute-start.13
  29.5 3.7 %main.5 = (f32[16,32,128]{2,1,0:T(8,128)S(1)}, f32[16,128,128]{2,1,0:T(8,128)S(1)}, bf16[16,128,128]{2,1,0:T(8,128)(2,1)S(1)}, bf16[2,128,128]{2,1,0:T(8,128)(2,...) custom-call(s32[6]{0:T(128)S(1)} %stack.43.meta_ref, ...), custom_call_target="tpu_custom_call" | custom-call | flops 4000000000 | bytes 1048576 | tf_op jit(solution)/shard_map/main/pallas_call | solution.py:513
  33.2 0.0 collective-permute-done.14
  33.2 0.0 collective-permute-done.13
  33.3 2.0 %edge.5 = (f32[16,128,128]{2,1,0:T(8,128)S(1)}, bf16[16,128,128]{2,1,0:T(8,128)(2,1)S(1)}, bf16[2,128,128]{2,1,0:T(8,128)(2,1)S(1)}, bf16[2,128,128]{2,1,0:T(8,128)(2,1)S(1)}) custom-call(s32[6]{0:T(128)S(1)} %stack.43.meta_ref, bf16[16,128,512]{2,1,0:T(8,128)(2,1)S(1)} %get-tuple-element.66.cw_ref, bf16[16,32,256]{2,1,0:T(8,128)(2,1)S(1)} %get-tuple-element.67.edge_ref, ...), custom_call_target="tpu_custom_call" | custom-call | flops 2000000000 | bytes 1048576 | tf_op jit(solution)/shard_map/edge/pallas_call | solution.py:526
  35.3 0.6 collective-permute-start.16
  35.9 1.5 %collective-permute-start.15 = (bf16[2,128,128]{2,1,0:T(8,128)(2,1)S(1)}, bf16[2,128,128]{2,1,0:T(8,128)(2,1)S(1)}, u32[]{:S(2)}, u32[]{:S(2)}) collective-permute-start(bf16[2,128,128]{2,1,0:T(8,128)(2,1)S(1)} %get-tuple-element.120), channel_id=1, source_target_pairs={{0,8},{1,2},{2,1},{3,4},{4,3},{5,6},{6,5},{7,15},{8,0},{9,10},{10,... | collective-permute-start | bytes 196616 | tf_op jit(solution)/shard_map/ppermute | solution.py:444
  37.4 0.0 collective-permute-done.16
  37.4 2.7 %collective-permute-done.15 = bf16[2,128,128]{2,1,0:T(8,128)(2,1)S(1)} collective-permute-done((bf16[2,128,128]{2,1,0:T(8,128)(2,1)S(1)}, bf16[2,128,128]{2,1,0:T(8,128)(2,1)S(1)}, u32[]{:S(2)}, u32[]{:S(2)}) %collective-permute-start.15) | collective-permute-done | bytes 65568 | tf_op jit(solution)/shard_map/ppermute | solution.py:444
  40.2 1.6 %collective-permute-start.18 = (bf16[20,16,128]{2,1,0:T(8,128)(2,1)S(1)}, bf16[20,16,128]{2,1,0:T(8,128)(2,1)S(1)}, u32[]{:S(2)}, u32[]{:S(2)}) collective-permute-start(bf16[20,16,128]{2,1,0:T(8,128)(2,1)S(1)} %get-tuple-element.107), channel_id=1, source_target_pairs={{0,8},{16,24},{8,0},{24,16},{1,9},{17,25},{9,1},{25,17},{2,10},{18... | collective-permute-start | bytes 245768 | tf_op jit(solution)/shard_map/ppermute | solution.py:51
  41.8 0.0 collective-permute-start.17
  41.8 3.0 %main.6 = (f32[16,32,128]{2,1,0:T(8,128)S(1)}, bf16[16,128,128]{2,1,0:T(8,128)(2,1)S(1)}, bf16[2,128,128]{2,1,0:T(8,128)(2,1)S(1)}, bf16[2,128,128]{2,1,0:T(8,128)(2,1)S(1)}) custom-call(s32[6]{0:T(128)S(1)} %stack.43.meta_ref, bf16[16,256,1024]{2,1,0:T(8,128)(2,1)S(1)} %get-tuple-element.69.ct_ref, bf16[16,128,1024]{2,1,0:T(8,128)(2,1)S(1)} %get-tuple-element.70.rt_ref, ...), custom_call_target="tpu_custom_call" | custom-call | flops 4000000000 | bytes 1048576 | tf_op jit(solution)/shard_map/main/pallas_call | solution.py:513
  44.9 0.4 collective-permute-done.18
  45.3 0.0 collective-permute-done.17
  45.3 1.6 %edge.6 = (bf16[16,128,128]{2,1,0:T(8,128)(2,1)S(1)}, bf16[2,128,128]{2,1,0:T(8,128)(2,1)S(1)}, bf16[2,128,128]{2,1,0:T(8,128)(2,1)S(1)}) custom-call(s32[6]{0:T(128)S(1)} %stack.43.meta_ref, bf16[16,128,512]{2,1,0:T(8,128)(2,1)S(1)} %get-tuple-element.53.cw_ref, bf16[16,32,256]{2,1,0:T(8,128)(2,1)S(1)} %get-tuple-element.54.edge_ref, ...), custom_call_target="tpu_custom_call" | custom-call | flops 2000000000 | bytes 1048576 | tf_op jit(solution)/shard_map/edge/pallas_call | solution.py:526
  47.0 0.2 collective-permute-start.20
  47.1 2.7 %collective-permute-start.19 = (bf16[2,128,128]{2,1,0:T(8,128)(2,1)S(1)}, bf16[2,128,128]{2,1,0:T(8,128)(2,1)S(1)}, u32[]{:S(2)}, u32[]{:S(2)}) collective-permute-start(bf16[2,128,128]{2,1,0:T(8,128)(2,1)S(1)} %get-tuple-element.116), channel_id=1, source_target_pairs={{0,8},{1,2},{2,1},{3,4},{4,3},{5,6},{6,5},{7,15},{8,0},{9,10},{10,... | collective-permute-start | bytes 196616 | tf_op jit(solution)/shard_map/ppermute | solution.py:444
  49.8 0.0 collective-permute-done.20
  49.9 2.2 %collective-permute-done.19 = bf16[2,128,128]{2,1,0:T(8,128)(2,1)S(1)} collective-permute-done((bf16[2,128,128]{2,1,0:T(8,128)(2,1)S(1)}, bf16[2,128,128]{2,1,0:T(8,128)(2,1)S(1)}, u32[]{:S(2)}, u32[]{:S(2)}) %collective-permute-start.19) | collective-permute-done | bytes 65568 | tf_op jit(solution)/shard_map/ppermute | solution.py:444
  52.2 2.1 %collective-permute-start.22 = (bf16[20,16,128]{2,1,0:T(8,128)(2,1)S(1)}, bf16[20,16,128]{2,1,0:T(8,128)(2,1)S(1)}, u32[]{:S(2)}, u32[]{:S(2)}) collective-permute-start(bf16[20,16,128]{2,1,0:T(8,128)(2,1)S(1)} %get-tuple-element.103), channel_id=1, source_target_pairs={{0,8},{16,24},{8,0},{24,16},{1,9},{17,25},{9,1},{25,17},{2,10},{18... | collective-permute-start | bytes 245768 | tf_op jit(solution)/shard_map/ppermute | solution.py:51
  54.2 0.0 collective-permute-start.21
  54.2 2.9 %main.7 = (f32[16,32,128]{2,1,0:T(8,128)S(1)}, f32[16,128,128]{2,1,0:T(8,128)S(1)}) custom-call(s32[6]{0:T(128)S(1)} %stack.43.meta_ref, bf16[16,256,1024]{2,1,0:T(8,128)(2,1)S(1)} %get-tuple-element.62.ct_ref, bf16[16,128,1024]{2,1,0:T(8,128)(2,1)S(1)} %get-tuple-element.68.rt_ref, bf16[16,128,128]{2,1,0:T(8,128)(2,1)S(1)} %get-tuple-element.83.field_ref, ...), custom_call_target="tpu_custom_call" | custom-call | flops 4000000000 | bytes 1048576 | tf_op jit(solution)/shard_map/main/pallas_call | solution.py:513
  57.2 0.3 collective-permute-done.22
  57.5 0.0 collective-permute-done.21
  57.5 2.5 %edge.7 = f32[16,128,128]{2,1,0:T(8,128)} custom-call(s32[6]{0:T(128)S(1)} %stack.43.meta_ref, bf16[16,128,512]{2,1,0:T(8,128)(2,1)S(1)} %get-tuple-element.66.cw_ref, bf16[16,32,256]{2,1,0:T(8,128)(2,1)S(1)} %get-tuple-element.67.edge_ref, f32[16,32,128]{2,1,0:T(8,128)S(1)} %get-tuple-element.87.rim_ref, ...), custom_call_target="tpu_custom_call" | custom-call | flops 2000000000 | bytes 1048576 | tf_op jit(solution)/shard_map/edge/pallas_call | solution.py:526
  (40 shorter events, 0.4 us)
Async XLA Ops:
  0.0 0.9 %copy-start.5 = (f32[4,16,2,4,33]{4,3,2,1,0:T(4,128)S(1)}, f32[4,16,2,4,33]{4,3,2,1,0:T(4,128)}, u32[]{:S(2)}) copy-start(f32[4,16,2,4,33]{4,3,2,1,0:T(4,128)} %param.9) | copy-start | bytes 202756
  1.0 5.9 %copy-start = (f32[16,16,1]{1,2,0:T(1,128)S(1)}, f32[16,16,1]{1,2,0:T(1,128)}, u32[]{:S(2)}) copy-start(f32[16,16,1]{1,2,0:T(1,128)} %param.12) | copy-start | bytes 3076
  1.0 5.9 %copy-start.1 = (s32[1,1,16,2]{2,3,1,0:T(2,128)S(1)}, s32[1,1,16,2]{2,3,1,0:T(2,128)}, u32[]{:S(2)}) copy-start(s32[1,1,16,2]{2,3,1,0:T(2,128)} %param.10) | copy-start | bytes 388
  1.0 5.9 %copy-start.2 = (f32[1,1,16,2]{2,3,1,0:T(2,128)S(1)}, f32[1,1,16,2]{2,3,1,0:T(2,128)}, u32[]{:S(2)}) copy-start(f32[1,1,16,2]{2,3,1,0:T(2,128)} %param.11) | copy-start | bytes 388
  1.0 6.0 %copy-start.3 = (f32[16,128,128]{2,1,0:T(8,128)S(1)}, f32[16,128,128]{2,1,0:T(8,128)}, u32[]{:S(2)}) copy-start(f32[16,128,128]{2,1,0:T(8,128)} %a_ref.9) | copy-start | bytes 3145732
  1.1 14.8 %copy-start.4 = (f32[16,128,128]{2,1,0:T(8,128)S(1)}, f32[16,128,128]{2,1,0:T(8,128)}, u32[]{:S(2)}) copy-start(f32[16,128,128]{2,1,0:T(8,128)} %a_ref.11) | copy-start | bytes 3145732
  1.1 8.8 %collective-permute-start.3 = (bf16[48,512]{1,0:T(8,128)(2,1)S(1)}, bf16[48,512]{1,0:T(8,128)(2,1)S(1)}, u32[]{:S(2)}, u32[]{:S(2)}) collective-permute-start(bf16[48,512]{1,0:T(8,128)(2,1)S(1)} %bank.1.refs_0_), channel_id=1, source_target_pairs={{0,6},{1,7},{2,4},{3,5},{4,2},{5,3},{6,0},{7,1},{8,14},{9,15},{10,... | collective-permute-start | bytes 147464 | tf_op jit(solution)/shard_map/ppermute | solution.py:457
  6.2 5.3 %collective-permute-start.2 = (bf16[48,512]{1,0:T(8,128)(2,1)S(1)}, bf16[48,512]{1,0:T(8,128)(2,1)S(1)}, u32[]{:S(2)}, u32[]{:S(2)}) collective-permute-start(bf16[48,512]{1,0:T(8,128)(2,1)S(1)} %bank.1.refs_0_), channel_id=1, source_target_pairs={{0,4},{1,5},{2,6},{3,7},{4,0},{5,1},{6,2},{7,3},{8,12},{9,13},{10,... | collective-permute-start | bytes 147464 | tf_op jit(solution)/shard_map/ppermute | solution.py:457
  6.2 6.5 %collective-permute-start.1 = (bf16[48,512]{1,0:T(8,128)(2,1)S(1)}, bf16[48,512]{1,0:T(8,128)(2,1)S(1)}, u32[]{:S(2)}, u32[]{:S(2)}) collective-permute-start(bf16[48,512]{1,0:T(8,128)(2,1)S(1)} %bank.1.refs_0_), channel_id=1, source_target_pairs={{0,2},{1,3},{2,0},{3,1},{4,6},{5,7},{6,4},{7,5},{8,10},{9,11},{10,... | collective-permute-start | bytes 147464 | tf_op jit(solution)/shard_map/ppermute | solution.py:457
  7.0 1.2 %collective-permute-start = (f32[4,128]{1,0:T(4,128)S(1)}, f32[4,128]{1,0:T(4,128)S(1)}, u32[]{:S(2)}, u32[]{:S(2)}) collective-permute-start(f32[4,128]{1,0:T(4,128)S(1)} %get-tuple-element.47.mine_ref.keys_ref), channel_id=1, source_target_pairs={{0,1},{2,3},{4,5},{6,7},{1,0},{3,2},{5,4},{7,6},{8,9},{10,11},{12,... | collective-permute-start | bytes 6152 | tf_op jit(solution)/shard_map/ppermute | solution.py:51
  7.5 6.0 %collective-permute-start.6 = (bf16[2,128,128]{2,1,0:T(8,128)(2,1)S(1)}, bf16[2,128,128]{2,1,0:T(8,128)(2,1)S(1)}, u32[]{:S(2)}, u32[]{:S(2)}) collective-permute-start(bf16[2,128,128]{2,1,0:T(8,128)(2,1)S(1)} %get-tuple-element.127), channel_id=1, source_target_pairs={{0,1},{2,3},{4,5},{6,7},{1,0},{3,2},{5,4},{7,6},{8,9},{10,11},{12,... | collective-permute-start | bytes 196616 | tf_op jit(solution)/shard_map/ppermute | solution.py:51
  8.1 5.3 %collective-permute-start.5 = (bf16[2,128,128]{2,1,0:T(8,128)(2,1)S(1)}, bf16[2,128,128]{2,1,0:T(8,128)(2,1)S(1)}, u32[]{:S(2)}, u32[]{:S(2)}) collective-permute-start(bf16[2,128,128]{2,1,0:T(8,128)(2,1)S(1)} %get-tuple-element.128), channel_id=1, source_target_pairs={{0,8},{1,2},{2,1},{3,4},{4,3},{5,6},{6,5},{7,15},{8,0},{9,10},{10,... | collective-permute-start | bytes 196616 | tf_op jit(solution)/shard_map/ppermute | solution.py:444
  9.9 15.2 %collective-permute-start.10 = (bf16[3,16,128]{2,1,0:T(8,128)(2,1)S(1)}, bf16[3,16,128]{2,1,0:T(8,128)(2,1)S(1)}, u32[]{:S(2)}, u32[]{:S(2)}) collective-permute-start(bf16[3,16,128]{2,1,0:T(8,128)(2,1)S(1)} %get-tuple-element.56.refs_1_), channel_id=1, source_target_pairs={{0,24},{8,16},{16,8},{24,0},{1,25},{9,17},{17,9},{25,1},{2,26},{10... | collective-permute-start | bytes 36872 | tf_op jit(solution)/shard_map/ppermute | solution.py:537
  11.4 13.7 %collective-permute-start.9 = (bf16[3,16,128]{2,1,0:T(8,128)(2,1)S(1)}, bf16[3,16,128]{2,1,0:T(8,128)(2,1)S(1)}, u32[]{:S(2)}, u32[]{:S(2)}) collective-permute-start(bf16[3,16,128]{2,1,0:T(8,128)(2,1)S(1)} %get-tuple-element.56.refs_1_), channel_id=1, source_target_pairs={{0,16},{8,24},{16,0},{24,8},{1,17},{9,25},{17,1},{25,9},{2,18},{10... | collective-permute-start | bytes 36872 | tf_op jit(solution)/shard_map/ppermute | solution.py:537
  13.4 1.9 %collective-permute-start.4 = (bf16[2,48,128]{2,1,0:T(8,128)(2,1)S(1)}, bf16[2,48,128]{2,1,0:T(8,128)(2,1)S(1)}, u32[]{:S(2)}, u32[]{:S(2)}) collective-permute-start(bf16[2,48,128]{2,1,0:T(8,128)(2,1)S(1)} %get-tuple-element.49), channel_id=1, source_target_pairs={{0,1},{2,3},{4,5},{6,7},{1,0},{3,2},{5,4},{7,6},{8,9},{10,11},{12,... | collective-permute-start | bytes 73736 | tf_op jit(solution)/shard_map/ppermute | solution.py:51
  13.6 7.6 %collective-permute-start.8 = (bf16[23,16,128]{2,1,0:T(8,128)(2,1)S(1)}, bf16[23,16,128]{2,1,0:T(8,128)(2,1)S(1)}, u32[]{:S(2)}, u32[]{:S(2)}) collective-permute-start(bf16[23,16,128]{2,1,0:T(8,128)(2,1)S(1)} %get-tuple-element.99), channel_id=1, source_target_pairs={{0,8},{16,24},{8,0},{24,16},{1,9},{17,25},{9,1},{25,17},{2,10},{18... | collective-permute-start | bytes 282632 | tf_op jit(solution)/shard_map/ppermute | solution.py:51
  15.1 6.1 %collective-permute-start.7 = (bf16[23,16,128]{2,1,0:T(8,128)(2,1)S(1)}, bf16[23,16,128]{2,1,0:T(8,128)(2,1)S(1)}, u32[]{:S(2)}, u32[]{:S(2)}) collective-permute-start(bf16[23,16,128]{2,1,0:T(8,128)(2,1)S(1)} %get-tuple-element.100), channel_id=1, source_target_pairs={{0,1},{1,0},{2,3},{3,2},{4,5},{5,4},{6,7},{7,6},{8,16},{9,17},{10,... | collective-permute-start | bytes 282632 | tf_op jit(solution)/shard_map/ppermute | solution.py:508
  21.2 3.9 %copy-start.6 = (f32[4,64,128]{2,1,0:T(8,128)S(1)}, f32[4,64,128]{2,1,0:T(8,128)}, u32[]{:S(2)}) copy-start(f32[4,64,128]{2,1,0:T(8,128)} %constant.46.clone.refs_0_) | copy-start | bytes 393220
  22.9 4.6 %collective-permute-start.12 = (bf16[2,128,128]{2,1,0:T(8,128)(2,1)S(1)}, bf16[2,128,128]{2,1,0:T(8,128)(2,1)S(1)}, u32[]{:S(2)}, u32[]{:S(2)}) collective-permute-start(bf16[2,128,128]{2,1,0:T(8,128)(2,1)S(1)} %get-tuple-element.123), channel_id=1, source_target_pairs={{0,1},{2,3},{4,5},{6,7},{1,0},{3,2},{5,4},{7,6},{8,9},{10,11},{12,... | collective-permute-start | bytes 196616 | tf_op jit(solution)/shard_map/ppermute | solution.py:51
  23.3 4.3 %collective-permute-start.11 = (bf16[2,128,128]{2,1,0:T(8,128)(2,1)S(1)}, bf16[2,128,128]{2,1,0:T(8,128)(2,1)S(1)}, u32[]{:S(2)}, u32[]{:S(2)}) collective-permute-start(bf16[2,128,128]{2,1,0:T(8,128)(2,1)S(1)} %get-tuple-element.124), channel_id=1, source_target_pairs={{0,8},{1,2},{2,1},{3,4},{4,3},{5,6},{6,5},{7,15},{8,0},{9,10},{10,... | collective-permute-start | bytes 196616 | tf_op jit(solution)/shard_map/ppermute | solution.py:444
  27.6 5.6 %collective-permute-start.14 = (bf16[20,16,128]{2,1,0:T(8,128)(2,1)S(1)}, bf16[20,16,128]{2,1,0:T(8,128)(2,1)S(1)}, u32[]{:S(2)}, u32[]{:S(2)}) collective-permute-start(bf16[20,16,128]{2,1,0:T(8,128)(2,1)S(1)} %get-tuple-element.111), channel_id=1, source_target_pairs={{0,8},{16,24},{8,0},{24,16},{1,9},{17,25},{9,1},{25,17},{2,10},{18... | collective-permute-start | bytes 245768 | tf_op jit(solution)/shard_map/ppermute | solution.py:51
  29.5 3.7 %collective-permute-start.13 = (bf16[20,16,128]{2,1,0:T(8,128)(2,1)S(1)}, bf16[20,16,128]{2,1,0:T(8,128)(2,1)S(1)}, u32[]{:S(2)}, u32[]{:S(2)}) collective-permute-start(bf16[20,16,128]{2,1,0:T(8,128)(2,1)S(1)} %get-tuple-element.112), channel_id=1, source_target_pairs={{0,1},{1,0},{2,3},{3,2},{4,5},{5,4},{6,7},{7,6},{8,16},{9,17},{10,... | collective-permute-start | bytes 245768 | tf_op jit(solution)/shard_map/ppermute | solution.py:508
  35.3 2.1 %collective-permute-start.16 = (bf16[2,128,128]{2,1,0:T(8,128)(2,1)S(1)}, bf16[2,128,128]{2,1,0:T(8,128)(2,1)S(1)}, u32[]{:S(2)}, u32[]{:S(2)}) collective-permute-start(bf16[2,128,128]{2,1,0:T(8,128)(2,1)S(1)} %get-tuple-element.119), channel_id=1, source_target_pairs={{0,1},{2,3},{4,5},{6,7},{1,0},{3,2},{5,4},{7,6},{8,9},{10,11},{12,... | collective-permute-start | bytes 196616 | tf_op jit(solution)/shard_map/ppermute | solution.py:51
  35.9 4.3 %collective-permute-start.15 = (bf16[2,128,128]{2,1,0:T(8,128)(2,1)S(1)}, bf16[2,128,128]{2,1,0:T(8,128)(2,1)S(1)}, u32[]{:S(2)}, u32[]{:S(2)}) collective-permute-start(bf16[2,128,128]{2,1,0:T(8,128)(2,1)S(1)} %get-tuple-element.120), channel_id=1, source_target_pairs={{0,8},{1,2},{2,1},{3,4},{4,3},{5,6},{6,5},{7,15},{8,0},{9,10},{10,... | collective-permute-start | bytes 196616 | tf_op jit(solution)/shard_map/ppermute | solution.py:444
  40.2 5.0 %collective-permute-start.18 = (bf16[20,16,128]{2,1,0:T(8,128)(2,1)S(1)}, bf16[20,16,128]{2,1,0:T(8,128)(2,1)S(1)}, u32[]{:S(2)}, u32[]{:S(2)}) collective-permute-start(bf16[20,16,128]{2,1,0:T(8,128)(2,1)S(1)} %get-tuple-element.107), channel_id=1, source_target_pairs={{0,8},{16,24},{8,0},{24,16},{1,9},{17,25},{9,1},{25,17},{2,10},{18... | collective-permute-start | bytes 245768 | tf_op jit(solution)/shard_map/ppermute | solution.py:51
  41.8 3.5 %collective-permute-start.17 = (bf16[20,16,128]{2,1,0:T(8,128)(2,1)S(1)}, bf16[20,16,128]{2,1,0:T(8,128)(2,1)S(1)}, u32[]{:S(2)}, u32[]{:S(2)}) collective-permute-start(bf16[20,16,128]{2,1,0:T(8,128)(2,1)S(1)} %get-tuple-element.108), channel_id=1, source_target_pairs={{0,1},{1,0},{2,3},{3,2},{4,5},{5,4},{6,7},{7,6},{8,16},{9,17},{10,... | collective-permute-start | bytes 245768 | tf_op jit(solution)/shard_map/ppermute | solution.py:508
  47.0 2.9 %collective-permute-start.20 = (bf16[2,128,128]{2,1,0:T(8,128)(2,1)S(1)}, bf16[2,128,128]{2,1,0:T(8,128)(2,1)S(1)}, u32[]{:S(2)}, u32[]{:S(2)}) collective-permute-start(bf16[2,128,128]{2,1,0:T(8,128)(2,1)S(1)} %get-tuple-element.115), channel_id=1, source_target_pairs={{0,1},{2,3},{4,5},{6,7},{1,0},{3,2},{5,4},{7,6},{8,9},{10,11},{12,... | collective-permute-start | bytes 196616 | tf_op jit(solution)/shard_map/ppermute | solution.py:51
  47.1 4.9 %collective-permute-start.19 = (bf16[2,128,128]{2,1,0:T(8,128)(2,1)S(1)}, bf16[2,128,128]{2,1,0:T(8,128)(2,1)S(1)}, u32[]{:S(2)}, u32[]{:S(2)}) collective-permute-start(bf16[2,128,128]{2,1,0:T(8,128)(2,1)S(1)} %get-tuple-element.116), channel_id=1, source_target_pairs={{0,8},{1,2},{2,1},{3,4},{4,3},{5,6},{6,5},{7,15},{8,0},{9,10},{10,... | collective-permute-start | bytes 196616 | tf_op jit(solution)/shard_map/ppermute | solution.py:444
  52.2 5.3 %collective-permute-start.22 = (bf16[20,16,128]{2,1,0:T(8,128)(2,1)S(1)}, bf16[20,16,128]{2,1,0:T(8,128)(2,1)S(1)}, u32[]{:S(2)}, u32[]{:S(2)}) collective-permute-start(bf16[20,16,128]{2,1,0:T(8,128)(2,1)S(1)} %get-tuple-element.103), channel_id=1, source_target_pairs={{0,8},{16,24},{8,0},{24,16},{1,9},{17,25},{9,1},{25,17},{2,10},{18... | collective-permute-start | bytes 245768 | tf_op jit(solution)/shard_map/ppermute | solution.py:51
  54.2 3.2 %collective-permute-start.21 = (bf16[20,16,128]{2,1,0:T(8,128)(2,1)S(1)}, bf16[20,16,128]{2,1,0:T(8,128)(2,1)S(1)}, u32[]{:S(2)}, u32[]{:S(2)}) collective-permute-start(bf16[20,16,128]{2,1,0:T(8,128)(2,1)S(1)} %get-tuple-element.104), channel_id=1, source_target_pairs={{0,1},{1,0},{2,3},{3,2},{4,5},{5,4},{6,7},{7,6},{8,16},{9,17},{10,... | collective-permute-start | bytes 245768 | tf_op jit(solution)/shard_map/ppermute | solution.py:508

commit v6 on v5

--- a/solution.py
+++ b/solution.py
@@ -29,14 +29,14 @@
     return lax.broadcasted_iota(jnp.int32, shape, len(shape) - 2)
 
 
-def call(body, outs, specs, scratch=(), name=None, flops=0, mib=16):
+def call(body, outs, specs, scratch=(), name=None, flops=0, to=VMEM):
     return pl.pallas_call(
         body,
         out_shape=outs,
         in_specs=specs,
-        out_specs=jax.tree.map(lambda _: VMEM, outs),
+        out_specs=jax.tree.map(lambda _: to, outs),
         scratch_shapes=list(scratch),
-        compiler_params=pltpu.CompilerParams(vmem_limit_bytes=mib * 1024 * 1024),
+        compiler_params=pltpu.CompilerParams(vmem_limit_bytes=16 * 1024 * 1024),
         cost_estimate=pl.CostEstimate(flops=flops, bytes_accessed=1 << 20, transcendentals=0),
         name=name,
     )
@@ -347,9 +347,14 @@
                 do(i)
 
 
-def edge_kernel(part, meta_ref, cw_ref, edge_ref, rim_ref, top_ref, bot_ref, a_ref, inv_ref, *refs):
-    count = len(refs) // 2
-    made, outs, q_ref = refs[:count], refs[count:-1], refs[-1]
+def edge_kernel(part, last, meta_ref, cw_ref, edge_ref, rim_ref, top_ref, bot_ref, a_ref, inv_ref, *refs):
+    if last:
+        made, (result, q_ref, whole, sems) = refs[:1], refs[1:]
+        outs = (whole,)
+    else:
+        count = len(refs) // 2
+        made, outs, q_ref = refs[:count], refs[count:-1], refs[-1]
+    copies = []
     depth = rim_ref.shape[0]
     inner = slice(HALO, TILE - HALO)
 
@@ -378,10 +383,16 @@
             columns(i)
         for i in range(PACK):
             rows(i)
+            if last and i % 4 == 3:
+                ready = pl.ds(g8 * PACK + i - 3, 4)
+                copies.append(pltpu.make_async_copy(whole.at[ready], result.at[ready], sems.at[len(copies)]))
+                copies[-1].start()
         return carry
 
     for g8 in range(depth // PACK):
         group(g8, 0)
+    for copy in copies:
+        copy.wait()
 
 
 def keys_kernel(ids_ref, mix_ref, illum_ref, keys_ref, plane_ref):
@@ -523,11 +534,13 @@
         if ct is None:
             *got, ct = got
         cw, rt, edge = ready
+        leaving = [pltpu.VMEM(volume.shape, F32), pltpu.SemaphoreType.DMA((depth // 4,))] if last else []
         done = call(
-            functools.partial(edge_kernel, part),
+            functools.partial(edge_kernel, part, last),
             outs,
             [SMEM] + [VMEM] * (7 + len(outs)),
-            [pltpu.VMEM((PACK, 2 * TILE, TILE), BF16)],
+            [pltpu.VMEM((PACK, 2 * TILE, TILE), BF16), *leaving],
+            to=pl.BlockSpec(memory_space=pl.ANY) if last else VMEM,
             name="edge",
             flops=2 * 10**9,
         )(meta, cw, edge, main, top, bot, other, inv, *got)

time: 60.2 us -> 60.2 us (level)
  no operation moved by 1% of the time
where the time goes in v6:
time: 60.2 us; the launch traced here: 60.1 us
  Pallas kernels  27 us (45%)
  starting transfers between devices  25.2 us (42%)
  waiting for transfers between devices  5.89 us (10%)
  local copies, waits for them, and re-layouts  1.14 us (2%)
    pallas_call x4, Pallas kernels, blur(): call(functools.partial(main_kernel, part, len(making) - 2 if making else...  15 us
    ppermute x10, starting transfers between devices, swap(): return lax.ppermute(cells, axis, pairs + [(j, i) for i, j in pairs])  8.86 us
    pallas_call x4, Pallas kernels, blur(): call(functools.partial(edge_kernel, part, last), outs, [SMEM] + [VMEM] *...  7.72 us
    ppermute x4, starting transfers between devices, exchanged(): lax.ppermute(jnp.where(even, to_left, to_right), ('row', 'col'), outer_co...  7.65 us
    ppermute x3, starting transfers between devices, shards(): lax.ppermute(bank, 'col', [(i, i ^ s) for i in range(n_col)])  5.76 us
    ppermute x4, waiting for transfers between devices, exchanged(): lax.ppermute(jnp.where(even, to_left, to_right), ('row', 'col'), outer_co...  5.02 us
    ppermute x2, starting transfers between devices, shards(): lax.ppermute(plane, 'row', [(i, i ^ s) for i in range(n_row)])  2.77 us
    pallas_call x1, Pallas kernels, bands(): call(functools.partial(bands_kernel, part, n_row), outs, [SMEM] + [VMEM]...  2.33 us
  transfers between devices with their start and end apart: 23, of which 6 were waited for; matrix products, arithmetic and copies ran while one was open for 0% of the time, Pallas kernels for 35%

profile of v6, /device:TPU:0, one launch (start us, length us, event | category | flops | bytes accessed | tf_op | source)
XLA Modules:
  0.0 60.1 jit_solution(10192842964984963583)
XLA Ops:
  0.0 0.9 %copy-done.5 = f32[4,16,2,4,33]{4,3,2,1,0:T(4,128)S(1)} copy-done((f32[4,16,2,4,33]{4,3,2,1,0:T(4,128)S(1)}, f32[4,16,2,4,33]{4,3,2,1,0:T(4,128)}, u32[]{:S(2)}) %copy-start.5) | copy-done | bytes 67608
  1.0 0.1 bank.1.refs_0_
  1.1 0.0 copy-start.4
  1.1 5.1 %collective-permute-start.3 = (bf16[48,512]{1,0:T(8,128)(2,1)S(1)}, bf16[48,512]{1,0:T(8,128)(2,1)S(1)}, u32[]{:S(2)}, u32[]{:S(2)}) collective-permute-start(bf16[48,512]{1,0:T(8,128)(2,1)S(1)} %bank.1.refs_0_), channel_id=1, source_target_pairs={{0,6},{1,7},{2,4},{3,5},{4,2},{5,3},{6,0},{7,1},{8,14},{9,15},{10,... | collective-permute-start | bytes 147464 | tf_op jit(solution)/shard_map/ppermute | solution.py:468
  6.2 0.0 collective-permute-start.2
  6.2 0.6 %collective-permute-start.1 = (bf16[48,512]{1,0:T(8,128)(2,1)S(1)}, bf16[48,512]{1,0:T(8,128)(2,1)S(1)}, u32[]{:S(2)}, u32[]{:S(2)}) collective-permute-start(bf16[48,512]{1,0:T(8,128)(2,1)S(1)} %bank.1.refs_0_), channel_id=1, source_target_pairs={{0,2},{1,3},{2,0},{3,1},{4,6},{5,7},{6,4},{7,5},{8,10},{9,11},{10,... | collective-permute-start | bytes 147464 | tf_op jit(solution)/shard_map/ppermute | solution.py:468
  6.8 0.2 keys.1
  7.0 0.0 collective-permute-start
  7.0 0.0 copy-done.3
  7.0 0.4 first.1
  7.5 0.6 collective-permute-start.6
  8.0 0.1 collective-permute-done.other_ref
  8.1 1.6 %collective-permute-start.5 = (bf16[2,128,128]{2,1,0:T(8,128)(2,1)S(1)}, bf16[2,128,128]{2,1,0:T(8,128)(2,1)S(1)}, u32[]{:S(2)}, u32[]{:S(2)}) collective-permute-start(bf16[2,128,128]{2,1,0:T(8,128)(2,1)S(1)} %get-tuple-element.128), channel_id=1, source_target_pairs={{0,8},{1,2},{2,1},{3,4},{4,3},{5,6},{6,5},{7,15},{8,0},{9,10},{10,... | collective-permute-start | bytes 196616 | tf_op jit(solution)/shard_map/ppermute | solution.py:455
  9.8 0.1 stack.43.meta_ref
  9.9 0.0 collective-permute-done.3.refs_3_
  9.9 1.5 %collective-permute-start.10 = (bf16[3,16,128]{2,1,0:T(8,128)(2,1)S(1)}, bf16[3,16,128]{2,1,0:T(8,128)(2,1)S(1)}, u32[]{:S(2)}, u32[]{:S(2)}) collective-permute-start(bf16[3,16,128]{2,1,0:T(8,128)(2,1)S(1)} %get-tuple-element.56.refs_1_), channel_id=1, source_target_pairs={{0,24},{8,16},{16,8},{24,0},{1,25},{9,17},{17,9},{25,1},{2,26},{10... | collective-permute-start | bytes 36872 | tf_op jit(solution)/shard_map/ppermute | solution.py:550
  11.4 0.0 collective-permute-done.2.refs_2_
  11.4 1.3 %collective-permute-start.9 = (bf16[3,16,128]{2,1,0:T(8,128)(2,1)S(1)}, bf16[3,16,128]{2,1,0:T(8,128)(2,1)S(1)}, u32[]{:S(2)}, u32[]{:S(2)}) collective-permute-start(bf16[3,16,128]{2,1,0:T(8,128)(2,1)S(1)} %get-tuple-element.56.refs_1_), channel_id=1, source_target_pairs={{0,16},{8,24},{16,0},{24,8},{1,17},{9,25},{17,1},{25,9},{2,18},{10... | collective-permute-start | bytes 36872 | tf_op jit(solution)/shard_map/ppermute | solution.py:550
  12.7 0.0 collective-permute-done.1.refs_1_
  12.7 0.7 %pick.1 = (bf16[2,48,128]{2,1,0:T(8,128)(2,1)S(1)}, bf16[2,48,128]{2,1,0:T(8,128)(2,1)S(1)}) custom-call(s32[6]{0:T(128)S(1)} %stack.43.meta_ref, f32[4,128]{1,0:T(4,128)S(1)} %get-tuple-element.47.mine_ref.keys_ref, f32[4,128]{1,0:T(4,128)S(1)} %collective-permute-done.other_ref, bf16[48,512]{1,0:T(8,128)(2,1)S(1)} %bank.1.refs_0_, ...), custom_call_target="tpu_custom_call" | custom-call | bytes 1048576 | tf_op jit(solution)/shard_map/pick/pallas_call | solution.py:482
  13.4 0.1 collective-permute-start.4
  13.5 0.0 collective-permute-done.6
  13.5 0.0 collective-permute-done.5
  13.6 1.6 %collective-permute-start.8 = (bf16[23,16,128]{2,1,0:T(8,128)(2,1)S(1)}, bf16[23,16,128]{2,1,0:T(8,128)(2,1)S(1)}, u32[]{:S(2)}, u32[]{:S(2)}) collective-permute-start(bf16[23,16,128]{2,1,0:T(8,128)(2,1)S(1)} %get-tuple-element.99), channel_id=1, source_target_pairs={{0,8},{16,24},{8,0},{24,16},{1,9},{17,25},{9,1},{25,17},{2,10},{18... | collective-permute-start | bytes 282632 | tf_op jit(solution)/shard_map/ppermute | solution.py:51
  15.1 0.2 collective-permute-start.7
  15.3 0.0 collective-permute-done.4.other_ref
  15.3 0.5 taps.1.ct_ref.rt_ref.uv_ref
  15.9 5.3 %main.4 = (f32[16,32,128]{2,1,0:T(8,128)S(1)}, bf16[16,128,128]{2,1,0:T(8,128)(2,1)S(1)}, bf16[2,128,128]{2,1,0:T(8,128)(2,1)S(1)}, bf16[2,128,128]{2,1,0:T(8,12...) custom-call(s32[6]{0:T(128)S(1)} %stack.43.meta_ref, ...), custom_call_target="tpu_custom_call" | custom-call | flops 4000000000 | bytes 1048576 | tf_op jit(solution)/shard_map/main/pallas_call | solution.py:524
  21.2 0.0 collective-permute-done.8
  21.2 0.0 collective-permute-done.7
  21.2 1.7 %edge.4 = (bf16[16,128,128]{2,1,0:T(8,128)(2,1)S(1)}, bf16[2,128,128]{2,1,0:T(8,128)(2,1)S(1)}, bf16[2,128,128]{2,1,0:T(8,128)(2,1)S(1)}) custom-call(s32[6]{0:T(128)S(1)} %stack.43.meta_ref, bf16[16,128,512]{2,1,0:T(8,128)(2,1)S(1)} %get-tuple-element.53.cw_ref, bf16[16,32,256]{2,1,0:T(8,128)(2,1)S(1)} %get-tuple-element.54.edge_ref, ...), custom_call_target="tpu_custom_call" | custom-call | flops 2000000000 | bytes 1048576 | tf_op jit(solution)/shard_map/edge/pallas_call | solution.py:538
  22.9 0.4 collective-permute-start.12
  23.3 1.8 %collective-permute-start.11 = (bf16[2,128,128]{2,1,0:T(8,128)(2,1)S(1)}, bf16[2,128,128]{2,1,0:T(8,128)(2,1)S(1)}, u32[]{:S(2)}, u32[]{:S(2)}) collective-permute-start(bf16[2,128,128]{2,1,0:T(8,128)(2,1)S(1)} %get-tuple-element.124), channel_id=1, source_target_pairs={{0,8},{1,2},{2,1},{3,4},{4,3},{5,6},{6,5},{7,15},{8,0},{9,10},{10,... | collective-permute-start | bytes 196616 | tf_op jit(solution)/shard_map/ppermute | solution.py:455
  25.1 0.0 collective-permute-done.10.refs_4_
  25.1 0.0 collective-permute-done.9.refs_3_
  25.1 2.3 %bands.1 = (bf16[16,256,1024]{2,1,0:T(8,128)(2,1)S(1)}, f32[2,128,8]{2,1,0:T(8,128)S(1)}) custom-call(s32[6]{0:T(128)S(1)} %stack.43.meta_ref, f32[2,16,8,256]{3,2,1,0:T(8,128)S(1)} %taps.1.ct_ref.rt_ref.uv_ref, f32[4,64,128]{2,1,0:T(8,128)S(1)} %copy-done.6, bf16[3,16,128]{2,1,0:T(8,128)(2,1)S(1)} %get-tuple-element.56.refs_1_, ...), custom_call_target="tpu_custom_call" | custom-call | flops 4000000000 | bytes 1048576 | tf_op jit(solution)/shard_map/bands/pallas_call | solution.py:504
  27.5 0.0 collective-permute-done.12
  27.5 0.1 collective-permute-done.11
  27.6 1.9 %collective-permute-start.14 = (bf16[20,16,128]{2,1,0:T(8,128)(2,1)S(1)}, bf16[20,16,128]{2,1,0:T(8,128)(2,1)S(1)}, u32[]{:S(2)}, u32[]{:S(2)}) collective-permute-start(bf16[20,16,128]{2,1,0:T(8,128)(2,1)S(1)} %get-tuple-element.111), channel_id=1, source_target_pairs={{0,8},{16,24},{8,0},{24,16},{1,9},{17,25},{9,1},{25,17},{2,10},{18... | collective-permute-start | bytes 245768 | tf_op jit(solution)/shard_map/ppermute | solution.py:51
  29.5 0.0 collective-permute-start.13
  29.5 3.7 %main.5 = (f32[16,32,128]{2,1,0:T(8,128)S(1)}, f32[16,128,128]{2,1,0:T(8,128)S(1)}, bf16[16,128,128]{2,1,0:T(8,128)(2,1)S(1)}, bf16[2,128,128]{2,1,0:T(8,128)(2,...) custom-call(s32[6]{0:T(128)S(1)} %stack.43.meta_ref, ...), custom_call_target="tpu_custom_call" | custom-call | flops 4000000000 | bytes 1048576 | tf_op jit(solution)/shard_map/main/pallas_call | solution.py:524
  33.2 0.0 collective-permute-done.14
  33.2 0.0 collective-permute-done.13
  33.3 2.0 %edge.5 = (f32[16,128,128]{2,1,0:T(8,128)S(1)}, bf16[16,128,128]{2,1,0:T(8,128)(2,1)S(1)}, bf16[2,128,128]{2,1,0:T(8,128)(2,1)S(1)}, bf16[2,128,128]{2,1,0:T(8,128)(2,1)S(1)}) custom-call(s32[6]{0:T(128)S(1)} %stack.43.meta_ref, bf16[16,128,512]{2,1,0:T(8,128)(2,1)S(1)} %get-tuple-element.66.cw_ref, bf16[16,32,256]{2,1,0:T(8,128)(2,1)S(1)} %get-tuple-element.67.edge_ref, ...), custom_call_target="tpu_custom_call" | custom-call | flops 2000000000 | bytes 1048576 | tf_op jit(solution)/shard_map/edge/pallas_call | solution.py:538
  35.3 0.6 collective-permute-start.16
  35.9 1.5 %collective-permute-start.15 = (bf16[2,128,128]{2,1,0:T(8,128)(2,1)S(1)}, bf16[2,128,128]{2,1,0:T(8,128)(2,1)S(1)}, u32[]{:S(2)}, u32[]{:S(2)}) collective-permute-start(bf16[2,128,128]{2,1,0:T(8,128)(2,1)S(1)} %get-tuple-element.120), channel_id=1, source_target_pairs={{0,8},{1,2},{2,1},{3,4},{4,3},{5,6},{6,5},{7,15},{8,0},{9,10},{10,... | collective-permute-start | bytes 196616 | tf_op jit(solution)/shard_map/ppermute | solution.py:455
  37.4 0.0 collective-permute-done.16
  37.4 2.7 %collective-permute-done.15 = bf16[2,128,128]{2,1,0:T(8,128)(2,1)S(1)} collective-permute-done((bf16[2,128,128]{2,1,0:T(8,128)(2,1)S(1)}, bf16[2,128,128]{2,1,0:T(8,128)(2,1)S(1)}, u32[]{:S(2)}, u32[]{:S(2)}) %collective-permute-start.15) | collective-permute-done | bytes 65568 | tf_op jit(solution)/shard_map/ppermute | solution.py:455
  40.2 1.6 %collective-permute-start.18 = (bf16[20,16,128]{2,1,0:T(8,128)(2,1)S(1)}, bf16[20,16,128]{2,1,0:T(8,128)(2,1)S(1)}, u32[]{:S(2)}, u32[]{:S(2)}) collective-permute-start(bf16[20,16,128]{2,1,0:T(8,128)(2,1)S(1)} %get-tuple-element.107), channel_id=1, source_target_pairs={{0,8},{16,24},{8,0},{24,16},{1,9},{17,25},{9,1},{25,17},{2,10},{18... | collective-permute-start | bytes 245768 | tf_op jit(solution)/shard_map/ppermute | solution.py:51
  41.8 0.0 collective-permute-start.17
  41.8 3.0 %main.6 = (f32[16,32,128]{2,1,0:T(8,128)S(1)}, bf16[16,128,128]{2,1,0:T(8,128)(2,1)S(1)}, bf16[2,128,128]{2,1,0:T(8,128)(2,1)S(1)}, bf16[2,128,128]{2,1,0:T(8,128)(2,1)S(1)}) custom-call(s32[6]{0:T(128)S(1)} %stack.43.meta_ref, bf16[16,256,1024]{2,1,0:T(8,128)(2,1)S(1)} %get-tuple-element.69.ct_ref, bf16[16,128,1024]{2,1,0:T(8,128)(2,1)S(1)} %get-tuple-element.70.rt_ref, ...), custom_call_target="tpu_custom_call" | custom-call | flops 4000000000 | bytes 1048576 | tf_op jit(solution)/shard_map/main/pallas_call | solution.py:524
  44.9 0.4 collective-permute-done.18
  45.3 0.0 collective-permute-done.17
  45.3 1.6 %edge.6 = (bf16[16,128,128]{2,1,0:T(8,128)(2,1)S(1)}, bf16[2,128,128]{2,1,0:T(8,128)(2,1)S(1)}, bf16[2,128,128]{2,1,0:T(8,128)(2,1)S(1)}) custom-call(s32[6]{0:T(128)S(1)} %stack.43.meta_ref, bf16[16,128,512]{2,1,0:T(8,128)(2,1)S(1)} %get-tuple-element.53.cw_ref, bf16[16,32,256]{2,1,0:T(8,128)(2,1)S(1)} %get-tuple-element.54.edge_ref, ...), custom_call_target="tpu_custom_call" | custom-call | flops 2000000000 | bytes 1048576 | tf_op jit(solution)/shard_map/edge/pallas_call | solution.py:538
  47.0 0.2 collective-permute-start.20
  47.1 2.7 %collective-permute-start.19 = (bf16[2,128,128]{2,1,0:T(8,128)(2,1)S(1)}, bf16[2,128,128]{2,1,0:T(8,128)(2,1)S(1)}, u32[]{:S(2)}, u32[]{:S(2)}) collective-permute-start(bf16[2,128,128]{2,1,0:T(8,128)(2,1)S(1)} %get-tuple-element.116), channel_id=1, source_target_pairs={{0,8},{1,2},{2,1},{3,4},{4,3},{5,6},{6,5},{7,15},{8,0},{9,10},{10,... | collective-permute-start | bytes 196616 | tf_op jit(solution)/shard_map/ppermute | solution.py:455
  49.8 0.0 collective-permute-done.20
  49.9 2.2 %collective-permute-done.19 = bf16[2,128,128]{2,1,0:T(8,128)(2,1)S(1)} collective-permute-done((bf16[2,128,128]{2,1,0:T(8,128)(2,1)S(1)}, bf16[2,128,128]{2,1,0:T(8,128)(2,1)S(1)}, u32[]{:S(2)}, u32[]{:S(2)}) %collective-permute-start.19) | collective-permute-done | bytes 65568 | tf_op jit(solution)/shard_map/ppermute | solution.py:455
  52.2 2.1 %collective-permute-start.22 = (bf16[20,16,128]{2,1,0:T(8,128)(2,1)S(1)}, bf16[20,16,128]{2,1,0:T(8,128)(2,1)S(1)}, u32[]{:S(2)}, u32[]{:S(2)}) collective-permute-start(bf16[20,16,128]{2,1,0:T(8,128)(2,1)S(1)} %get-tuple-element.103), channel_id=1, source_target_pairs={{0,8},{16,24},{8,0},{24,16},{1,9},{17,25},{9,1},{25,17},{2,10},{18... | collective-permute-start | bytes 245768 | tf_op jit(solution)/shard_map/ppermute | solution.py:51
  54.2 0.0 collective-permute-start.21
  54.2 2.9 %main.7 = (f32[16,32,128]{2,1,0:T(8,128)S(1)}, f32[16,128,128]{2,1,0:T(8,128)S(1)}) custom-call(s32[6]{0:T(128)S(1)} %stack.43.meta_ref, bf16[16,256,1024]{2,1,0:T(8,128)(2,1)S(1)} %get-tuple-element.62.ct_ref, bf16[16,128,1024]{2,1,0:T(8,128)(2,1)S(1)} %get-tuple-element.68.rt_ref, bf16[16,128,128]{2,1,0:T(8,128)(2,1)S(1)} %get-tuple-element.83.field_ref, ...), custom_call_target="tpu_custom_call" | custom-call | flops 4000000000 | bytes 1048576 | tf_op jit(solution)/shard_map/main/pallas_call | solution.py:524
  57.2 0.3 collective-permute-done.22
  57.5 0.0 collective-permute-done.21
  57.5 2.4 %edge.7 = f32[16,128,128]{2,1,0:T(8,128)} custom-call(s32[6]{0:T(128)S(1)} %stack.43.meta_ref, bf16[16,128,512]{2,1,0:T(8,128)(2,1)S(1)} %get-tuple-element.66.cw_ref, bf16[16,32,256]{2,1,0:T(8,128)(2,1)S(1)} %get-tuple-element.67.edge_ref, f32[16,32,128]{2,1,0:T(8,128)S(1)} %get-tuple-element.87.rim_ref, ...), custom_call_target="tpu_custom_call" | custom-call | flops 2000000000 | bytes 1048576 | tf_op jit(solution)/shard_map/edge/pallas_call | solution.py:538
  (40 shorter events, 0.4 us)
Async XLA Ops:
  0.0 0.9 %copy-start.5 = (f32[4,16,2,4,33]{4,3,2,1,0:T(4,128)S(1)}, f32[4,16,2,4,33]{4,3,2,1,0:T(4,128)}, u32[]{:S(2)}) copy-start(f32[4,16,2,4,33]{4,3,2,1,0:T(4,128)} %param.9) | copy-start | bytes 202756
  1.0 5.9 %copy-start = (f32[16,16,1]{1,2,0:T(1,128)S(1)}, f32[16,16,1]{1,2,0:T(1,128)}, u32[]{:S(2)}) copy-start(f32[16,16,1]{1,2,0:T(1,128)} %param.12) | copy-start | bytes 3076
  1.0 5.9 %copy-start.1 = (s32[1,1,16,2]{2,3,1,0:T(2,128)S(1)}, s32[1,1,16,2]{2,3,1,0:T(2,128)}, u32[]{:S(2)}) copy-start(s32[1,1,16,2]{2,3,1,0:T(2,128)} %param.10) | copy-start | bytes 388
  1.0 5.9 %copy-start.2 = (f32[1,1,16,2]{2,3,1,0:T(2,128)S(1)}, f32[1,1,16,2]{2,3,1,0:T(2,128)}, u32[]{:S(2)}) copy-start(f32[1,1,16,2]{2,3,1,0:T(2,128)} %param.11) | copy-start | bytes 388
  1.0 6.0 %copy-start.3 = (f32[16,128,128]{2,1,0:T(8,128)S(1)}, f32[16,128,128]{2,1,0:T(8,128)}, u32[]{:S(2)}) copy-start(f32[16,128,128]{2,1,0:T(8,128)} %a_ref.9) | copy-start | bytes 3145732
  1.1 14.8 %copy-start.4 = (f32[16,128,128]{2,1,0:T(8,128)S(1)}, f32[16,128,128]{2,1,0:T(8,128)}, u32[]{:S(2)}) copy-start(f32[16,128,128]{2,1,0:T(8,128)} %a_ref.11) | copy-start | bytes 3145732
  1.1 8.8 %collective-permute-start.3 = (bf16[48,512]{1,0:T(8,128)(2,1)S(1)}, bf16[48,512]{1,0:T(8,128)(2,1)S(1)}, u32[]{:S(2)}, u32[]{:S(2)}) collective-permute-start(bf16[48,512]{1,0:T(8,128)(2,1)S(1)} %bank.1.refs_0_), channel_id=1, source_target_pairs={{0,6},{1,7},{2,4},{3,5},{4,2},{5,3},{6,0},{7,1},{8,14},{9,15},{10,... | collective-permute-start | bytes 147464 | tf_op jit(solution)/shard_map/ppermute | solution.py:468
  6.2 5.3 %collective-permute-start.2 = (bf16[48,512]{1,0:T(8,128)(2,1)S(1)}, bf16[48,512]{1,0:T(8,128)(2,1)S(1)}, u32[]{:S(2)}, u32[]{:S(2)}) collective-permute-start(bf16[48,512]{1,0:T(8,128)(2,1)S(1)} %bank.1.refs_0_), channel_id=1, source_target_pairs={{0,4},{1,5},{2,6},{3,7},{4,0},{5,1},{6,2},{7,3},{8,12},{9,13},{10,... | collective-permute-start | bytes 147464 | tf_op jit(solution)/shard_map/ppermute | solution.py:468
  6.2 6.5 %collective-permute-start.1 = (bf16[48,512]{1,0:T(8,128)(2,1)S(1)}, bf16[48,512]{1,0:T(8,128)(2,1)S(1)}, u32[]{:S(2)}, u32[]{:S(2)}) collective-permute-start(bf16[48,512]{1,0:T(8,128)(2,1)S(1)} %bank.1.refs_0_), channel_id=1, source_target_pairs={{0,2},{1,3},{2,0},{3,1},{4,6},{5,7},{6,4},{7,5},{8,10},{9,11},{10,... | collective-permute-start | bytes 147464 | tf_op jit(solution)/shard_map/ppermute | solution.py:468
  7.0 1.2 %collective-permute-start = (f32[4,128]{1,0:T(4,128)S(1)}, f32[4,128]{1,0:T(4,128)S(1)}, u32[]{:S(2)}, u32[]{:S(2)}) collective-permute-start(f32[4,128]{1,0:T(4,128)S(1)} %get-tuple-element.47.mine_ref.keys_ref), channel_id=1, source_target_pairs={{0,1},{2,3},{4,5},{6,7},{1,0},{3,2},{5,4},{7,6},{8,9},{10,11},{12,... | collective-permute-start | bytes 6152 | tf_op jit(solution)/shard_map/ppermute | solution.py:51
  7.5 6.0 %collective-permute-start.6 = (bf16[2,128,128]{2,1,0:T(8,128)(2,1)S(1)}, bf16[2,128,128]{2,1,0:T(8,128)(2,1)S(1)}, u32[]{:S(2)}, u32[]{:S(2)}) collective-permute-start(bf16[2,128,128]{2,1,0:T(8,128)(2,1)S(1)} %get-tuple-element.127), channel_id=1, source_target_pairs={{0,1},{2,3},{4,5},{6,7},{1,0},{3,2},{5,4},{7,6},{8,9},{10,11},{12,... | collective-permute-start | bytes 196616 | tf_op jit(solution)/shard_map/ppermute | solution.py:51
  8.1 5.3 %collective-permute-start.5 = (bf16[2,128,128]{2,1,0:T(8,128)(2,1)S(1)}, bf16[2,128,128]{2,1,0:T(8,128)(2,1)S(1)}, u32[]{:S(2)}, u32[]{:S(2)}) collective-permute-start(bf16[2,128,128]{2,1,0:T(8,128)(2,1)S(1)} %get-tuple-element.128), channel_id=1, source_target_pairs={{0,8},{1,2},{2,1},{3,4},{4,3},{5,6},{6,5},{7,15},{8,0},{9,10},{10,... | collective-permute-start | bytes 196616 | tf_op jit(solution)/shard_map/ppermute | solution.py:455
  9.9 15.2 %collective-permute-start.10 = (bf16[3,16,128]{2,1,0:T(8,128)(2,1)S(1)}, bf16[3,16,128]{2,1,0:T(8,128)(2,1)S(1)}, u32[]{:S(2)}, u32[]{:S(2)}) collective-permute-start(bf16[3,16,128]{2,1,0:T(8,128)(2,1)S(1)} %get-tuple-element.56.refs_1_), channel_id=1, source_target_pairs={{0,24},{8,16},{16,8},{24,0},{1,25},{9,17},{17,9},{25,1},{2,26},{10... | collective-permute-start | bytes 36872 | tf_op jit(solution)/shard_map/ppermute | solution.py:550
  11.4 13.7 %collective-permute-start.9 = (bf16[3,16,128]{2,1,0:T(8,128)(2,1)S(1)}, bf16[3,16,128]{2,1,0:T(8,128)(2,1)S(1)}, u32[]{:S(2)}, u32[]{:S(2)}) collective-permute-start(bf16[3,16,128]{2,1,0:T(8,128)(2,1)S(1)} %get-tuple-element.56.refs_1_), channel_id=1, source_target_pairs={{0,16},{8,24},{16,0},{24,8},{1,17},{9,25},{17,1},{25,9},{2,18},{10... | collective-permute-start | bytes 36872 | tf_op jit(solution)/shard_map/ppermute | solution.py:550
  13.4 1.9 %collective-permute-start.4 = (bf16[2,48,128]{2,1,0:T(8,128)(2,1)S(1)}, bf16[2,48,128]{2,1,0:T(8,128)(2,1)S(1)}, u32[]{:S(2)}, u32[]{:S(2)}) collective-permute-start(bf16[2,48,128]{2,1,0:T(8,128)(2,1)S(1)} %get-tuple-element.49), channel_id=1, source_target_pairs={{0,1},{2,3},{4,5},{6,7},{1,0},{3,2},{5,4},{7,6},{8,9},{10,11},{12,... | collective-permute-start | bytes 73736 | tf_op jit(solution)/shard_map/ppermute | solution.py:51
  13.6 7.6 %collective-permute-start.8 = (bf16[23,16,128]{2,1,0:T(8,128)(2,1)S(1)}, bf16[23,16,128]{2,1,0:T(8,128)(2,1)S(1)}, u32[]{:S(2)}, u32[]{:S(2)}) collective-permute-start(bf16[23,16,128]{2,1,0:T(8,128)(2,1)S(1)} %get-tuple-element.99), channel_id=1, source_target_pairs={{0,8},{16,24},{8,0},{24,16},{1,9},{17,25},{9,1},{25,17},{2,10},{18... | collective-permute-start | bytes 282632 | tf_op jit(solution)/shard_map/ppermute | solution.py:51
  15.1 6.1 %collective-permute-start.7 = (bf16[23,16,128]{2,1,0:T(8,128)(2,1)S(1)}, bf16[23,16,128]{2,1,0:T(8,128)(2,1)S(1)}, u32[]{:S(2)}, u32[]{:S(2)}) collective-permute-start(bf16[23,16,128]{2,1,0:T(8,128)(2,1)S(1)} %get-tuple-element.100), channel_id=1, source_target_pairs={{0,1},{1,0},{2,3},{3,2},{4,5},{5,4},{6,7},{7,6},{8,16},{9,17},{10,... | collective-permute-start | bytes 282632 | tf_op jit(solution)/shard_map/ppermute | solution.py:519
  21.2 3.9 %copy-start.6 = (f32[4,64,128]{2,1,0:T(8,128)S(1)}, f32[4,64,128]{2,1,0:T(8,128)}, u32[]{:S(2)}) copy-start(f32[4,64,128]{2,1,0:T(8,128)} %constant.46.clone.refs_0_) | copy-start | bytes 393220
  22.9 4.6 %collective-permute-start.12 = (bf16[2,128,128]{2,1,0:T(8,128)(2,1)S(1)}, bf16[2,128,128]{2,1,0:T(8,128)(2,1)S(1)}, u32[]{:S(2)}, u32[]{:S(2)}) collective-permute-start(bf16[2,128,128]{2,1,0:T(8,128)(2,1)S(1)} %get-tuple-element.123), channel_id=1, source_target_pairs={{0,1},{2,3},{4,5},{6,7},{1,0},{3,2},{5,4},{7,6},{8,9},{10,11},{12,... | collective-permute-start | bytes 196616 | tf_op jit(solution)/shard_map/ppermute | solution.py:51
  23.3 4.3 %collective-permute-start.11 = (bf16[2,128,128]{2,1,0:T(8,128)(2,1)S(1)}, bf16[2,128,128]{2,1,0:T(8,128)(2,1)S(1)}, u32[]{:S(2)}, u32[]{:S(2)}) collective-permute-start(bf16[2,128,128]{2,1,0:T(8,128)(2,1)S(1)} %get-tuple-element.124), channel_id=1, source_target_pairs={{0,8},{1,2},{2,1},{3,4},{4,3},{5,6},{6,5},{7,15},{8,0},{9,10},{10,... | collective-permute-start | bytes 196616 | tf_op jit(solution)/shard_map/ppermute | solution.py:455
  27.6 5.6 %collective-permute-start.14 = (bf16[20,16,128]{2,1,0:T(8,128)(2,1)S(1)}, bf16[20,16,128]{2,1,0:T(8,128)(2,1)S(1)}, u32[]{:S(2)}, u32[]{:S(2)}) collective-permute-start(bf16[20,16,128]{2,1,0:T(8,128)(2,1)S(1)} %get-tuple-element.111), channel_id=1, source_target_pairs={{0,8},{16,24},{8,0},{24,16},{1,9},{17,25},{9,1},{25,17},{2,10},{18... | collective-permute-start | bytes 245768 | tf_op jit(solution)/shard_map/ppermute | solution.py:51
  29.5 3.7 %collective-permute-start.13 = (bf16[20,16,128]{2,1,0:T(8,128)(2,1)S(1)}, bf16[20,16,128]{2,1,0:T(8,128)(2,1)S(1)}, u32[]{:S(2)}, u32[]{:S(2)}) collective-permute-start(bf16[20,16,128]{2,1,0:T(8,128)(2,1)S(1)} %get-tuple-element.112), channel_id=1, source_target_pairs={{0,1},{1,0},{2,3},{3,2},{4,5},{5,4},{6,7},{7,6},{8,16},{9,17},{10,... | collective-permute-start | bytes 245768 | tf_op jit(solution)/shard_map/ppermute | solution.py:519
  35.3 2.1 %collective-permute-start.16 = (bf16[2,128,128]{2,1,0:T(8,128)(2,1)S(1)}, bf16[2,128,128]{2,1,0:T(8,128)(2,1)S(1)}, u32[]{:S(2)}, u32[]{:S(2)}) collective-permute-start(bf16[2,128,128]{2,1,0:T(8,128)(2,1)S(1)} %get-tuple-element.119), channel_id=1, source_target_pairs={{0,1},{2,3},{4,5},{6,7},{1,0},{3,2},{5,4},{7,6},{8,9},{10,11},{12,... | collective-permute-start | bytes 196616 | tf_op jit(solution)/shard_map/ppermute | solution.py:51
  35.9 4.3 %collective-permute-start.15 = (bf16[2,128,128]{2,1,0:T(8,128)(2,1)S(1)}, bf16[2,128,128]{2,1,0:T(8,128)(2,1)S(1)}, u32[]{:S(2)}, u32[]{:S(2)}) collective-permute-start(bf16[2,128,128]{2,1,0:T(8,128)(2,1)S(1)} %get-tuple-element.120), channel_id=1, source_target_pairs={{0,8},{1,2},{2,1},{3,4},{4,3},{5,6},{6,5},{7,15},{8,0},{9,10},{10,... | collective-permute-start | bytes 196616 | tf_op jit(solution)/shard_map/ppermute | solution.py:455
  40.2 5.0 %collective-permute-start.18 = (bf16[20,16,128]{2,1,0:T(8,128)(2,1)S(1)}, bf16[20,16,128]{2,1,0:T(8,128)(2,1)S(1)}, u32[]{:S(2)}, u32[]{:S(2)}) collective-permute-start(bf16[20,16,128]{2,1,0:T(8,128)(2,1)S(1)} %get-tuple-element.107), channel_id=1, source_target_pairs={{0,8},{16,24},{8,0},{24,16},{1,9},{17,25},{9,1},{25,17},{2,10},{18... | collective-permute-start | bytes 245768 | tf_op jit(solution)/shard_map/ppermute | solution.py:51
  41.8 3.5 %collective-permute-start.17 = (bf16[20,16,128]{2,1,0:T(8,128)(2,1)S(1)}, bf16[20,16,128]{2,1,0:T(8,128)(2,1)S(1)}, u32[]{:S(2)}, u32[]{:S(2)}) collective-permute-start(bf16[20,16,128]{2,1,0:T(8,128)(2,1)S(1)} %get-tuple-element.108), channel_id=1, source_target_pairs={{0,1},{1,0},{2,3},{3,2},{4,5},{5,4},{6,7},{7,6},{8,16},{9,17},{10,... | collective-permute-start | bytes 245768 | tf_op jit(solution)/shard_map/ppermute | solution.py:519
  47.0 2.9 %collective-permute-start.20 = (bf16[2,128,128]{2,1,0:T(8,128)(2,1)S(1)}, bf16[2,128,128]{2,1,0:T(8,128)(2,1)S(1)}, u32[]{:S(2)}, u32[]{:S(2)}) collective-permute-start(bf16[2,128,128]{2,1,0:T(8,128)(2,1)S(1)} %get-tuple-element.115), channel_id=1, source_target_pairs={{0,1},{2,3},{4,5},{6,7},{1,0},{3,2},{5,4},{7,6},{8,9},{10,11},{12,... | collective-permute-start | bytes 196616 | tf_op jit(solution)/shard_map/ppermute | solution.py:51
  47.1 4.9 %collective-permute-start.19 = (bf16[2,128,128]{2,1,0:T(8,128)(2,1)S(1)}, bf16[2,128,128]{2,1,0:T(8,128)(2,1)S(1)}, u32[]{:S(2)}, u32[]{:S(2)}) collective-permute-start(bf16[2,128,128]{2,1,0:T(8,128)(2,1)S(1)} %get-tuple-element.116), channel_id=1, source_target_pairs={{0,8},{1,2},{2,1},{3,4},{4,3},{5,6},{6,5},{7,15},{8,0},{9,10},{10,... | collective-permute-start | bytes 196616 | tf_op jit(solution)/shard_map/ppermute | solution.py:455
  52.2 5.3 %collective-permute-start.22 = (bf16[20,16,128]{2,1,0:T(8,128)(2,1)S(1)}, bf16[20,16,128]{2,1,0:T(8,128)(2,1)S(1)}, u32[]{:S(2)}, u32[]{:S(2)}) collective-permute-start(bf16[20,16,128]{2,1,0:T(8,128)(2,1)S(1)} %get-tuple-element.103), channel_id=1, source_target_pairs={{0,8},{16,24},{8,0},{24,16},{1,9},{17,25},{9,1},{25,17},{2,10},{18... | collective-permute-start | bytes 245768 | tf_op jit(solution)/shard_map/ppermute | solution.py:51
  54.2 3.2 %collective-permute-start.21 = (bf16[20,16,128]{2,1,0:T(8,128)(2,1)S(1)}, bf16[20,16,128]{2,1,0:T(8,128)(2,1)S(1)}, u32[]{:S(2)}, u32[]{:S(2)}) collective-permute-start(bf16[20,16,128]{2,1,0:T(8,128)(2,1)S(1)} %get-tuple-element.104), channel_id=1, source_target_pairs={{0,1},{1,0},{2,3},{3,2},{4,5},{5,4},{6,7},{7,6},{8,16},{9,17},{10,... | collective-permute-start | bytes 245768 | tf_op jit(solution)/shard_map/ppermute | solution.py:519
